TPU v7x, 32 devices: a whole 2x2x4 slice. The times are simulated.
32 devices in a mesh: tile: 4 (over y, x), tm: 8 (over z, core).
Axes of the slice: x: 2, y: 2, z: 4, core: 2. Of those that a mesh axis runs over, the one named last changes fastest.
Arguments:
- movie: bfloat16 [128, 256, 512], P('tm', None, 'tile'), may hold values from -6 to 6
- omega: bfloat16 [2, 4, 32, 128], P(None, 'tile', None, 'tm'), may hold values from -0.5 to 0.5
- time_taps: bfloat16 [17], replicated, may hold values from 0.019897461 to 0.099609375
- space_taps: bfloat16 [17], replicated, may hold values from 0.099609375 to 0.29882812
Outputs:
- basis: float32 [32, 256, 512], P(None, 'tm', 'tile')
- coefficients: float32 [2, 4, 32, 128], P(None, 'tile', None, 'tm')
All inputs are finite; a program needn't handle non-finite values.
Results may differ from a plain program's by a relative error of at most 0.024.
Values may be sent and summed in bfloat16 or wider, within the bound.
No kernel may reach another device: no remote copies, remote signals or barrier semaphores. Data moves between devices by JAX's collectives and lax.ppermute only.
A program may use at most 64 MiB of HBM per device.

v0:
```python
import math

import jax
import jax.numpy as jnp
from jax import lax
from jax.sharding import PartitionSpec as P

H = 128
TY = 2


def with_halo(block, sides, width):
    for axis, dim in sides:
        count = lax.axis_size(axis)
        forward = [(i, i + 1) for i in range(count - 1)]
        backward = [(target, source) for source, target in forward]
        low = lax.ppermute(
            lax.slice_in_dim(block, block.shape[dim] - width, None, axis=dim), axis, forward
        )
        high = lax.ppermute(lax.slice_in_dim(block, 0, width, axis=dim), axis, backward)
        block = jnp.concatenate([low, block, high], axis=dim)
    return block


def band(tap_row, out_count, in_count, offset_by):
    row_ids = lax.broadcasted_iota(jnp.int32, (out_count, in_count), 0)
    col_ids = lax.broadcasted_iota(jnp.int32, (out_count, in_count), 1)
    offsets = col_ids - row_ids + offset_by
    picks = jnp.arange(tap_row.shape[0], dtype=jnp.int32)
    hits = (offsets[:, :, None] == picks).astype(jnp.float32)
    return jnp.sum(hits * tap_row.astype(jnp.float32), axis=2).astype(jnp.bfloat16)


def orthonormal(matrix):
    gram_block = jnp.dot(matrix, matrix.T, precision=lax.Precision.HIGHEST)
    factor_low = jnp.linalg.cholesky(gram_block)
    return jax.scipy.linalg.solve_triangular(factor_low, matrix, lower=True)


def local(movie, omega, time_taps, space_taps):
    frames, image_rows, tile_cols = movie.shape
    radius = (time_taps.shape[0] - 1) // 2
    tile_rows = H
    stack = TY
    pixels = tile_rows * tile_cols
    rank_count = omega.shape[2]
    row_share = image_rows // lax.axis_size("tm")
    time_band = band(time_taps, frames, frames + 2 * radius, 0)
    padded = with_halo(movie, (("tm", 0),), radius)
    flat_rows = padded.reshape(frames + 2 * radius, image_rows * tile_cols)
    low_time = jnp.dot(time_band, flat_rows, preferred_element_type=jnp.float32)
    centre = flat_rows[radius : radius + frames].astype(jnp.float32)
    temporal = (centre - low_time).astype(jnp.bfloat16).reshape(frames, image_rows, tile_cols)
    temporal = with_halo(temporal, (("tile", 2),), radius)
    across = band(space_taps, tile_cols, tile_cols + 2 * radius, 0).T
    smooth_x = jnp.dot(temporal, across, preferred_element_type=jnp.float32).astype(jnp.bfloat16)
    down_band = band(space_taps, image_rows, image_rows, radius)
    lowpass = jnp.einsum("ab,fbw->faw", down_band, smooth_x, preferred_element_type=jnp.float32)
    centre_z = temporal[:, :, radius : radius + tile_cols].astype(jnp.float32)
    filtered = (centre_z - lowpass).astype(jnp.bfloat16).reshape(frames, stack, pixels)
    row_start = lax.axis_index("tm") * row_share

    def to_image(tiled):
        shaped = tiled.reshape(stack, rank_count, tile_rows, tile_cols)
        return jnp.transpose(shaped, (1, 0, 2, 3)).reshape(rank_count, image_rows, tile_cols)

    def subspace(partial_value):
        summed = lax.psum(partial_value.astype(jnp.bfloat16), "tm").astype(jnp.float32)
        basis_all = jax.vmap(orthonormal)(summed)
        own_rows = lax.dynamic_slice_in_dim(to_image(basis_all), row_start, row_share, 1)
        return (basis_all.astype(jnp.bfloat16), own_rows)

    omega_local = omega[:, 0]
    sketch = jnp.einsum("tkf,ftp->tkp", omega_local, filtered, preferred_element_type=jnp.float32)
    first_basis, unused_rows = subspace(sketch)
    loadings = jnp.einsum(
        "ftp,tkp->ftk", filtered, first_basis, preferred_element_type=jnp.float32
    ).astype(jnp.bfloat16)
    refined = jnp.einsum("ftk,ftp->tkp", loadings, filtered, preferred_element_type=jnp.float32)
    final_basis, final_rows = subspace(refined)
    coefficients = jnp.einsum(
        "tkp,ftp->tkf", final_basis, filtered, preferred_element_type=jnp.float32
    )
    return (final_rows * math.sqrt(pixels), coefficients[:, None])


def solution(mesh):
    in_specs = (P("tm", None, "tile"), P(None, "tile", None, "tm"), P(), P())
    out_specs = (P(None, "tm", "tile"), P(None, "tile", None, "tm"))
    return jax.shard_map(local, mesh=mesh, in_specs=in_specs, out_specs=out_specs, check_vma=False)
```

profile of v0, /device:TPU:4, one launch (start us, length us, event | category | flops | bytes accessed | tf_op | source)
XLA Modules:
  0.0 223.2 jit_solution(14975354881845812317)
XLA Ops:
  7.2 0.0 copy-start
  7.2 0.0 copy-start.3
  7.2 0.0 all-reduce.3.cloned.1.call-start
  7.2 1.4 fusion.46
  8.6 0.0 copy-start.4
  8.6 0.0 copy-start.5
  8.6 1.8 collective-permute-start
  10.4 1.3 collective-permute-start.1
  11.7 0.0 copy-done.3
  11.7 0.2 convert.1
  11.9 0.0 copy-done.4
  12.0 0.0 copy-done.5
  12.0 0.1 select_reduce_fusion.2
  12.1 0.5 select_reduce_fusion
  12.6 0.0 collective-permute-done
  12.6 2.9 %collective-permute-done.1 = bf16[8,256,128]{2,1,0:T(8,128)(2,1)S(1)} collective-permute-done((bf16[8,256,128]{2,1,0:T(8,128)(2,1)S(1)}, bf16[8,256,128]{2,1,0:T(8,128)(2,1)S(1)}, u32[]{:S(2)}, u32[]{:S(2)}) %collective-permute-start.1) | collective-permute-done | bytes 524320 | tf_op jit(solution)/shard_map/ppermute | solution.py:20
  15.5 0.2 pad_maximum_fusion
  15.8 2.3 %fusion.10 = bf16[2,8,256,128]{3,1,2,0:T(8,128)(2,1)S(1)} fusion(bf16[4,8,256,128]{3,2,1,0:T(8,128)(2,1)S(1)} %bitcast.75, f32[2,8,256,128]{3,2,1,0:T(8,128)S(1)} %convert.1, bf16[16,32]{1,0:T(8,128)(2,1)S(1)} %select_reduce_fusion.2), kind=kOutput, calls=%fused_computation.20 | convolution fusion | flops 34603008 | bytes 5243904 | tf_op jit(solution)/shard_map/dot_general | solution.py:51
  18.1 0.2 copy.59
  18.3 0.5 copy.38
  18.8 3.4 %collective-permute-start.2 = (bf16[16,256,8]{1,2,0:T(8,128)(2,1)S(1)}, bf16[16,256,8]{1,2,0:T(8,128)(2,1)S(1)}, u32[]{:S(2)}, u32[]{:S(2)}) collective-permute-start(bf16[16,256,8]{1,2,0:T(8,128)(2,1)S(1)} %get-tuple-element.12), channel_id=1, source_target_pairs={{0,8},{8,16},{16,24},{1,9},{9,17},{17,25},{2,10},{10,18},{18,26},{... | collective-permute-start | bytes 196616 | tf_op jit(solution)/shard_map/ppermute | solution.py:17
  22.3 3.3 %collective-permute-start.3 = (bf16[16,256,8]{1,2,0:T(8,128)(2,1)S(1)}, bf16[16,256,8]{1,2,0:T(8,128)(2,1)S(1)}, u32[]{:S(2)}, u32[]{:S(2)}) collective-permute-start(bf16[16,256,8]{1,2,0:T(8,128)(2,1)S(1)} %get-tuple-element.13), channel_id=1, source_target_pairs={{8,0},{16,8},{24,16},{9,1},{17,9},{25,17},{10,2},{18,10},{26,18},{... | collective-permute-start | bytes 196616 | tf_op jit(solution)/shard_map/ppermute | solution.py:20
  25.6 0.2 select_reduce_fusion.1
  25.8 0.1 collective-permute-done.2
  25.9 2.5 %collective-permute-done.3 = bf16[16,256,8]{1,2,0:T(8,128)(2,1)S(1)} collective-permute-done((bf16[16,256,8]{1,2,0:T(8,128)(2,1)S(1)}, bf16[16,256,8]{1,2,0:T(8,128)(2,1)S(1)}, u32[]{:S(2)}, u32[]{:S(2)}) %collective-permute-start.3) | collective-permute-done | bytes 65568 | tf_op jit(solution)/shard_map/ppermute | solution.py:20
  28.4 1.5 fusion.7
  30.0 0.7 copy.43
  30.6 0.3 reshape.57
  30.9 0.0 copy-done
  30.9 2.6 %fusion.1 = bf16[2,32,16384]{2,1,0:T(8,128)(2,1)} fusion(bf16[16,2,16384]{2,1,0:T(2,128)(2,1)S(1)} %reshape.57, bf16[2,1,32,16]{2,3,1,0:T(8,128)(2,1)S(1)} %copy-done), kind=kOutput, calls=%fused_computation.5 | convolution fusion | flops 34603008 | bytes 3147776 | tf_op jit(solution)/shard_map/tkf,ftp->tkp/dot_general | solution.py:74
  33.6 0.0 all-reduce.3.cloned.1.call-update
  33.6 0.0 all-reduce.5.cloned.1.call-start
  33.7 71.6 %all-reduce.3.cloned.1.call-done = bf16[2,32,16384]{2,1,0:T(8,128)(2,1)} async-done(((bf16[2,32,16384]{2,1,0:T(8,128)(2,1)}), bf16[2,32,16384]{2,1,0:T(8,128)(2,1)}) %all-reduce.3.cloned.1.call-update) | async-done | bytes 2097168 | tf_op jit(solution)/shard_map/psum | solution.py:68
  105.2 0.0 copy-start.2
  105.2 3.0 %fusion.47 = f32[2,32,32]{2,1,0:T(8,128)S(1)} fusion(bf16[2,32,16384]{2,1,0:T(8,128)(2,1)} %all-reduce.3.cloned.1.call-done), kind=kOutput, calls=%fused_computation.63 | convolution fusion | flops 67108864 | bytes 2105344 | tf_op jit(solution)/shard_map/vmap()/dot_general | solution.py:35
  108.3 0.1 copy.45
  108.4 6.0 %custom-call.8 = f32[2,32,32]{2,1,0:T(8,128)S(1)} custom-call(f32[2,32,32]{2,1,0:T(8,128)S(1)} %fusion.40), custom_call_target="Cholesky" | custom-call | tf_op jit(solution)/shard_map/vmap(jit(cholesky))/cholesky | solution.py:36
  114.5 0.1 compare_reduce_fusion.1
  114.6 0.1 select_bitcast_fusion.1
  114.7 4.9 %custom-call.9 = f32[2,1,32,32]{2,3,1,0:T(8,128)S(1)} custom-call(f32[2,1,32,32]{3,2,1,0:T(8,128)S(1)} %select_bitcast_fusion.1), custom_call_target="InvertDiagBlocksLowerTriangular" | custom-call | tf_op jit(solution)/shard_map/vmap(jit(_solve_triangular))/triangular_solve | solution.py:37
  119.6 0.0 copy-done.2
  119.6 4.8 %convolution_convert_fusion.1 = bf16[2,32,16384]{2,1,0:T(8,128)(2,1)} fusion(bf16[2,32,16384]{2,1,0:T(8,128)(2,1)S(1)} %copy-done.2, f32[2,1,32,32]{2,3,1,0:T(8,128)S(1)} %custom-call.9), kind=kOutput, calls=%fused_computation.3 | convolution fusion | flops 404750336 | bytes 4202496 | tf_op jit(solution)/shard_map/vmap(jit(_solve_triangular))/triangular_solve | solution.py:37
  124.4 5.3 %convolution_convert_fusion = bf16[2,32,16384]{2,1,0:T(8,128)(2,1)} fusion(bf16[2,32,16384]{2,1,0:T(8,128)(2,1)} %convolution_convert_fusion.1, bf16[16,2,16384]{2,1,0:T(2,128)(2,1)S(1)} %reshape.57), kind=kOutput, calls=%fused_computation.2 | convolution fusion | flops 68158464 | bytes 5242880 | tf_op jit(solution)/shard_map/ftk,ftp->tkp/dot_general | solution.py:79
  129.6 0.0 all-reduce.5.cloned.1.call-update
  129.7 64.7 %all-reduce.5.cloned.1.call-done = bf16[2,32,16384]{2,1,0:T(8,128)(2,1)} async-done(((bf16[2,32,16384]{2,1,0:T(8,128)(2,1)}), bf16[2,32,16384]{2,1,0:T(8,128)(2,1)}) %all-reduce.5.cloned.1.call-update) | async-done | bytes 2097168 | tf_op jit(solution)/shard_map/psum | solution.py:68
  194.3 0.0 copy-start.1
  194.3 3.0 %fusion.48 = f32[2,32,32]{2,1,0:T(8,128)S(1)} fusion(bf16[2,32,16384]{2,1,0:T(8,128)(2,1)} %all-reduce.5.cloned.1.call-done), kind=kOutput, calls=%fused_computation.64 | convolution fusion | flops 67108864 | bytes 2105344 | tf_op jit(solution)/shard_map/vmap()/dot_general | solution.py:35
  197.4 0.1 copy.49
  197.5 5.9 %custom-call.10 = f32[2,32,32]{2,1,0:T(8,128)S(1)} custom-call(f32[2,32,32]{2,1,0:T(8,128)S(1)} %fusion.38), custom_call_target="Cholesky" | custom-call | tf_op jit(solution)/shard_map/vmap(jit(cholesky))/cholesky | solution.py:36
  203.4 0.1 compare_reduce_fusion
  203.5 0.1 select_bitcast_fusion
  203.6 4.9 %custom-call.11 = f32[2,1,32,32]{2,3,1,0:T(8,128)S(1)} custom-call(f32[2,1,32,32]{3,2,1,0:T(8,128)S(1)} %select_bitcast_fusion), custom_call_target="InvertDiagBlocksLowerTriangular" | custom-call | tf_op jit(solution)/shard_map/vmap(jit(_solve_triangular))/triangular_solve | solution.py:37
  208.5 0.0 copy-done.1
  208.5 3.9 %fusion.2 = f32[2,32,16384]{2,1,0:T(8,128)S(1)} fusion(bf16[2,32,16384]{2,1,0:T(8,128)(2,1)S(1)} %copy-done.1, f32[2,1,32,32]{2,3,1,0:T(8,128)S(1)} %custom-call.11), kind=kOutput, calls=%fused_computation.9 | convolution fusion | flops 403701760 | bytes 6299648 | tf_op jit(solution)/shard_map/vmap(jit(_solve_triangular))/triangular_solve | solution.py:37
  212.3 1.5 fusion.23
  213.8 0.7 copy.60
  214.5 0.5 bitcast_bitcast_fusion
  215.0 0.5 copy.51
  215.5 0.9 dynamic-slice_multiply_fusion
  (12 shorter events, 0.2 us)
Async XLA Ops:
  7.2 23.8 %copy-start = (bf16[2,1,32,16]{2,3,1,0:T(8,128)(2,1)S(1)}, bf16[2,1,32,16]{2,3,1,0:T(8,128)(2,1)}, u32[]{:S(2)}) copy-start(bf16[2,1,32,16]{2,3,1,0:T(8,128)(2,1)} %param.8) | copy-start | bytes 6148
  7.2 4.5 %copy-start.3 = (bf16[16,256,128]{2,1,0:T(8,128)(2,1)S(1)}, bf16[16,256,128]{2,1,0:T(8,128)(2,1)}, u32[]{:S(2)}) copy-start(bf16[16,256,128]{2,1,0:T(8,128)(2,1)} %param.7) | copy-start | bytes 3145732
  7.2 98.1 %all-reduce.3.cloned.1.call-start = ((), (), s32[]{:S(2)}) async-start(), calls=%async_computation | async-start | bytes 4194304 | tf_op jit(solution)/shard_map/psum | solution.py:68
  8.6 3.3 %copy-start.4 = (bf16[17]{0:T(256)(128)(2,1)S(1)}, bf16[17]{0:T(256)(128)(2,1)}, u32[]{:S(2)}) copy-start(bf16[17]{0:T(256)(128)(2,1)} %param.9) | copy-start | bytes 106
  8.6 3.3 %copy-start.5 = (bf16[17]{0:T(256)(128)(2,1)S(1)}, bf16[17]{0:T(256)(128)(2,1)}, u32[]{:S(2)}) copy-start(bf16[17]{0:T(256)(128)(2,1)} %param.10) | copy-start | bytes 106
  8.6 4.0 %collective-permute-start = (bf16[8,256,128]{2,1,0:T(8,128)(2,1)S(1)}, bf16[8,256,128]{2,1,0:T(8,128)(2,1)S(1)}, u32[]{:S(2)}, u32[]{:S(2)}) collective-permute-start(bf16[8,256,128]{2,1,0:T(8,128)(2,1)S(1)} %get-tuple-element.14), channel_id=1, source_target_pairs={{0,1},{1,2},{2,3},{3,4},{4,5},{5,6},{6,7},{8,9},{9,10},{10,11},{11... | collective-permute-start | bytes 1572872 | tf_op jit(solution)/shard_map/ppermute | solution.py:17
  10.4 5.1 %collective-permute-start.1 = (bf16[8,256,128]{2,1,0:T(8,128)(2,1)S(1)}, bf16[8,256,128]{2,1,0:T(8,128)(2,1)S(1)}, u32[]{:S(2)}, u32[]{:S(2)}) collective-permute-start(bf16[8,256,128]{2,1,0:T(8,128)(2,1)S(1)} %get-tuple-element.15), channel_id=1, source_target_pairs={{1,0},{2,1},{3,2},{4,3},{5,4},{6,5},{7,6},{9,8},{10,9},{11,10},{12... | collective-permute-start | bytes 1572872 | tf_op jit(solution)/shard_map/ppermute | solution.py:20
  18.8 7.1 %collective-permute-start.2 = (bf16[16,256,8]{1,2,0:T(8,128)(2,1)S(1)}, bf16[16,256,8]{1,2,0:T(8,128)(2,1)S(1)}, u32[]{:S(2)}, u32[]{:S(2)}) collective-permute-start(bf16[16,256,8]{1,2,0:T(8,128)(2,1)S(1)} %get-tuple-element.12), channel_id=1, source_target_pairs={{0,8},{8,16},{16,24},{1,9},{9,17},{17,25},{2,10},{10,18},{18,26},{... | collective-permute-start | bytes 196616 | tf_op jit(solution)/shard_map/ppermute | solution.py:17
  22.3 6.2 %collective-permute-start.3 = (bf16[16,256,8]{1,2,0:T(8,128)(2,1)S(1)}, bf16[16,256,8]{1,2,0:T(8,128)(2,1)S(1)}, u32[]{:S(2)}, u32[]{:S(2)}) collective-permute-start(bf16[16,256,8]{1,2,0:T(8,128)(2,1)S(1)} %get-tuple-element.13), channel_id=1, source_target_pairs={{8,0},{16,8},{24,16},{9,1},{17,9},{25,17},{10,2},{18,10},{26,18},{... | collective-permute-start | bytes 196616 | tf_op jit(solution)/shard_map/ppermute | solution.py:20
  33.6 160.7 %all-reduce.5.cloned.1.call-start = ((), (), s32[]{:S(2)}) async-start(), calls=%async_computation.1 | async-start | bytes 4194304 | tf_op jit(solution)/shard_map/psum | solution.py:68
  105.2 14.3 %copy-start.2 = (bf16[2,32,16384]{2,1,0:T(8,128)(2,1)S(1)}, bf16[2,32,16384]{2,1,0:T(8,128)(2,1)}, u32[]{:S(2)}) copy-start(bf16[2,32,16384]{2,1,0:T(8,128)(2,1)} %all-reduce.3.cloned.1.call-done) | copy-start | bytes 6291460
  194.3 14.2 %copy-start.1 = (bf16[2,32,16384]{2,1,0:T(8,128)(2,1)S(1)}, bf16[2,32,16384]{2,1,0:T(8,128)(2,1)}, u32[]{:S(2)}) copy-start(bf16[2,32,16384]{2,1,0:T(8,128)(2,1)} %all-reduce.5.cloned.1.call-done) | copy-start | bytes 6291460
Sparse Core Ops, SparseCore 0:
  33.7 71.4 all-reduce.2
  129.8 64.4 all-reduce.4
where the time goes:
time: 225 us; the launch traced here: 223 us
  waiting for transfers between devices  142 us (63%)
  matrix products  27.9 us (12%)
  other arithmetic  24.3 us (11%)
  between operations  14.3 us (6%)
  starting transfers between devices  9.88 us (4%)
  local copies, waits for them, and re-layouts  4.95 us (2%)
    psum x2, waiting for transfers between devices, subspace(): lax.psum(partial_value.astype(jnp.bfloat16), 'tm').astype(jnp.float32)  136 us
    another operation x7, other arithmetic, orthonormal(): factor_low = jnp.linalg.cholesky(gram_block)  12.2 us
    another operation x5, other arithmetic, orthonormal(): return jax.scipy.linalg.solve_triangular(factor_low, matrix, lower=True)  9.99 us
    another operation x2, matrix products, orthonormal(): return jax.scipy.linalg.solve_triangular(factor_low, matrix, lower=True)  8.64 us
    dot_general x2, matrix products, orthonormal(): gram_block = jnp.dot(matrix, matrix.T, precision=lax.Precision.HIGHEST)  6.08 us
    ppermute x2, waiting for transfers between devices, with_halo(): lax.ppermute(lax.slice_in_dim(block, 0, width, axis=dim), axis, backward)  5.41 us
    dot_general x1, matrix products, local(): jnp.einsum('ftk,ftp->tkp', loadings, filtered, preferred_element_type=jnp...  5.26 us
    ppermute x2, starting transfers between devices, with_halo(): lax.ppermute(lax.slice_in_dim(block, block.shape[dim] - width, None, axis...  5.17 us
  transfers between devices with their start and end apart: 6, of which 5 were waited for; matrix products, arithmetic and copies ran while one was open for 0% of the time, Pallas kernels for 0%

commit v1 on v0

v1 whole, which is shorter than its diff:
```python
import functools
import math

import jax
import jax.numpy as jnp
from jax import lax
from jax.experimental import pallas as pl
from jax.experimental.pallas import tpu as pltpu
from jax.sharding import PartitionSpec as P

TY = 2
VMEM = pl.BlockSpec(memory_space=pltpu.VMEM)
SMEM = pl.BlockSpec(memory_space=pltpu.SMEM)
F32 = jnp.float32
BF16 = jnp.bfloat16
PARAMS = pltpu.CompilerParams(vmem_limit_bytes=40 * 1024 * 1024)


def call(kernel, outs, ins, scratch=(), flops=0):
    moved = sum(v.size * v.dtype.itemsize for v in (*outs, *ins))
    return pl.pallas_call(
        kernel,
        out_shape=outs,
        in_specs=[VMEM] * len(ins),
        out_specs=[VMEM] * len(outs),
        scratch_shapes=scratch,
        compiler_params=PARAMS,
        cost_estimate=pl.CostEstimate(flops=flops, bytes_accessed=moved, transcendentals=0),
    )(*ins)


def toeplitz(taps, rows, cols, shift):
    offsets = (
        lax.broadcasted_iota(jnp.int32, (rows, cols), 1)
        - lax.broadcasted_iota(jnp.int32, (rows, cols), 0)
        + shift
    )
    picks = jnp.arange(taps.shape[0], dtype=jnp.int32)
    hits = (offsets[:, :, None] == picks).astype(F32)
    return jnp.sum(hits * taps.astype(F32), axis=2)


def contract(left, right, left_dim, right_dim):
    return lax.dot_general(
        left, right, (((left_dim,), (right_dim,)), ((), ())), preferred_element_type=F32
    )


def split(value):
    high = value.astype(BF16)
    return high, (value - high.astype(F32)).astype(BF16)


def edges_kernel(x_ref, low_ref, high_ref):
    frames, _, cols = x_ref.shape
    width = low_ref.shape[1]
    row = lax.broadcasted_iota(jnp.int32, (2 * width, cols), 0)
    col = lax.broadcasted_iota(jnp.int32, (2 * width, cols), 1)
    wanted = jnp.where(row < width, row, row + cols - 2 * width)
    pick = jnp.where(col == wanted, 1.0, 0.0).astype(BF16)
    for f in range(frames):
        both = contract(pick, x_ref[f], 1, 1).astype(BF16)
        low_ref[f] = both[:width]
        high_ref[f] = both[width:]


def spatial_kernel(axis, x_ref, hl_ref, hr_ref, bx_ref, bh_ref, dy_ref, om_ref, *rest):
    outs, rows_scr, anchor_scr = rest[:-2], rest[-2], rest[-1]
    frames, rows, cols = x_ref.shape
    count = len(outs)
    share = rows // count
    ranks = om_ref.shape[2]
    me = lax.axis_index(axis)
    bx, bh, dy = bx_ref[...], bh_ref[...], dy_ref[...]

    def halo(f):
        return jnp.concatenate([hl_ref[f].astype(F32), hr_ref[f].astype(F32)], axis=0)

    total = jnp.zeros((rows, cols), F32)
    halo_total = jnp.zeros((bh.shape[0], rows), F32)
    for f in range(frames):
        total = total + x_ref[f].astype(F32)
        halo_total = halo_total + halo(f)
    anchor = (total * (1.0 / frames)).astype(BF16)
    halo_anchor = (halo_total * (1.0 / frames)).astype(BF16)

    def across(block, edge):
        return contract(block, bx, 1, 0) + contract(edge, bh, 0, 0)

    high, low = split(across(anchor, halo_anchor))
    both = contract(dy, jnp.concatenate([high, low], axis=1), 1, 0)
    anchor_s = anchor.astype(F32) - both[:, :cols] - both[:, cols:]
    anchor_out = anchor_s.astype(BF16)
    anchor_scr[...] = anchor_out
    left_over = anchor_s - anchor_out.astype(F32)
    anchor32 = anchor.astype(F32)
    halo32 = halo_anchor.astype(F32)

    def pair(p, carry):
        blocks, smooths = [], []
        for f in (2 * p, 2 * p + 1):
            block = (x_ref[f].astype(F32) - anchor32).astype(BF16)
            edge = (halo(f) - halo32).astype(BF16)
            blocks.append(block)
            smooths.append(across(block, edge).astype(BF16))
        both = contract(dy, jnp.concatenate(smooths, axis=1), 1, 0)
        for i, f in enumerate((2 * p, 2 * p + 1)):
            value = blocks[i].astype(F32) - both[:, i * cols : (i + 1) * cols] + left_over
            rows_scr[pl.ds(f, rows, stride=frames), :] = value
        return carry

    lax.fori_loop(0, frames // 2, pair, 0)
    for k, out in enumerate(outs):
        dest = me ^ k
        start = pl.multiple_of(dest * (share * frames), share * frames)
        block = rows_scr[pl.ds(start, share * frames), :].astype(BF16)
        out[0:share] = block.reshape(share, frames, cols)
        start = pl.multiple_of(dest * share, share)
        out[share : share + share // frames] = anchor_scr[pl.ds(start, share), :].reshape(
            share // frames, frames, cols
        )
        out[share + share // frames, :, 0:ranks] = om_ref[dest // (count // TY)]
        out[share + share // frames, :, ranks:] = jnp.zeros((frames, cols - ranks), BF16)


def temporal_kernel(axis, *refs):
    count = len(refs) - 7
    pieces = refs[:count]
    lhs_ref, m_ref, gram_ref, om_ref, data_scr, anchor_scr, gram_scr = refs[count:]
    share, _, frames, cols = data_scr.shape
    all_frames = count * frames
    me = lax.axis_index(axis)
    for k in range(count):
        src = me ^ k
        data_scr[:, src] = pieces[k][0:share]
        anchor = pieces[k][share : share + share // frames].reshape(share, cols)
        anchor_scr[pl.ds(src, share, stride=count), :] = anchor.astype(F32)
        om_ref[src] = pieces[k][share + share // frames]
    lhs = lhs_ref[...]
    gram_scr[...] = jnp.zeros_like(gram_scr)

    def pair(p, carry):
        blocks, feeds = [], []
        for r in (2 * p, 2 * p + 1):
            block = data_scr[r].reshape(all_frames, cols)
            start = pl.multiple_of(r * count, count)
            anchor = anchor_scr[pl.ds(start, count), :]
            blocks.append(block)
            feeds.append(
                jnp.concatenate([block, jnp.concatenate([anchor, anchor], 0).astype(BF16)], axis=0)
            )
        low = contract(lhs, jnp.concatenate(feeds, axis=1), 1, 0)
        value = (jnp.concatenate(blocks, axis=1).astype(F32) + low).astype(BF16)
        m_ref[2 * p] = value[:, :cols]
        m_ref[2 * p + 1] = value[:, cols:]
        gram_scr[...] += contract(value, value, 1, 1)
        return carry

    lax.fori_loop(0, share // 2, pair, 0)
    gram_ref[...] = gram_scr[...]


def exact(left, right, left_dim, right_dim):
    return lax.dot_general(
        left,
        right,
        (((left_dim,), (right_dim,)), ((), ())),
        precision=lax.Precision.HIGHEST,
        preferred_element_type=F32,
    )


def whiten(gram, *others):
    size = gram.shape[0]
    ids = lax.broadcasted_iota(jnp.int32, (size, 128), 0)
    work = [jnp.concatenate([gram, jnp.zeros((size, 128 - size), F32)], axis=1), *others]
    scale = jnp.zeros((size, 128), F32)
    panel = 8
    for start in range(0, size, panel):
        cols = [
            jnp.broadcast_to(work[0][:, j : j + 1], (size, 128)) for j in range(start, start + panel)
        ]
        for j in range(start, start + panel):
            inverse = 1.0 / cols[j - start][j : j + 1]
            factor = jnp.where(ids > j, cols[j - start] * inverse, 0.0)
            scale = jnp.where(ids == j, inverse, scale)
            for m in range(j - start + 1, panel):
                cols[m] = cols[m] - factor * cols[m][j : j + 1]
            for i in range(len(work)):
                value = work[i]
                width = value.shape[1]
                parts = [
                    value[:, c : c + 128] - factor * value[j : j + 1, c : c + 128]
                    for c in range(0, width, 128)
                ]
                work[i] = parts[0] if len(parts) == 1 else jnp.concatenate(parts, axis=1)
    scale = jnp.sqrt(scale)
    results = []
    for value in work[1:]:
        parts = [value[:, c : c + 128] * scale for c in range(0, value.shape[1], 128)]
        results.append(parts[0] if len(parts) == 1 else jnp.concatenate(parts, axis=1))
    return results


def factor_kernel(axis, count, ranks, pixels, om_ref, *refs):
    grams, (mix_ref, own_ref, send_ref) = refs[:-3], refs[-3:]
    frames = own_ref.shape[1]
    all_frames = grams[0].shape[0]
    me = lax.axis_index(axis)
    gram = grams[0][...]
    for other in grams[1:]:
        gram = gram + other[...]
    omega = om_ref[...].reshape(all_frames, om_ref.shape[2]).astype(F32).T[:ranks]
    sketch = exact(omega, gram, 1, 0)
    (load,) = whiten(exact(sketch, omega, 1, 1), sketch)
    back = exact(load, gram, 1, 0)
    mix, coef = whiten(exact(back, load, 1, 1), load, back)
    mix_ref[...] = mix * math.sqrt(pixels)
    ids = lax.broadcasted_iota(jnp.int32, (all_frames, frames), 0)
    lane = lax.broadcasted_iota(jnp.int32, (all_frames, frames), 1)
    for ref, who in ((own_ref, me), (send_ref, me ^ (count // TY))):
        pick = jnp.where(ids == lane + who * frames, 1.0, 0.0)
        ref[...] = exact(coef, pick, 1, 0)


def basis_kernel(m_ref, mix_ref, out_ref):
    share, _, cols = m_ref.shape
    ranks = mix_ref.shape[0]
    high, low = split(mix_ref[...])
    lhs = jnp.concatenate([high, low], axis=0)
    for p in range(share // 2):
        data = jnp.concatenate([m_ref[2 * p], m_ref[2 * p + 1]], axis=1)
        both = contract(lhs, data, 1, 0)
        value = both[:ranks] + both[ranks:]
        for i in range(2):
            out_ref[pl.ds(2 * p + i, ranks, stride=share), :] = value[:, i * cols : (i + 1) * cols]


def local(movie, omega, time_taps, space_taps):
    frames, rows, cols = movie.shape
    radius = (space_taps.shape[0] - 1) // 2
    count = lax.axis_size("tm")
    tiles = lax.axis_size("tile")
    ranks = omega.shape[2]
    share = rows // count
    all_frames = frames * count
    group = count // TY
    pixels = (rows // TY) * cols

    def shape(dims, dtype):
        return jax.ShapeDtypeStruct(dims, dtype)

    low, high = call(edges_kernel, [shape((frames, radius, rows), BF16)] * 2, [movie])
    right = [(i, i + 1) for i in range(tiles - 1)]
    left = [(j, i) for i, j in right]
    halo_left = lax.ppermute(high, "tile", right)
    halo_right = lax.ppermute(low, "tile", left)

    taps_back = space_taps[::-1]
    bx = toeplitz(taps_back, cols, cols, radius).astype(BF16)
    bh = jnp.concatenate(
        [
            toeplitz(taps_back, radius, cols, 2 * radius),
            toeplitz(taps_back, radius, cols, radius - cols),
        ],
        axis=0,
    ).astype(BF16)
    dy = toeplitz(space_taps, rows, rows, radius).astype(BF16)
    band = toeplitz(time_taps, all_frames, all_frames, radius)
    own = (
        lax.broadcasted_iota(jnp.int32, (all_frames, count), 0) // frames
        == lax.broadcasted_iota(jnp.int32, (all_frames, count), 1)
    ).astype(F32)
    sums = own - jnp.sum(band.reshape(all_frames, count, frames), axis=2)
    sums_high = lax.reduce_precision(sums, 8, 7)
    lhs = jnp.concatenate([-band, sums_high, sums - sums_high], axis=1).astype(BF16)

    om = jnp.transpose(omega[:, 0], (0, 2, 1))
    slots = share + share // frames + 1
    pieces = call(
        functools.partial(spatial_kernel, "tm"),
        [shape((slots, frames, cols), BF16)] * count,
        [movie, halo_left, halo_right, bx, bh, dy, om],
        [pltpu.VMEM((rows * frames, cols), F32), pltpu.VMEM((rows, cols), BF16)],
    )
    pieces = [pieces[0]] + [
        lax.ppermute(pieces[k], "tm", [(i, i ^ k) for i in range(count)]) for k in range(1, count)
    ]
    matrix, gram, om_all = call(
        functools.partial(temporal_kernel, "tm"),
        [
            shape((share, all_frames, cols), BF16),
            shape((all_frames, all_frames), F32),
            shape((count, frames, cols), BF16),
        ],
        [*pieces, lhs],
        [
            pltpu.VMEM((share, count, frames, cols), BF16),
            pltpu.VMEM((share * count, cols), F32),
            pltpu.VMEM((all_frames, all_frames), F32),
        ],
    )
    grams = [gram] + [
        lax.ppermute(gram, "tm", [(i, i ^ k) for i in range(count)]) for k in range(1, group)
    ]
    mix, coef_own, coef_send = call(
        functools.partial(factor_kernel, "tm", count, ranks, pixels),
        [shape((ranks, all_frames), F32), *([shape((ranks, frames), F32)] * 2)],
        [om_all, *grams],
    )
    coef_other = lax.ppermute(coef_send, "tm", [(i, i ^ group) for i in range(count)])
    (basis,) = call(basis_kernel, [shape((ranks * share, cols), F32)], [matrix, mix])
    tile_row = lax.axis_index("tm") // group
    first = jnp.where(tile_row == 0, coef_own, coef_other)
    second = jnp.where(tile_row == 0, coef_other, coef_own)
    return basis.reshape(ranks, share, cols), jnp.stack([first, second])[:, None]


def solution(mesh):
    in_specs = (P("tm", None, "tile"), P(None, "tile", None, "tm"), P(), P())
    out_specs = (P(None, "tm", "tile"), P(None, "tile", None, "tm"))
    return jax.shard_map(local, mesh=mesh, in_specs=in_specs, out_specs=out_specs, check_vma=False)
```

time: 225 us -> 66.6 us (0.30)
  the two profiles are of different devices: /device:TPU:4 before, /device:TPU:0 now
where the time goes in v1:
time: 66.6 us; the launch traced here: 66.4 us
  starting transfers between devices  24.7 us (37%)
  waiting for transfers between devices  23.6 us (35%)
  Pallas kernels  14 us (21%)
  local copies, waits for them, and re-layouts  2.3 us (3%)
  other arithmetic  1.06 us (2%)
  between operations  0.81 us (1%)
    ppermute x7, waiting for transfers between devices, local(): lax.ppermute(pieces[k], 'tm', [(i, i ^ k) for i in range(count)])  15.6 us
    pallas_call x5, Pallas kernels, call(): pl.pallas_call(kernel, out_shape=outs, in_specs=[VMEM] * len(ins), out_sp...  14 us
    ppermute x7, starting transfers between devices, local(): lax.ppermute(pieces[k], 'tm', [(i, i ^ k) for i in range(count)])  8.2 us
    ppermute x3, starting transfers between devices, local(): lax.ppermute(gram, 'tm', [(i, i ^ k) for i in range(count)])  7.6 us
    ppermute x1, starting transfers between devices, local(): halo_left = lax.ppermute(high, 'tile', right)  4.86 us
    ppermute x3, waiting for transfers between devices, local(): lax.ppermute(gram, 'tm', [(i, i ^ k) for i in range(count)])  3.69 us
    ppermute x1, waiting for transfers between devices, local(): halo_right = lax.ppermute(low, 'tile', left)  3.42 us
    ppermute x1, starting transfers between devices, local(): lax.ppermute(coef_send, 'tm', [(i, i ^ group) for i in range(count)])  2.72 us
  transfers between devices with their start and end apart: 13, of which 7 were waited for; matrix products, arithmetic and copies ran while one was open for 2% of the time, Pallas kernels for 2%

profile of v1, /device:TPU:0, one launch (start us, length us, event | category | flops | bytes accessed | tf_op | source)
XLA Modules:
  0.0 66.4 jit_solution(3059211223136511784)
XLA Ops:
  0.6 0.0 copy-start
  0.6 1.2 %copy-done = bf16[16,256,128]{2,1,0:T(8,128)(2,1)S(1)} copy-done((bf16[16,256,128]{2,1,0:T(8,128)(2,1)S(1)}, bf16[16,256,128]{2,1,0:T(8,128)(2,1)}, u32[]{:S(2)}) %copy-start) | copy-done | bytes 1048600
  1.9 0.0 copy-start.3
  1.9 0.0 copy-start.4
  1.9 0.0 copy-start.1
  1.9 0.0 copy-start.2
  1.9 0.4 shard_map.59
  2.2 4.9 %collective-permute-start = (bf16[16,8,256]{2,1,0:T(8,128)(2,1)S(1)}, bf16[16,8,256]{2,1,0:T(8,128)(2,1)S(1)}, u32[]{:S(2)}, u32[]{:S(2)}) collective-permute-start(bf16[16,8,256]{2,1,0:T(8,128)(2,1)S(1)} %get-tuple-element.18), channel_id=1, source_target_pairs={{0,8},{8,16},{16,24},{1,9},{9,17},{17,25},{2,10},{10,18},{18,26},{... | collective-permute-start | bytes 196616 | tf_op jit(solution)/shard_map/ppermute | solution.py:256
  7.1 1.3 %collective-permute-start.1 = (bf16[16,8,256]{2,1,0:T(8,128)(2,1)S(1)}, bf16[16,8,256]{2,1,0:T(8,128)(2,1)S(1)}, u32[]{:S(2)}, u32[]{:S(2)}) collective-permute-start(bf16[16,8,256]{2,1,0:T(8,128)(2,1)S(1)} %get-tuple-element.19), channel_id=1, source_target_pairs={{8,0},{16,8},{24,16},{9,1},{17,9},{25,17},{10,2},{18,10},{26,18},{... | collective-permute-start | bytes 196616 | tf_op jit(solution)/shard_map/ppermute | solution.py:257
  8.5 0.0 copy-done.3
  8.5 0.1 rev.3
  8.6 0.0 copy-done.4
  8.6 0.3 select_reduce_fusion.1
  8.9 0.1 copy.15
  9.0 0.1 copy.17
  9.1 0.1 copy.16
  9.2 0.1 select_reduce_fusion.4
  9.3 0.5 select_reduce_fusion.dy_ref
  9.8 0.0 collective-permute-done.hl_ref
  9.8 3.4 %collective-permute-done.1.hr_ref = bf16[16,8,256]{2,1,0:T(8,128)(2,1)S(1)} collective-permute-done((bf16[16,8,256]{2,1,0:T(8,128)(2,1)S(1)}, bf16[16,8,256]{2,1,0:T(8,128)(2,1)S(1)}, u32[]{:S(2)}, u32[]{:S(2)}) %collective-permute-start.1) | collective-permute-done | bytes 65568 | tf_op jit(solution)/shard_map/ppermute | solution.py:257
  13.3 0.0 copy-done.1
  13.3 0.0 copy-done.2
  13.3 4.6 %shard_map.60 = (bf16[35,16,128]{2,1,0:T(8,128)(2,1)S(1)}, bf16[35,16,128]{2,1,0:T(8,128)(2,1)S(1)}, bf16[35,16,128]{2,1,0:T(8,128)(2,1)S(1)}, bf16[35,16,128]{2...) custom-call(bf16[16,256,128]{2,1,0:T(8,128)(2,1)S(1)} %copy-done.1, ...), custom_call_target="tpu_custom_call" | custom-call | bytes 2496512 | tf_op jit(solution)/shard_map/pallas_call | solution.py:21
  17.8 0.1 collective-permute-start.2
  17.9 1.6 %collective-permute-start.3 = (bf16[35,16,128]{2,1,0:T(8,128)(2,1)S(1)}, bf16[35,16,128]{2,1,0:T(8,128)(2,1)S(1)}, u32[]{:S(2)}, u32[]{:S(2)}) collective-permute-start(bf16[35,16,128]{2,1,0:T(8,128)(2,1)S(1)} %get-tuple-element.22), channel_id=1, source_target_pairs={{0,2},{1,3},{2,0},{3,1},{4,6},{5,7},{6,4},{7,5},{8,10},{9,11},{10,... | collective-permute-start | bytes 430088 | tf_op jit(solution)/shard_map/ppermute | solution.py:287
  19.6 0.3 collective-permute-start.4
  19.9 2.6 %collective-permute-start.5 = (bf16[35,16,128]{2,1,0:T(8,128)(2,1)S(1)}, bf16[35,16,128]{2,1,0:T(8,128)(2,1)S(1)}, u32[]{:S(2)}, u32[]{:S(2)}) collective-permute-start(bf16[35,16,128]{2,1,0:T(8,128)(2,1)S(1)} %get-tuple-element.24), channel_id=1, source_target_pairs={{0,4},{1,5},{2,6},{3,7},{4,0},{5,1},{6,2},{7,3},{8,12},{9,13},{10,... | collective-permute-start | bytes 430088 | tf_op jit(solution)/shard_map/ppermute | solution.py:287
  22.4 0.0 collective-permute-start.6
  22.5 0.0 collective-permute-done.2.refs_1_
  22.5 3.6 %collective-permute-start.7 = (bf16[35,16,128]{2,1,0:T(8,128)(2,1)S(1)}, bf16[35,16,128]{2,1,0:T(8,128)(2,1)S(1)}, u32[]{:S(2)}, u32[]{:S(2)}) collective-permute-start(bf16[35,16,128]{2,1,0:T(8,128)(2,1)S(1)} %get-tuple-element.26), channel_id=1, source_target_pairs={{0,6},{1,7},{2,4},{3,5},{4,2},{5,3},{6,0},{7,1},{8,14},{9,15},{10,... | collective-permute-start | bytes 430088 | tf_op jit(solution)/shard_map/ppermute | solution.py:287
  26.1 4.0 %collective-permute-done.3.refs_2_ = bf16[35,16,128]{2,1,0:T(8,128)(2,1)S(1)} collective-permute-done((bf16[35,16,128]{2,1,0:T(8,128)(2,1)S(1)}, bf16[35,16,128]{2,1,0:T(8,128)(2,1)S(1)}, u32[]{:S(2)}, u32[]{:S(2)}) %collective-permute-start.3) | collective-permute-done | bytes 143392 | tf_op jit(solution)/shard_map/ppermute | solution.py:287
  30.1 0.0 collective-permute-start.8
  30.1 0.1 pad_maximum_fusion.refs_8_
  30.2 2.1 %collective-permute-done.4.refs_3_ = bf16[35,16,128]{2,1,0:T(8,128)(2,1)S(1)} collective-permute-done((bf16[35,16,128]{2,1,0:T(8,128)(2,1)S(1)}, bf16[35,16,128]{2,1,0:T(8,128)(2,1)S(1)}, u32[]{:S(2)}, u32[]{:S(2)}) %collective-permute-start.4) | collective-permute-done | bytes 143392 | tf_op jit(solution)/shard_map/ppermute | solution.py:287
  32.2 0.0 collective-permute-done.5.refs_4_
  32.3 9.5 %collective-permute-done.6.refs_5_ = bf16[35,16,128]{2,1,0:T(8,128)(2,1)S(1)} collective-permute-done((bf16[35,16,128]{2,1,0:T(8,128)(2,1)S(1)}, bf16[35,16,128]{2,1,0:T(8,128)(2,1)S(1)}, u32[]{:S(2)}, u32[]{:S(2)}) %collective-permute-start.6) | collective-permute-done | bytes 143392 | tf_op jit(solution)/shard_map/ppermute | solution.py:287
  41.8 0.0 collective-permute-done.7.refs_6_
  41.8 0.0 collective-permute-done.8.refs_7_
  41.8 5.3 %shard_map.61 = (bf16[32,128,128]{2,1,0:T(8,128)(2,1)S(1)}, f32[128,128]{1,0:T(8,128)S(1)}, bf16[8,16,128]{2,1,0:T(8,128)(2,1)S(1)}) custom-call(bf16[35,16,128]{2,1,0:T(8,128)(2,1)S(1)} %get-tuple-element.20.refs_0_, bf16[35,16,128]{2,1,0:T(8,128)(2,1)S(1)} %collective-permute-done.2.refs_1_, bf16[35,16,128]{2,1,0:T(8,128)(2,1)S(1)} %collective-permute-done.3.refs_2_, ...), custom_call_target="tpu_custom_call" | custom-call | bytes 2330624 | tf_op jit(solution)/shard_map/pallas_call | solution.py:21
  47.1 7.4 %collective-permute-start.10 = (f32[128,128]{1,0:T(8,128)S(1)}, f32[128,128]{1,0:T(8,128)S(1)}, u32[]{:S(2)}, u32[]{:S(2)}) collective-permute-start(f32[128,128]{1,0:T(8,128)S(1)} %get-tuple-element.30.refs_0_), channel_id=1, source_target_pairs={{0,2},{1,3},{2,0},{3,1},{4,6},{5,7},{6,4},{7,5},{8,10},{9,11},{10,... | collective-permute-start | bytes 196616 | tf_op jit(solution)/shard_map/ppermute | solution.py:304
  54.5 0.0 collective-permute-start.11
  54.5 0.2 collective-permute-start.9
  54.7 2.1 %collective-permute-done.10.refs_2_ = f32[128,128]{1,0:T(8,128)S(1)} collective-permute-done((f32[128,128]{1,0:T(8,128)S(1)}, f32[128,128]{1,0:T(8,128)S(1)}, u32[]{:S(2)}, u32[]{:S(2)}) %collective-permute-start.10) | collective-permute-done | bytes 65568 | tf_op jit(solution)/shard_map/ppermute | solution.py:304
  56.7 1.6 %collective-permute-done.11.refs_3_ = f32[128,128]{1,0:T(8,128)S(1)} collective-permute-done((f32[128,128]{1,0:T(8,128)S(1)}, f32[128,128]{1,0:T(8,128)S(1)}, u32[]{:S(2)}, u32[]{:S(2)}) %collective-permute-start.11) | collective-permute-done | bytes 65568 | tf_op jit(solution)/shard_map/ppermute | solution.py:304
  58.4 0.0 collective-permute-done.9.refs_1_
  58.4 2.5 %shard_map.62 = (f32[32,128]{1,0:T(8,128)S(1)}, f32[32,16]{1,0:T(8,128)S(1)}, f32[32,16]{1,0:T(8,128)S(1)}) custom-call(bf16[8,16,128]{2,1,0:T(8,128)(2,1)S(1)} %get-tuple-element.29.om_ref, f32[128,128]{1,0:T(8,128)S(1)} %get-tuple-element.30.refs_0_, f32[128,128]{1,0:T(8,128)S(1)} %collective-permute-done.9.refs_1_, ...), custom_call_target="tpu_custom_call" | custom-call | bytes 315392 | tf_op jit(solution)/shard_map/pallas_call | solution.py:21
  60.9 2.7 %collective-permute-start.12 = (f32[32,16]{1,0:T(8,128)S(1)}, f32[32,16]{1,0:T(8,128)S(1)}, u32[]{:S(2)}, u32[]{:S(2)}) collective-permute-start(f32[32,16]{1,0:T(8,128)S(1)} %get-tuple-element.33), channel_id=1, source_target_pairs={{0,4},{1,5},{2,6},{3,7},{4,0},{5,1},{6,2},{7,3},{8,12},{9,13},{10,... | collective-permute-start | bytes 6152 | tf_op jit(solution)/shard_map/ppermute | solution.py:311
  63.6 1.3 %shard_map.63 = f32[1024,128]{1,0:T(8,128)} custom-call(bf16[32,128,128]{2,1,0:T(8,128)(2,1)S(1)} %get-tuple-element.28.m_ref, f32[32,128]{1,0:T(8,128)S(1)} %get-tuple-element.31.mix_ref), custom_call_target="tpu_custom_call" | custom-call | bytes 1589248 | tf_op jit(solution)/shard_map/pallas_call | solution.py:21
  64.9 0.8 %collective-permute-done.12 = f32[32,16]{1,0:T(8,128)S(1)} collective-permute-done((f32[32,16]{1,0:T(8,128)S(1)}, f32[32,16]{1,0:T(8,128)S(1)}, u32[]{:S(2)}, u32[]{:S(2)}) %collective-permute-start.12) | collective-permute-done | bytes 2080 | tf_op jit(solution)/shard_map/ppermute | solution.py:311
  65.7 0.7 %copy.18 = f32[2,1,32,16]{2,3,1,0:T(8,128)} copy(f32[2,1,32,16]{3,2,0,1:T(8,128)S(1)} %maximum_bitcast_fusion) | data formatting | bytes 8192
  (15 shorter events, 0.1 us)
Async XLA Ops:
  0.6 1.2 %copy-start = (bf16[16,256,128]{2,1,0:T(8,128)(2,1)S(1)}, bf16[16,256,128]{2,1,0:T(8,128)(2,1)}, u32[]{:S(2)}) copy-start(bf16[16,256,128]{2,1,0:T(8,128)(2,1)} %x_ref.3) | copy-start | bytes 3145732
  1.9 6.6 %copy-start.3 = (bf16[17]{0:T(256)(128)(2,1)S(1)}, bf16[17]{0:T(256)(128)(2,1)}, u32[]{:S(2)}) copy-start(bf16[17]{0:T(256)(128)(2,1)} %param.7) | copy-start | bytes 106
  1.9 6.7 %copy-start.4 = (bf16[17]{0:T(256)(128)(2,1)S(1)}, bf16[17]{0:T(256)(128)(2,1)}, u32[]{:S(2)}) copy-start(bf16[17]{0:T(256)(128)(2,1)} %param.6) | copy-start | bytes 106
  1.9 11.4 %copy-start.1 = (bf16[16,256,128]{2,1,0:T(8,128)(2,1)S(1)}, bf16[16,256,128]{2,1,0:T(8,128)(2,1)}, u32[]{:S(2)}) copy-start(bf16[16,256,128]{2,1,0:T(8,128)(2,1)} %x_ref.3) | copy-start | bytes 3145732
  1.9 11.4 %copy-start.2 = (bf16[2,1,32,16]{2,3,1,0:T(8,128)(2,1)S(1)}, bf16[2,1,32,16]{2,3,1,0:T(8,128)(2,1)}, u32[]{:S(2)}) copy-start(bf16[2,1,32,16]{2,3,1,0:T(8,128)(2,1)} %param.5) | copy-start | bytes 6148
  2.2 7.6 %collective-permute-start = (bf16[16,8,256]{2,1,0:T(8,128)(2,1)S(1)}, bf16[16,8,256]{2,1,0:T(8,128)(2,1)S(1)}, u32[]{:S(2)}, u32[]{:S(2)}) collective-permute-start(bf16[16,8,256]{2,1,0:T(8,128)(2,1)S(1)} %get-tuple-element.18), channel_id=1, source_target_pairs={{0,8},{8,16},{16,24},{1,9},{9,17},{17,25},{2,10},{10,18},{18,26},{... | collective-permute-start | bytes 196616 | tf_op jit(solution)/shard_map/ppermute | solution.py:256
  7.1 6.2 %collective-permute-start.1 = (bf16[16,8,256]{2,1,0:T(8,128)(2,1)S(1)}, bf16[16,8,256]{2,1,0:T(8,128)(2,1)S(1)}, u32[]{:S(2)}, u32[]{:S(2)}) collective-permute-start(bf16[16,8,256]{2,1,0:T(8,128)(2,1)S(1)} %get-tuple-element.19), channel_id=1, source_target_pairs={{8,0},{16,8},{24,16},{9,1},{17,9},{25,17},{10,2},{18,10},{26,18},{... | collective-permute-start | bytes 196616 | tf_op jit(solution)/shard_map/ppermute | solution.py:257
  17.8 4.7 %collective-permute-start.2 = (bf16[35,16,128]{2,1,0:T(8,128)(2,1)S(1)}, bf16[35,16,128]{2,1,0:T(8,128)(2,1)S(1)}, u32[]{:S(2)}, u32[]{:S(2)}) collective-permute-start(bf16[35,16,128]{2,1,0:T(8,128)(2,1)S(1)} %get-tuple-element.21), channel_id=1, source_target_pairs={{0,1},{1,0},{2,3},{3,2},{4,5},{5,4},{6,7},{7,6},{8,9},{9,8},{10,11... | collective-permute-start | bytes 430088 | tf_op jit(solution)/shard_map/ppermute | solution.py:287
  17.9 12.2 %collective-permute-start.3 = (bf16[35,16,128]{2,1,0:T(8,128)(2,1)S(1)}, bf16[35,16,128]{2,1,0:T(8,128)(2,1)S(1)}, u32[]{:S(2)}, u32[]{:S(2)}) collective-permute-start(bf16[35,16,128]{2,1,0:T(8,128)(2,1)S(1)} %get-tuple-element.22), channel_id=1, source_target_pairs={{0,2},{1,3},{2,0},{3,1},{4,6},{5,7},{6,4},{7,5},{8,10},{9,11},{10,... | collective-permute-start | bytes 430088 | tf_op jit(solution)/shard_map/ppermute | solution.py:287
  19.6 12.7 %collective-permute-start.4 = (bf16[35,16,128]{2,1,0:T(8,128)(2,1)S(1)}, bf16[35,16,128]{2,1,0:T(8,128)(2,1)S(1)}, u32[]{:S(2)}, u32[]{:S(2)}) collective-permute-start(bf16[35,16,128]{2,1,0:T(8,128)(2,1)S(1)} %get-tuple-element.23), channel_id=1, source_target_pairs={{0,3},{1,2},{2,1},{3,0},{4,7},{5,6},{6,5},{7,4},{8,11},{9,10},{10,... | collective-permute-start | bytes 430088 | tf_op jit(solution)/shard_map/ppermute | solution.py:287
  19.9 12.4 %collective-permute-start.5 = (bf16[35,16,128]{2,1,0:T(8,128)(2,1)S(1)}, bf16[35,16,128]{2,1,0:T(8,128)(2,1)S(1)}, u32[]{:S(2)}, u32[]{:S(2)}) collective-permute-start(bf16[35,16,128]{2,1,0:T(8,128)(2,1)S(1)} %get-tuple-element.24), channel_id=1, source_target_pairs={{0,4},{1,5},{2,6},{3,7},{4,0},{5,1},{6,2},{7,3},{8,12},{9,13},{10,... | collective-permute-start | bytes 430088 | tf_op jit(solution)/shard_map/ppermute | solution.py:287
  22.4 19.3 %collective-permute-start.6 = (bf16[35,16,128]{2,1,0:T(8,128)(2,1)S(1)}, bf16[35,16,128]{2,1,0:T(8,128)(2,1)S(1)}, u32[]{:S(2)}, u32[]{:S(2)}) collective-permute-start(bf16[35,16,128]{2,1,0:T(8,128)(2,1)S(1)} %get-tuple-element.25), channel_id=1, source_target_pairs={{0,5},{1,4},{2,7},{3,6},{4,1},{5,0},{6,3},{7,2},{8,13},{9,12},{10,... | collective-permute-start | bytes 430088 | tf_op jit(solution)/shard_map/ppermute | solution.py:287
  22.5 19.3 %collective-permute-start.7 = (bf16[35,16,128]{2,1,0:T(8,128)(2,1)S(1)}, bf16[35,16,128]{2,1,0:T(8,128)(2,1)S(1)}, u32[]{:S(2)}, u32[]{:S(2)}) collective-permute-start(bf16[35,16,128]{2,1,0:T(8,128)(2,1)S(1)} %get-tuple-element.26), channel_id=1, source_target_pairs={{0,6},{1,7},{2,4},{3,5},{4,2},{5,3},{6,0},{7,1},{8,14},{9,15},{10,... | collective-permute-start | bytes 430088 | tf_op jit(solution)/shard_map/ppermute | solution.py:287
  30.1 11.7 %collective-permute-start.8 = (bf16[35,16,128]{2,1,0:T(8,128)(2,1)S(1)}, bf16[35,16,128]{2,1,0:T(8,128)(2,1)S(1)}, u32[]{:S(2)}, u32[]{:S(2)}) collective-permute-start(bf16[35,16,128]{2,1,0:T(8,128)(2,1)S(1)} %get-tuple-element.27), channel_id=1, source_target_pairs={{0,7},{1,6},{2,5},{3,4},{4,3},{5,2},{6,1},{7,0},{8,15},{9,14},{10,... | collective-permute-start | bytes 430088 | tf_op jit(solution)/shard_map/ppermute | solution.py:287
  47.1 9.6 %collective-permute-start.10 = (f32[128,128]{1,0:T(8,128)S(1)}, f32[128,128]{1,0:T(8,128)S(1)}, u32[]{:S(2)}, u32[]{:S(2)}) collective-permute-start(f32[128,128]{1,0:T(8,128)S(1)} %get-tuple-element.30.refs_0_), channel_id=1, source_target_pairs={{0,2},{1,3},{2,0},{3,1},{4,6},{5,7},{6,4},{7,5},{8,10},{9,11},{10,... | collective-permute-start | bytes 196616 | tf_op jit(solution)/shard_map/ppermute | solution.py:304
  54.5 3.9 %collective-permute-start.11 = (f32[128,128]{1,0:T(8,128)S(1)}, f32[128,128]{1,0:T(8,128)S(1)}, u32[]{:S(2)}, u32[]{:S(2)}) collective-permute-start(f32[128,128]{1,0:T(8,128)S(1)} %get-tuple-element.30.refs_0_), channel_id=1, source_target_pairs={{0,3},{1,2},{2,1},{3,0},{4,7},{5,6},{6,5},{7,4},{8,11},{9,10},{10,... | collective-permute-start | bytes 196616 | tf_op jit(solution)/shard_map/ppermute | solution.py:304
  54.5 3.9 %collective-permute-start.9 = (f32[128,128]{1,0:T(8,128)S(1)}, f32[128,128]{1,0:T(8,128)S(1)}, u32[]{:S(2)}, u32[]{:S(2)}) collective-permute-start(f32[128,128]{1,0:T(8,128)S(1)} %get-tuple-element.30.refs_0_), channel_id=1, source_target_pairs={{0,1},{1,0},{2,3},{3,2},{4,5},{5,4},{6,7},{7,6},{8,9},{9,8},{10,11... | collective-permute-start | bytes 196616 | tf_op jit(solution)/shard_map/ppermute | solution.py:304
  60.9 4.8 %collective-permute-start.12 = (f32[32,16]{1,0:T(8,128)S(1)}, f32[32,16]{1,0:T(8,128)S(1)}, u32[]{:S(2)}, u32[]{:S(2)}) collective-permute-start(f32[32,16]{1,0:T(8,128)S(1)} %get-tuple-element.33), channel_id=1, source_target_pairs={{0,4},{1,5},{2,6},{3,7},{4,0},{5,1},{6,2},{7,3},{8,12},{9,13},{10,... | collective-permute-start | bytes 6152 | tf_op jit(solution)/shard_map/ppermute | solution.py:311

commit v2 on v1

v2 whole, which is shorter than its diff:
```python
import functools
import math

import jax
import jax.numpy as jnp
from jax import lax
from jax.experimental import pallas as pl
from jax.experimental.pallas import tpu as pltpu
from jax.sharding import PartitionSpec as P

TY = 2
F32 = jnp.float32
BF16 = jnp.bfloat16


def call(kernel, outs, ins, scratch=(), places=None):
    places = places or [pltpu.VMEM] * len(ins)
    return pl.pallas_call(
        kernel,
        out_shape=outs,
        in_specs=[pl.BlockSpec(memory_space=place) for place in places],
        out_specs=[pl.BlockSpec(memory_space=pltpu.VMEM)] * len(outs),
        scratch_shapes=scratch,
        compiler_params=pltpu.CompilerParams(vmem_limit_bytes=40 * 1024 * 1024),
        cost_estimate=pl.CostEstimate(flops=0, bytes_accessed=0, transcendentals=0),
    )(*ins)


def toeplitz(tap_row, rows, cols, shift, sign=1):
    offsets = sign * (
        lax.broadcasted_iota(jnp.int32, (rows, cols), 1)
        - lax.broadcasted_iota(jnp.int32, (rows, cols), 0)
    )
    offsets = offsets + shift
    total = jnp.zeros((rows, cols), F32)
    for t in range(tap_row.shape[1]):
        total = jnp.where(offsets == t, tap_row[:, t : t + 1], total)
    return total


def contract(left, right, left_dim, right_dim):
    return lax.dot_general(
        left, right, (((left_dim,), (right_dim,)), ((), ())), preferred_element_type=F32
    )


def split(value):
    high = value.astype(BF16)
    return high, (value - high.astype(F32)).astype(BF16)


def turned(value, shift):
    return pltpu.roll(value, shift % value.shape[1], 1)


def early_kernel(axis, count, share, x_hbm, taps_ref, *rest):
    head_ref, tail_ref, x_ref, rows_scr, anchor_scr, sem = rest
    frames, rows, cols = x_hbm.shape
    span, part = x_ref.shape[1], 2 * share
    radius = (taps_ref.shape[1] - 1) // 2
    me = lax.axis_index(axis)
    chip = (me // 2) ^ (count // 4)
    first = jnp.clip(chip * part - (span - part) // 2, 0, rows - span)
    first = pl.multiple_of(first, 16)
    inner = pl.multiple_of(chip * part - first, 16)
    copy = pltpu.make_async_copy(x_hbm.at[:, pl.ds(first, span), :], x_ref, sem)
    copy.start()
    taps = taps_ref[...].astype(F32)
    bx = toeplitz(taps, cols, cols, radius, -1).astype(BF16)
    dy = toeplitz(taps, part, span, radius - inner).astype(BF16)
    copy.wait()

    total = jnp.zeros((span, cols), F32)
    for f in range(frames):
        total = total + x_ref[f].astype(F32)
    anchor = (total * (1.0 / frames)).astype(BF16)
    anchor32 = anchor.astype(F32)
    high, low = split(contract(anchor, bx, 1, 0))
    both = contract(dy, jnp.concatenate([high, low], axis=1), 1, 0)
    rows_scr[0:span, :] = anchor32
    centre = rows_scr[pl.ds(inner, part), :]
    anchor_s = centre - both[:, :cols] - both[:, cols:]
    anchor_out = anchor_s.astype(BF16)
    anchor_scr[...] = anchor_out
    left_over = anchor_s - anchor_out.astype(F32)
    for p in range(frames // 2):
        smooths, blocks = [], []
        for f in (2 * p, 2 * p + 1):
            block = (x_ref[f].astype(F32) - anchor32).astype(BF16)
            smooths.append(contract(block, bx, 1, 0).astype(BF16))
            own = x_ref[f, pl.ds(inner, part), :].astype(F32) - centre
            blocks.append(own.astype(BF16).astype(F32))
        both = contract(dy, jnp.concatenate(smooths, axis=1), 1, 0)
        for i, f in enumerate((2 * p, 2 * p + 1)):
            value = blocks[i] - both[:, i * cols : (i + 1) * cols] + left_over
            rows_scr[pl.ds(f, part, stride=frames), :] = value
    lead = head_ref.shape[0] // 2
    rest = share - lead
    for h in range(2):
        index = (me ^ h) % 2
        put_rows(head_ref, h * lead, index * share, lead, rows_scr)
        at = h * (rest + share // frames)
        put_rows(tail_ref, at, index * share + lead, rest, rows_scr)
        put_anchor(tail_ref, at + rest, index * share, share, anchor_scr)


def put_rows(out_ref, at, first, size, rows_scr):
    _, frames, cols = out_ref.shape
    start = pl.multiple_of(first * frames, frames)
    block = rows_scr[pl.ds(start, size * frames), :].astype(BF16)
    out_ref[at : at + size] = block.reshape(size, frames, cols)


def put_anchor(out_ref, at, first, share, anchor_scr):
    _, frames, cols = out_ref.shape
    size = share // frames
    block = anchor_scr[pl.ds(pl.multiple_of(first, share), share), :].astype(BF16)
    out_ref[at : at + size] = block.reshape(size, frames, cols)


def put_edges(out_ref, at, index, rows_scr, anchor_scr, share, frames, width):
    cols = out_ref.shape[2]
    packed = cols // (2 * width)
    groups = share // packed
    lane = lax.broadcasted_iota(jnp.int32, (frames, cols), 1) // (2 * width)
    start = pl.multiple_of(index * (share * frames), share * frames)
    for group in range(groups):
        tile = jnp.zeros((frames, cols), F32)
        for q in range(packed):
            begin = pl.multiple_of(start + (group * packed + q) * frames, frames)
            value = rows_scr[pl.ds(begin, frames), :]
            tile = jnp.where(lane == q, turned(value, width + 2 * width * q), tile)
        out_ref[at + group] = tile.astype(BF16)
    first = pl.multiple_of(index * share, share)
    tile = jnp.zeros((frames, cols), F32)
    for q in range(packed):
        value = jnp.concatenate(
            [
                anchor_scr[pl.ds(first + q, groups, stride=packed), :],
                jnp.zeros((frames - groups, cols), F32),
            ],
            axis=0,
        )
        tile = jnp.where(lane == q, turned(value, width + 2 * width * q), tile)
    out_ref[at + groups] = tile.astype(BF16)


def edges_kernel(x_ref, after_ref, low_ref, high_ref):
    frames, _, cols = x_ref.shape
    width = low_ref.shape[1]
    row = lax.broadcasted_iota(jnp.int32, (2 * width, cols), 0)
    col = lax.broadcasted_iota(jnp.int32, (2 * width, cols), 1)
    wanted = jnp.where(row < width, row, row + cols - 2 * width)
    pick = jnp.where(col == wanted, 1.0, 0.0).astype(BF16)
    for f in range(frames):
        both = contract(pick, x_ref[f], 1, 1).astype(BF16)
        low_ref[f] = both[:width]
        high_ref[f] = both[width:]


def bands_kernel(space_ref, time_ref, bx_ref, bh_ref, dy_ref, lhs_ref):
    rows, cols = dy_ref.shape[0], bx_ref.shape[0]
    space, time = space_ref[...].astype(F32), time_ref[...].astype(F32)
    radius = (space.shape[1] - 1) // 2
    bx_ref[...] = toeplitz(space, cols, cols, radius, -1).astype(BF16)
    bh_ref[0:radius] = toeplitz(space, radius, cols, 0, -1).astype(BF16)
    bh_ref[radius:] = toeplitz(space, radius, cols, radius + cols, -1).astype(BF16)
    dy_ref[...] = toeplitz(space, rows, rows, radius).astype(BF16)
    all_frames = lhs_ref.shape[0]
    count = (lhs_ref.shape[1] - all_frames) // 2
    frames = all_frames // count
    band = toeplitz(time, all_frames, all_frames, radius)
    ids = lax.broadcasted_iota(jnp.int32, (all_frames, count), 0) // frames
    lane = lax.broadcasted_iota(jnp.int32, (all_frames, count), 1)
    sums = jnp.where(ids == lane, 1.0, 0.0)
    for j in range(count):
        piece = jnp.sum(band[:, j * frames : (j + 1) * frames], axis=1, keepdims=True)
        sums = jnp.where(lane == j, sums - piece, sums)
    high, low = split(sums)
    lhs_ref[:, 0:all_frames] = (-band).astype(BF16)
    lhs_ref[:, all_frames:] = jnp.concatenate([high.astype(F32), low.astype(F32)], 1).astype(BF16)


def spatial_kernel(axis, early, x_ref, hl_ref, hr_ref, bx_ref, bh_ref, dy_ref, om_ref, *rest):
    outs, rows_scr, anchor_scr = rest[:-2], rest[-2], rest[-1]
    frames, rows, cols = x_ref.shape
    count = 2 * (len(outs) - 1)
    share = rows // count
    ranks = om_ref.shape[2]
    width = hl_ref.shape[1]
    me = lax.axis_index(axis)
    bx, bh, dy = bx_ref[...], bh_ref[...], dy_ref[...]

    def halo(f):
        return jnp.concatenate([hl_ref[f].astype(F32), hr_ref[f].astype(F32)], axis=0)

    total = jnp.zeros((rows, cols), F32)
    halo_total = jnp.zeros((bh.shape[0], rows), F32)
    for f in range(frames):
        total = total + x_ref[f].astype(F32)
        halo_total = halo_total + halo(f)
    anchor = (total * (1.0 / frames)).astype(BF16)
    halo_anchor = (halo_total * (1.0 / frames)).astype(BF16)

    def across(block, edge):
        return contract(block, bx, 1, 0) + contract(edge, bh, 0, 0)

    high, low = split(across(anchor, halo_anchor))
    both = contract(dy, jnp.concatenate([high, low], axis=1), 1, 0)
    anchor_s = anchor.astype(F32) - both[:, :cols] - both[:, cols:]
    anchor_out = anchor_s.astype(BF16).astype(F32)
    anchor_scr[...] = anchor_out
    left_over = anchor_s - anchor_out
    anchor32 = anchor.astype(F32)
    halo32 = halo_anchor.astype(F32)

    for p in range(frames // 2):
        blocks, smooths = [], []
        for f in (2 * p, 2 * p + 1):
            block = (x_ref[f].astype(F32) - anchor32).astype(BF16)
            edge = (halo(f) - halo32).astype(BF16)
            blocks.append(block)
            smooths.append(across(block, edge).astype(BF16))
        both = contract(dy, jnp.concatenate(smooths, axis=1), 1, 0)
        for i, f in enumerate((2 * p, 2 * p + 1)):
            value = blocks[i].astype(F32) - both[:, i * cols : (i + 1) * cols] + left_over
            rows_scr[pl.ds(f, rows, stride=frames), :] = value

    args = (rows_scr, anchor_scr, share, frames)
    half = share + share // frames
    edge_half = share // (cols // (2 * width)) + 1
    for out, z, blocks in [(outs[0], 0, (0,)), (outs[1], 0, (1,))] + [
        (outs[1 + z // 2], z, (0, 1)) for z in range(2, count, 2)
    ]:
        for i, h in enumerate(blocks):
            dest = me ^ (z + h)
            if z == early:
                put_edges(out, i * edge_half, dest, *args, width)
            else:
                put_rows(out, i * half, dest * share, share, rows_scr)
                put_anchor(out, i * half + share, dest * share, share, anchor_scr)
        last = out.shape[0] - 1
        out[last, :, 0:ranks] = om_ref[(me ^ z) // (count // TY)]
        out[last, :, ranks:] = jnp.zeros((frames, cols - ranks), BF16)


def temporal_kernel(axis, width, early, count, *refs):
    own, pair = refs[:2]
    came, handed = refs[2 : 1 + count // 2], refs[1 + count // 2 : count]
    heads, tails = refs[count : count + 2], refs[count + 2 : count + 4]
    lhs_ref, m_ref, gram_ref, om_ref, data_scr, anchor_scr = refs[count + 4 :]
    share, _, frames, cols = data_scr.shape
    all_frames = count * frames
    me = lax.axis_index(axis)
    packed = cols // (2 * width)
    groups = share // packed
    half = share + share // frames
    lanes = lax.broadcasted_iota(jnp.int32, (frames, cols), 1)
    at_edge = (lanes < width) | (lanes >= cols - width)

    def take_block(ref, at, src):
        data_scr[:, src] = ref[at : at + share]
        anchor = ref[at + share : at + half].reshape(share, cols)
        anchor_scr[pl.ds(src, share, stride=count), :] = anchor.astype(F32)

    def take_edges(head, tail, h, ref, edge_at, src):
        lead = head.shape[0] // 2
        at = h * (half - lead) + share - lead
        anchor = tail[at : at + share // frames].reshape(share, cols).astype(F32)
        anchor_scr[pl.ds(src, share, stride=count), :] = anchor
        last = ref[edge_at + groups].astype(F32)
        for q in range(packed):
            edge = turned(last, -(width + 2 * width * q))[:groups]
            where = pl.ds(src + q * count, groups, stride=count * packed)
            old = anchor_scr[where, :]
            anchor_scr[where, :] = jnp.where(at_edge[:groups], edge, old)
        for group in range(groups):
            tile = ref[edge_at + group].astype(F32)
            for q in range(packed):
                r = group * packed + q
                edge = turned(tile, -(width + 2 * width * q))
                main = head[h * lead + r] if r < lead else tail[h * (half - lead) + r - lead]
                value = jnp.where(at_edge, edge, main.astype(F32))
                data_scr[r, src] = value.astype(BF16)

    for k in range(count):
        src = me ^ k
        z, h = k // 2 * 2, k % 2
        ref = (own, pair)[h] if z == 0 else (came, handed)[h][z // 2 - 1]
        om_ref[src] = ref[ref.shape[0] - 1]
        if z == early:
            take_edges(heads[h], tails[h], h, ref, h * (groups + 1), src)
        else:
            take_block(ref, 0 if z == 0 else h * half, src)
    lhs = lhs_ref[...]
    gram = jnp.zeros((all_frames, all_frames), F32)
    for p in range(share // 2):
        blocks, feeds = [], []
        for r in (2 * p, 2 * p + 1):
            block = data_scr[r].reshape(all_frames, cols)
            anchor = anchor_scr[r * count : (r + 1) * count, :]
            blocks.append(block)
            feeds.append(
                jnp.concatenate([block, jnp.concatenate([anchor, anchor], 0).astype(BF16)], axis=0)
            )
        low = contract(lhs, jnp.concatenate(feeds, axis=1), 1, 0)
        value = (jnp.concatenate(blocks, axis=1).astype(F32) + low).astype(BF16)
        m_ref[2 * p] = value[:, :cols]
        m_ref[2 * p + 1] = value[:, cols:]
        gram = gram + contract(value, value, 1, 1)
    gram_ref[...] = gram


def exact(left, right, left_dim, right_dim):
    return lax.dot_general(
        left,
        right,
        (((left_dim,), (right_dim,)), ((), ())),
        precision=lax.Precision.HIGHEST,
        preferred_element_type=F32,
    )


def whiten(gram, *others):
    size = gram.shape[0]
    ids = lax.broadcasted_iota(jnp.int32, (size, 128), 0)
    work = [jnp.concatenate([gram, jnp.zeros((size, 128 - size), F32)], axis=1), *others]
    scale = jnp.zeros((size, 128), F32)
    panel = 8
    for start in range(0, size, panel):
        cols = [
            jnp.broadcast_to(work[0][:, j : j + 1], (size, 128)) for j in range(start, start + panel)
        ]
        for j in range(start, start + panel):
            inverse = 1.0 / cols[j - start][j : j + 1]
            factor = jnp.where(ids > j, cols[j - start] * inverse, 0.0)
            scale = jnp.where(ids == j, inverse, scale)
            for m in range(j - start + 1, panel):
                cols[m] = cols[m] - factor * cols[m][j : j + 1]
            for i in range(len(work)):
                value = work[i]
                width = value.shape[1]
                parts = [
                    value[:, c : c + 128] - factor * value[j : j + 1, c : c + 128]
                    for c in range(0, width, 128)
                ]
                work[i] = parts[0] if len(parts) == 1 else jnp.concatenate(parts, axis=1)
    scale = jnp.sqrt(scale)
    results = []
    for value in work[1:]:
        parts = [value[:, c : c + 128] * scale for c in range(0, value.shape[1], 128)]
        results.append(parts[0] if len(parts) == 1 else jnp.concatenate(parts, axis=1))
    return results


def factor_kernel(axis, count, ranks, pixels, om_ref, *refs):
    grams, (mix_ref, own_ref, send_ref) = refs[:-3], refs[-3:]
    frames = own_ref.shape[0]
    all_frames = grams[0].shape[0]
    me = lax.axis_index(axis)
    gram = grams[0][...]
    for other in grams[1:]:
        gram = gram + other[...]
    omega = om_ref[...].reshape(all_frames, om_ref.shape[2]).astype(F32).T[:ranks]
    sketch = exact(omega, gram, 1, 0)
    (load,) = whiten(exact(sketch, omega, 1, 1), sketch)
    back = exact(load, gram, 1, 0)
    mix, coef = whiten(exact(back, load, 1, 1), load, back)
    mix_ref[...] = mix * math.sqrt(pixels)
    ids = lax.broadcasted_iota(jnp.int32, (frames, all_frames), 0)
    lane = lax.broadcasted_iota(jnp.int32, (frames, all_frames), 1)
    for ref, who in ((own_ref, me), (send_ref, me ^ (count // TY))):
        pick = jnp.where(lane == ids + who * frames, 1.0, 0.0)
        ref[...] = exact(pick, coef, 1, 1)


def basis_kernel(m_ref, mix_ref, out_ref):
    share, _, cols = m_ref.shape
    ranks = mix_ref.shape[0]
    high, low = split(mix_ref[...])
    lhs = jnp.concatenate([high, low], axis=0)
    for p in range(share // 2):
        data = jnp.concatenate([m_ref[2 * p], m_ref[2 * p + 1]], axis=1)
        both = contract(lhs, data, 1, 0)
        value = both[:ranks] + both[ranks:]
        for i in range(2):
            out_ref[pl.ds(2 * p + i, ranks, stride=share), :] = value[:, i * cols : (i + 1) * cols]


def local(movie, omega, time_taps, space_taps):
    frames, rows, cols = movie.shape
    radius = (space_taps.shape[0] - 1) // 2
    count = lax.axis_size("tm")
    tiles = lax.axis_size("tile")
    ranks = omega.shape[2]
    share = rows // count
    all_frames = frames * count
    group = count // TY
    pixels = (rows // TY) * cols
    early = count // 2
    packed = cols // (2 * radius)
    half = share + share // frames

    def shape(dims, dtype):
        return jax.ShapeDtypeStruct(dims, dtype)

    def swap(value, k):
        return lax.ppermute(value, "tm", [(i, i ^ k) for i in range(count)])

    space_row, time_row = space_taps[None], time_taps[None]
    part = 2 * share
    span = part + 32
    lead = 3 * share // 8
    head, tail = call(
        functools.partial(early_kernel, "tm", count, share),
        [shape((2 * size, frames, cols), BF16) for size in (lead, half - lead)],
        [movie, space_row],
        [
            pltpu.VMEM((frames, span, cols), BF16),
            pltpu.VMEM((part * frames, cols), F32),
            pltpu.VMEM((part, cols), BF16),
            pltpu.SemaphoreType.DMA,
        ],
        [pl.ANY, pltpu.VMEM],
    )
    head_came, tail_came = swap(head, early), swap(tail, early)
    low, high = call(
        edges_kernel,
        [shape((frames, radius, rows), BF16)] * 2,
        [movie, head],
        (),
        [pltpu.VMEM, pl.ANY],
    )
    right = [(i, i + 1) for i in range(tiles - 1)]
    left = [(j, i) for i, j in right]
    halo_left = lax.ppermute(high, "tile", right)
    halo_right = lax.ppermute(low, "tile", left)
    bx, bh, dy, lhs = call(
        bands_kernel,
        [
            shape((cols, cols), BF16),
            shape((2 * radius, cols), BF16),
            shape((rows, rows), BF16),
            shape((all_frames, all_frames + 2 * count), BF16),
        ],
        [space_row, time_row],
    )
    om = jnp.transpose(omega[:, 0], (0, 2, 1))
    slots = [half + 1, half + 1] + [
        2 * (share // packed + 1) + 1 if z == early else 2 * half + 1 for z in range(2, count, 2)
    ]
    own, pair, *parts = call(
        functools.partial(spatial_kernel, "tm", early),
        [shape((n, frames, cols), BF16) for n in slots],
        [movie, halo_left, halo_right, bx, bh, dy, om],
        [pltpu.VMEM((rows * frames, cols), F32), pltpu.VMEM((rows, cols), F32)],
    )
    came = {}

    def send(z, *after):
        value = lax.optimization_barrier((parts[z // 2 - 1], *after))[0]
        came[z] = swap(value, z)

    for z in range(early + 2, count, 2):
        send(z, head_came)
    send(early)
    for z in range(2, early, 2):
        send(z, tail_came, came[early])
    pair = swap(lax.optimization_barrier((pair, came[early]))[0], 1)
    came = [came[z] for z in range(2, count, 2)]
    handed = [swap(value, 1) for value in came]
    mains = [head_came, swap(head_came, 1), tail_came, swap(tail_came, 1)]
    matrix, gram, om_all = call(
        functools.partial(temporal_kernel, "tm", radius, early, count),
        [
            shape((share, all_frames, cols), BF16),
            shape((all_frames, all_frames), F32),
            shape((count, frames, cols), BF16),
        ],
        [own, pair, *came, *handed, *mains, lhs],
        [
            pltpu.VMEM((share, count, frames, cols), BF16),
            pltpu.VMEM((share * count, cols), F32),
        ],
    )
    grams = [gram] + [swap(gram, k) for k in range(1, group)]
    mix, coef_own, coef_send = call(
        functools.partial(factor_kernel, "tm", count, ranks, pixels),
        [shape((ranks, all_frames), F32), *([shape((frames, ranks), F32)] * 2)],
        [om_all, *grams],
    )
    coef_other = swap(coef_send, group)
    (basis,) = call(basis_kernel, [shape((ranks * share, cols), F32)], [matrix, mix])
    tile_row = lax.axis_index("tm") // group
    first = jnp.where(tile_row == 0, coef_own, coef_other)
    second = jnp.where(tile_row == 0, coef_other, coef_own)
    coefficients = jnp.transpose(jnp.stack([first, second]), (0, 2, 1))[:, None]
    return basis.reshape(ranks, share, cols), coefficients


def solution(mesh):
    in_specs = (P("tm", None, "tile"), P(None, "tile", None, "tm"), P(), P())
    out_specs = (P(None, "tm", "tile"), P(None, "tile", None, "tm"))
    return jax.shard_map(local, mesh=mesh, in_specs=in_specs, out_specs=out_specs, check_vma=False)
```

time: 66.6 us -> 56.6 us (0.85)
  starting transfers between devices: 24.7 us -> 17.6 us
  Pallas kernels: 14 us -> 11.3 us
  waiting for transfers between devices: 23.6 us -> 24.3 us
    ppermute x11 -> x15, starting transfers between devices: 18.5 us -> 12.8 us  [swap(): return lax.ppermute(value, 'tm', [(i, i ^ k) for i in range(count)])]
    pallas_call x5 -> x7, Pallas kernels: 14 us -> 11.3 us  [call(): pl.pallas_call(kernel, out_shape=outs, in_specs=[pl.BlockSpec(memory_spac...]
    ppermute x1, starting transfers between devices: 4.86 us -> 3.54 us  [local(): halo_left = lax.ppermute(high, 'tile', right)]
    ppermute x11 -> x15, waiting for transfers between devices: 20.1 us -> 21 us  [swap(): return lax.ppermute(value, 'tm', [(i, i ^ k) for i in range(count)])]
    reduce_sum x4 -> x0, other arithmetic: 0.86 us -> none  [the longest x3 0.85 us: toeplitz(): return jnp.sum(hits * taps.astype(F32), axis=2)]
    unnamed x11 -> x10, local copies, waits for them, and re-layouts: 1.91 us -> 1.88 us
  transfers between devices with their start and end apart: 13 -> 17, of which waited for: 7 -> 9; matrix products, arithmetic and copies ran while one was open for 2% -> 0% of each run, Pallas kernels for 2% -> 10%
where the time goes in v2:
time: 56.6 us; the launch traced here: 56.4 us
  waiting for transfers between devices  24.3 us (43%)
  starting transfers between devices  17.6 us (31%)
  Pallas kernels  11.3 us (20%)
  local copies, waits for them, and re-layouts  1.88 us (3%)
  between operations  0.72 us (1%)
  other arithmetic  0.62 us (1%)
    ppermute x15, waiting for transfers between devices, swap(): return lax.ppermute(value, 'tm', [(i, i ^ k) for i in range(count)])  21 us
    ppermute x15, starting transfers between devices, swap(): return lax.ppermute(value, 'tm', [(i, i ^ k) for i in range(count)])  12.8 us
    pallas_call x7, Pallas kernels, call(): pl.pallas_call(kernel, out_shape=outs, in_specs=[pl.BlockSpec(memory_spac...  11.3 us
    ppermute x1, starting transfers between devices, local(): halo_left = lax.ppermute(high, 'tile', right)  3.54 us
    ppermute x1, waiting for transfers between devices, local(): halo_right = lax.ppermute(low, 'tile', left)  3.25 us
    unnamed x10, local copies, waits for them, and re-layouts  1.88 us
    ppermute x1, starting transfers between devices, local(): halo_right = lax.ppermute(low, 'tile', left)  1.29 us
  transfers between devices with their start and end apart: 17, of which 9 were waited for; matrix products, arithmetic and copies ran while one was open for 0% of the time, Pallas kernels for 10%

profile of v2, /device:TPU:0, one launch (start us, length us, event | category | flops | bytes accessed | tf_op | source)
XLA Modules:
  0.0 56.4 jit_solution(7384893146884692375)
XLA Ops:
  0.6 0.0 copy-start.3
  0.6 0.6 %copy-done.3 = bf16[17]{0:T(256)(128)(2,1)S(1)} copy-done((bf16[17]{0:T(256)(128)(2,1)S(1)}, bf16[17]{0:T(256)(128)(2,1)}, u32[]{:S(2)}) %copy-start.3) | copy-done | bytes 58
  1.3 0.0 copy-start
  1.3 1.2 %copy-done = bf16[16,256,128]{2,1,0:T(8,128)(2,1)S(1)} copy-done((bf16[16,256,128]{2,1,0:T(8,128)(2,1)S(1)}, bf16[16,256,128]{2,1,0:T(8,128)(2,1)}, u32[]{:S(2)}) %copy-start) | copy-done | bytes 1048600
  2.5 0.0 copy-start.1
  2.5 1.8 %shard_map.59 = (bf16[24,16,128]{2,1,0:T(8,128)(2,1)S(1)}, bf16[44,16,128]{2,1,0:T(8,128)(2,1)S(1)}) custom-call(bf16[16,256,128]{2,1,0:T(8,128)(2,1)S(1)} %copy-done, bf16[1,17]{1,0:T(2,128)(2,1)S(1)} %bitcast.17), custom_call_target="tpu_custom_call" | custom-call | tf_op jit(solution)/shard_map/pallas_call | solution.py:18
  4.4 4.1 %collective-permute-start.4 = (bf16[44,16,128]{2,1,0:T(8,128)(2,1)S(1)}, bf16[44,16,128]{2,1,0:T(8,128)(2,1)S(1)}, u32[]{:S(2)}, u32[]{:S(2)}) collective-permute-start(bf16[44,16,128]{2,1,0:T(8,128)(2,1)S(1)} %get-tuple-element.35), channel_id=1, source_target_pairs={{0,4},{1,5},{2,6},{3,7},{4,0},{5,1},{6,2},{7,3},{8,12},{9,13},{10,... | collective-permute-start | bytes 540680 | tf_op jit(solution)/shard_map/ppermute | solution.py:408
  8.5 0.0 copy-start.4
  8.5 0.4 shard_map.60
  8.8 0.0 copy-start.2
  8.8 3.5 %collective-permute-start = (bf16[16,8,256]{2,1,0:T(8,128)(2,1)S(1)}, bf16[16,8,256]{2,1,0:T(8,128)(2,1)S(1)}, u32[]{:S(2)}, u32[]{:S(2)}) collective-permute-start(bf16[16,8,256]{2,1,0:T(8,128)(2,1)S(1)} %get-tuple-element.25), channel_id=1, source_target_pairs={{0,8},{8,16},{16,24},{1,9},{9,17},{17,25},{2,10},{10,18},{18,26},{... | collective-permute-start | bytes 196616 | tf_op jit(solution)/shard_map/ppermute | solution.py:436
  12.4 1.3 %collective-permute-start.1 = (bf16[16,8,256]{2,1,0:T(8,128)(2,1)S(1)}, bf16[16,8,256]{2,1,0:T(8,128)(2,1)S(1)}, u32[]{:S(2)}, u32[]{:S(2)}) collective-permute-start(bf16[16,8,256]{2,1,0:T(8,128)(2,1)S(1)} %get-tuple-element.26), channel_id=1, source_target_pairs={{8,0},{16,8},{24,16},{9,1},{17,9},{25,17},{10,2},{18,10},{26,18},{... | collective-permute-start | bytes 196616 | tf_op jit(solution)/shard_map/ppermute | solution.py:437
  13.7 0.4 collective-permute-start.6
  14.1 0.0 copy-done.4
  14.1 1.2 %shard_map.61 = (bf16[128,128]{1,0:T(8,128)(2,1)S(1)}, bf16[16,128]{1,0:T(8,128)(2,1)S(1)}, bf16[256,256]{1,0:T(8,128)(2,1)S(1)}, bf16[128,144]{1,0:T(8,128)(2,1)S(1)}) custom-call(bf16[1,17]{1,0:T(2,128)(2,1)S(1)} %bitcast.18, bf16[1,17]{1,0:T(2,128)(2,1)S(1)} %bitcast.19), custom_call_target="tpu_custom_call" | custom-call | tf_op jit(solution)/shard_map/pallas_call | solution.py:18
  15.3 0.0 collective-permute-done.hl_ref
  15.3 3.2 %collective-permute-done.1.hr_ref = bf16[16,8,256]{2,1,0:T(8,128)(2,1)S(1)} collective-permute-done((bf16[16,8,256]{2,1,0:T(8,128)(2,1)S(1)}, bf16[16,8,256]{2,1,0:T(8,128)(2,1)S(1)}, u32[]{:S(2)}, u32[]{:S(2)}) %collective-permute-start.1) | collective-permute-done | bytes 65568 | tf_op jit(solution)/shard_map/ppermute | solution.py:437
  18.5 0.0 copy-done.1
  18.5 0.0 copy-done.2
  18.5 2.9 %shard_map.62 = (bf16[35,16,128]{2,1,0:T(8,128)(2,1)S(1)}, bf16[35,16,128]{2,1,0:T(8,128)(2,1)S(1)}, bf16[69,16,128]{2,1,0:T(8,128)(2,1)S(1)}, bf16[11,16,128]{2,1,0:T(8,128)(2,1)S(1)}, bf16[69,16,128]{2,1,0:T(8,128)(2,1)S(1)}) custom-call(bf16[16,256,128]{2,1,0:T(8,128)(2,1)S(1)} %copy-done.1, bf16[16,8,256]{2,1,0:T(8,128)(2,1)S(1)} %collective-permute-done.hl_ref, ...), custom_call_target="tpu_custom_call" | custom-call | tf_op jit(solution)/shard_map/pallas_call | solution.py:18
  21.4 0.4 collective-permute-start.2
  21.8 0.0 collective-permute-done.6.refs_8_
  21.8 3.6 %collective-permute-start.7 = (bf16[69,16,128]{2,1,0:T(8,128)(2,1)S(1)}, bf16[69,16,128]{2,1,0:T(8,128)(2,1)S(1)}, u32[]{:S(2)}, u32[]{:S(2)}) collective-permute-start(bf16[69,16,128]{2,1,0:T(8,128)(2,1)S(1)} %get-tuple-element.38), channel_id=1, source_target_pairs={{0,6},{1,7},{2,4},{3,5},{4,2},{5,3},{6,0},{7,1},{8,14},{9,15},{10,... | collective-permute-start | bytes 847880 | tf_op jit(solution)/shard_map/ppermute | solution.py:408
  25.4 6.8 %collective-permute-done.2.refs_3_ = bf16[11,16,128]{2,1,0:T(8,128)(2,1)S(1)} collective-permute-done((bf16[11,16,128]{2,1,0:T(8,128)(2,1)S(1)}, bf16[11,16,128]{2,1,0:T(8,128)(2,1)S(1)}, u32[]{:S(2)}, u32[]{:S(2)}) %collective-permute-start.2) | collective-permute-done | bytes 45088 | tf_op jit(solution)/shard_map/ppermute | solution.py:408
  32.2 0.0 collective-permute-done.4.refs_10_
  32.2 0.0 collective-permute-start.5
  32.2 1.8 %collective-permute-done.7.refs_4_ = bf16[69,16,128]{2,1,0:T(8,128)(2,1)S(1)} collective-permute-done((bf16[69,16,128]{2,1,0:T(8,128)(2,1)S(1)}, bf16[69,16,128]{2,1,0:T(8,128)(2,1)S(1)}, u32[]{:S(2)}, u32[]{:S(2)}) %collective-permute-start.7) | collective-permute-done | bytes 282656 | tf_op jit(solution)/shard_map/ppermute | solution.py:408
  34.1 0.0 collective-permute-start.10
  34.1 4.8 %collective-permute-done.5.refs_2_ = bf16[69,16,128]{2,1,0:T(8,128)(2,1)S(1)} collective-permute-done((bf16[69,16,128]{2,1,0:T(8,128)(2,1)S(1)}, bf16[69,16,128]{2,1,0:T(8,128)(2,1)S(1)}, u32[]{:S(2)}, u32[]{:S(2)}) %collective-permute-start.5) | collective-permute-done | bytes 282656 | tf_op jit(solution)/shard_map/ppermute | solution.py:408
  38.8 0.0 collective-permute-start.8
  38.8 0.5 collective-permute-start.12
  39.3 0.0 collective-permute-start.9
  39.4 0.5 collective-permute-start.3
  39.9 0.9 %collective-permute-done.9.refs_6_ = bf16[11,16,128]{2,1,0:T(8,128)(2,1)S(1)} collective-permute-done((bf16[11,16,128]{2,1,0:T(8,128)(2,1)S(1)}, bf16[11,16,128]{2,1,0:T(8,128)(2,1)S(1)}, u32[]{:S(2)}, u32[]{:S(2)}) %collective-permute-start.9) | collective-permute-done | bytes 45088 | tf_op jit(solution)/shard_map/ppermute | solution.py:408
  40.7 0.1 collective-permute-start.11
  40.9 1.2 %collective-permute-done.11.refs_9_ = bf16[24,16,128]{2,1,0:T(8,128)(2,1)S(1)} collective-permute-done((bf16[24,16,128]{2,1,0:T(8,128)(2,1)S(1)}, bf16[24,16,128]{2,1,0:T(8,128)(2,1)S(1)}, u32[]{:S(2)}, u32[]{:S(2)}) %collective-permute-start.11) | collective-permute-done | bytes 98336 | tf_op jit(solution)/shard_map/ppermute | solution.py:408
  42.0 0.0 collective-permute-done.3.refs_1_
  42.0 0.0 collective-permute-done.12.refs_11_
  42.0 0.0 collective-permute-done.10.refs_7_
  42.0 0.0 collective-permute-done.8.refs_5_
  42.1 1.2 %shard_map.63 = (bf16[32,128,128]{2,1,0:T(8,128)(2,1)S(1)}, f32[128,128]{1,0:T(8,128)S(1)}, bf16[8,16,128]{2,1,0:T(8,128)(2,1)S(1)}) custom-call(bf16[35,16,128]{2,1,0:T(8,128)(2,1)S(1)} %get-tuple-element.30.refs_0_, bf16[35,16,128]{2,1,0:T(8,128)(2,1)S(1)} %collective-permute-done.3.refs_1_, bf16[69,16,128]{2,1,0:T(8,128)(2,1)S(1)} %collective-permute-done.5.refs_2_, ...), custom_call_target="tpu_custom_call" | custom-call | tf_op jit(solution)/shard_map/pallas_call | solution.py:18
  43.3 0.2 collective-permute-start.13
  43.5 0.6 %collective-permute-start.14 = (f32[128,128]{1,0:T(8,128)S(1)}, f32[128,128]{1,0:T(8,128)S(1)}, u32[]{:S(2)}, u32[]{:S(2)}) collective-permute-start(f32[128,128]{1,0:T(8,128)S(1)} %get-tuple-element.42.refs_0_), channel_id=1, source_target_pairs={{0,2},{1,3},{2,0},{3,1},{4,6},{5,7},{6,4},{7,5},{8,10},{9,11},{10,... | collective-permute-start | bytes 196616 | tf_op jit(solution)/shard_map/ppermute | solution.py:408
  44.1 1.1 %collective-permute-start.15 = (f32[128,128]{1,0:T(8,128)S(1)}, f32[128,128]{1,0:T(8,128)S(1)}, u32[]{:S(2)}, u32[]{:S(2)}) collective-permute-start(f32[128,128]{1,0:T(8,128)S(1)} %get-tuple-element.42.refs_0_), channel_id=1, source_target_pairs={{0,3},{1,2},{2,1},{3,0},{4,7},{5,6},{6,5},{7,4},{8,11},{9,10},{10,... | collective-permute-start | bytes 196616 | tf_op jit(solution)/shard_map/ppermute | solution.py:408
  45.2 0.0 collective-permute-done.13.refs_1_
  45.2 3.2 %collective-permute-done.14.refs_2_ = f32[128,128]{1,0:T(8,128)S(1)} collective-permute-done((f32[128,128]{1,0:T(8,128)S(1)}, f32[128,128]{1,0:T(8,128)S(1)}, u32[]{:S(2)}, u32[]{:S(2)}) %collective-permute-start.14) | collective-permute-done | bytes 65568 | tf_op jit(solution)/shard_map/ppermute | solution.py:408
  48.4 0.3 collective-permute-done.15.refs_3_
  48.7 2.5 %shard_map.64 = (f32[32,128]{1,0:T(8,128)S(1)}, f32[16,32]{1,0:T(8,128)S(1)}, f32[16,32]{1,0:T(8,128)S(1)}) custom-call(bf16[8,16,128]{2,1,0:T(8,128)(2,1)S(1)} %get-tuple-element.41.om_ref, f32[128,128]{1,0:T(8,128)S(1)} %get-tuple-element.42.refs_0_, f32[128,128]{1,0:T(8,128)S(1)} %collective-permute-done.13.refs_1_, ...), custom_call_target="tpu_custom_call" | custom-call | tf_op jit(solution)/shard_map/pallas_call | solution.py:18
  51.2 1.2 %collective-permute-start.16 = (f32[16,32]{1,0:T(8,128)S(1)}, f32[16,32]{1,0:T(8,128)S(1)}, u32[]{:S(2)}, u32[]{:S(2)}) collective-permute-start(f32[16,32]{1,0:T(8,128)S(1)} %get-tuple-element.45), channel_id=1, source_target_pairs={{0,4},{1,5},{2,6},{3,7},{4,0},{5,1},{6,2},{7,3},{8,12},{9,13},{10,... | collective-permute-start | bytes 6152 | tf_op jit(solution)/shard_map/ppermute | solution.py:408
  52.4 1.3 %shard_map.65 = f32[1024,128]{1,0:T(8,128)} custom-call(bf16[32,128,128]{2,1,0:T(8,128)(2,1)S(1)} %get-tuple-element.40.m_ref, f32[32,128]{1,0:T(8,128)S(1)} %get-tuple-element.43.mix_ref), custom_call_target="tpu_custom_call" | custom-call | tf_op jit(solution)/shard_map/pallas_call | solution.py:18
  53.7 2.1 %collective-permute-done.16 = f32[16,32]{1,0:T(8,128)S(1)} collective-permute-done((f32[16,32]{1,0:T(8,128)S(1)}, f32[16,32]{1,0:T(8,128)S(1)}, u32[]{:S(2)}, u32[]{:S(2)}) %collective-permute-start.16) | collective-permute-done | bytes 2080 | tf_op jit(solution)/shard_map/ppermute | solution.py:408
  55.8 0.6 %maximum_bitcast_fusion = f32[2,1,32,16]{2,3,1,0:T(8,128)} fusion(f32[1,16,32]{2,1,0:T(8,128)S(1)} %get-tuple-element.49, f32[1,16,32]{2,1,0:T(8,128)S(1)} %get-tuple-element.48), kind=kLoop, calls=%fused_computation | loop fusion | flops 1024 | bytes 8192
  (1 shorter events, 0.0 us)
Async XLA Ops:
  0.6 0.7 %copy-start.3 = (bf16[17]{0:T(256)(128)(2,1)S(1)}, bf16[17]{0:T(256)(128)(2,1)}, u32[]{:S(2)}) copy-start(bf16[17]{0:T(256)(128)(2,1)} %param.7) | copy-start | bytes 106
  1.3 1.2 %copy-start = (bf16[16,256,128]{2,1,0:T(8,128)(2,1)S(1)}, bf16[16,256,128]{2,1,0:T(8,128)(2,1)}, u32[]{:S(2)}) copy-start(bf16[16,256,128]{2,1,0:T(8,128)(2,1)} %x_ref.3) | copy-start | bytes 3145732
  2.5 16.0 %copy-start.1 = (bf16[16,256,128]{2,1,0:T(8,128)(2,1)S(1)}, bf16[16,256,128]{2,1,0:T(8,128)(2,1)}, u32[]{:S(2)}) copy-start(bf16[16,256,128]{2,1,0:T(8,128)(2,1)} %x_ref.3) | copy-start | bytes 3145732
  4.4 27.9 %collective-permute-start.4 = (bf16[44,16,128]{2,1,0:T(8,128)(2,1)S(1)}, bf16[44,16,128]{2,1,0:T(8,128)(2,1)S(1)}, u32[]{:S(2)}, u32[]{:S(2)}) collective-permute-start(bf16[44,16,128]{2,1,0:T(8,128)(2,1)S(1)} %get-tuple-element.35), channel_id=1, source_target_pairs={{0,4},{1,5},{2,6},{3,7},{4,0},{5,1},{6,2},{7,3},{8,12},{9,13},{10,... | collective-permute-start | bytes 540680 | tf_op jit(solution)/shard_map/ppermute | solution.py:408
  8.5 5.6 %copy-start.4 = (bf16[17]{0:T(256)(128)(2,1)S(1)}, bf16[17]{0:T(256)(128)(2,1)}, u32[]{:S(2)}) copy-start(bf16[17]{0:T(256)(128)(2,1)} %param.6) | copy-start | bytes 106
  8.8 9.7 %copy-start.2 = (bf16[2,1,32,16]{2,3,1,0:T(8,128)(2,1)S(1)}, bf16[2,1,32,16]{2,3,1,0:T(8,128)(2,1)}, u32[]{:S(2)}) copy-start(bf16[2,1,32,16]{2,3,1,0:T(8,128)(2,1)} %param.5) | copy-start | bytes 6148
  8.8 6.5 %collective-permute-start = (bf16[16,8,256]{2,1,0:T(8,128)(2,1)S(1)}, bf16[16,8,256]{2,1,0:T(8,128)(2,1)S(1)}, u32[]{:S(2)}, u32[]{:S(2)}) collective-permute-start(bf16[16,8,256]{2,1,0:T(8,128)(2,1)S(1)} %get-tuple-element.25), channel_id=1, source_target_pairs={{0,8},{8,16},{16,24},{1,9},{9,17},{17,25},{2,10},{10,18},{18,26},{... | collective-permute-start | bytes 196616 | tf_op jit(solution)/shard_map/ppermute | solution.py:436
  12.4 6.2 %collective-permute-start.1 = (bf16[16,8,256]{2,1,0:T(8,128)(2,1)S(1)}, bf16[16,8,256]{2,1,0:T(8,128)(2,1)S(1)}, u32[]{:S(2)}, u32[]{:S(2)}) collective-permute-start(bf16[16,8,256]{2,1,0:T(8,128)(2,1)S(1)} %get-tuple-element.26), channel_id=1, source_target_pairs={{8,0},{16,8},{24,16},{9,1},{17,9},{25,17},{10,2},{18,10},{26,18},{... | collective-permute-start | bytes 196616 | tf_op jit(solution)/shard_map/ppermute | solution.py:437
  13.7 8.2 %collective-permute-start.6 = (bf16[24,16,128]{2,1,0:T(8,128)(2,1)S(1)}, bf16[24,16,128]{2,1,0:T(8,128)(2,1)S(1)}, u32[]{:S(2)}, u32[]{:S(2)}) collective-permute-start(bf16[24,16,128]{2,1,0:T(8,128)(2,1)S(1)} %get-tuple-element.24.after_ref), channel_id=1, source_target_pairs={{0,4},{1,5},{2,6},{3,7},{4,0},{5,1},{6,2},{7,3},{8,12},{9,13},{10,... | collective-permute-start | bytes 294920 | tf_op jit(solution)/shard_map/ppermute | solution.py:408
  21.4 10.8 %collective-permute-start.2 = (bf16[11,16,128]{2,1,0:T(8,128)(2,1)S(1)}, bf16[11,16,128]{2,1,0:T(8,128)(2,1)S(1)}, u32[]{:S(2)}, u32[]{:S(2)}) collective-permute-start(bf16[11,16,128]{2,1,0:T(8,128)(2,1)S(1)} %get-tuple-element.32), channel_id=1, source_target_pairs={{0,4},{1,5},{2,6},{3,7},{4,0},{5,1},{6,2},{7,3},{8,12},{9,13},{10,... | collective-permute-start | bytes 135176 | tf_op jit(solution)/shard_map/ppermute | solution.py:408
  21.8 12.2 %collective-permute-start.7 = (bf16[69,16,128]{2,1,0:T(8,128)(2,1)S(1)}, bf16[69,16,128]{2,1,0:T(8,128)(2,1)S(1)}, u32[]{:S(2)}, u32[]{:S(2)}) collective-permute-start(bf16[69,16,128]{2,1,0:T(8,128)(2,1)S(1)} %get-tuple-element.38), channel_id=1, source_target_pairs={{0,6},{1,7},{2,4},{3,5},{4,2},{5,3},{6,0},{7,1},{8,14},{9,15},{10,... | collective-permute-start | bytes 847880 | tf_op jit(solution)/shard_map/ppermute | solution.py:408
  32.2 6.6 %collective-permute-start.5 = (bf16[69,16,128]{2,1,0:T(8,128)(2,1)S(1)}, bf16[69,16,128]{2,1,0:T(8,128)(2,1)S(1)}, u32[]{:S(2)}, u32[]{:S(2)}) collective-permute-start(bf16[69,16,128]{2,1,0:T(8,128)(2,1)S(1)} %get-tuple-element.36), channel_id=1, source_target_pairs={{0,2},{1,3},{2,0},{3,1},{4,6},{5,7},{6,4},{7,5},{8,10},{9,11},{10,... | collective-permute-start | bytes 847880 | tf_op jit(solution)/shard_map/ppermute | solution.py:408
  34.1 8.0 %collective-permute-start.10 = (bf16[69,16,128]{2,1,0:T(8,128)(2,1)S(1)}, bf16[69,16,128]{2,1,0:T(8,128)(2,1)S(1)}, u32[]{:S(2)}, u32[]{:S(2)}) collective-permute-start(bf16[69,16,128]{2,1,0:T(8,128)(2,1)S(1)} %collective-permute-done.7.refs_4_), channel_id=1, source_target_pairs={{0,1},{1,0},{2,3},{3,2},{4,5},{5,4},{6,7},{7,6},{8,9},{9,8},{10,11... | collective-permute-start | bytes 847880 | tf_op jit(solution)/shard_map/ppermute | solution.py:408
  38.8 3.2 %collective-permute-start.8 = (bf16[69,16,128]{2,1,0:T(8,128)(2,1)S(1)}, bf16[69,16,128]{2,1,0:T(8,128)(2,1)S(1)}, u32[]{:S(2)}, u32[]{:S(2)}) collective-permute-start(bf16[69,16,128]{2,1,0:T(8,128)(2,1)S(1)} %collective-permute-done.5.refs_2_), channel_id=1, source_target_pairs={{0,1},{1,0},{2,3},{3,2},{4,5},{5,4},{6,7},{7,6},{8,9},{9,8},{10,11... | collective-permute-start | bytes 847880 | tf_op jit(solution)/shard_map/ppermute | solution.py:408
  38.8 3.2 %collective-permute-start.12 = (bf16[44,16,128]{2,1,0:T(8,128)(2,1)S(1)}, bf16[44,16,128]{2,1,0:T(8,128)(2,1)S(1)}, u32[]{:S(2)}, u32[]{:S(2)}) collective-permute-start(bf16[44,16,128]{2,1,0:T(8,128)(2,1)S(1)} %collective-permute-done.4.refs_10_), channel_id=1, source_target_pairs={{0,1},{1,0},{2,3},{3,2},{4,5},{5,4},{6,7},{7,6},{8,9},{9,8},{10,11... | collective-permute-start | bytes 540680 | tf_op jit(solution)/shard_map/ppermute | solution.py:408
  39.3 1.4 %collective-permute-start.9 = (bf16[11,16,128]{2,1,0:T(8,128)(2,1)S(1)}, bf16[11,16,128]{2,1,0:T(8,128)(2,1)S(1)}, u32[]{:S(2)}, u32[]{:S(2)}) collective-permute-start(bf16[11,16,128]{2,1,0:T(8,128)(2,1)S(1)} %collective-permute-done.2.refs_3_), channel_id=1, source_target_pairs={{0,1},{1,0},{2,3},{3,2},{4,5},{5,4},{6,7},{7,6},{8,9},{9,8},{10,11... | collective-permute-start | bytes 135176 | tf_op jit(solution)/shard_map/ppermute | solution.py:408
  39.4 2.7 %collective-permute-start.3 = (bf16[35,16,128]{2,1,0:T(8,128)(2,1)S(1)}, bf16[35,16,128]{2,1,0:T(8,128)(2,1)S(1)}, u32[]{:S(2)}, u32[]{:S(2)}) collective-permute-start(bf16[35,16,128]{2,1,0:T(8,128)(2,1)S(1)} %get-tuple-element.33), channel_id=1, source_target_pairs={{0,1},{1,0},{2,3},{3,2},{4,5},{5,4},{6,7},{7,6},{8,9},{9,8},{10,11... | collective-permute-start | bytes 430088 | tf_op jit(solution)/shard_map/ppermute | solution.py:408
  40.7 1.3 %collective-permute-start.11 = (bf16[24,16,128]{2,1,0:T(8,128)(2,1)S(1)}, bf16[24,16,128]{2,1,0:T(8,128)(2,1)S(1)}, u32[]{:S(2)}, u32[]{:S(2)}) collective-permute-start(bf16[24,16,128]{2,1,0:T(8,128)(2,1)S(1)} %collective-permute-done.6.refs_8_), channel_id=1, source_target_pairs={{0,1},{1,0},{2,3},{3,2},{4,5},{5,4},{6,7},{7,6},{8,9},{9,8},{10,11... | collective-permute-start | bytes 294920 | tf_op jit(solution)/shard_map/ppermute | solution.py:408
  43.3 1.9 %collective-permute-start.13 = (f32[128,128]{1,0:T(8,128)S(1)}, f32[128,128]{1,0:T(8,128)S(1)}, u32[]{:S(2)}, u32[]{:S(2)}) collective-permute-start(f32[128,128]{1,0:T(8,128)S(1)} %get-tuple-element.42.refs_0_), channel_id=1, source_target_pairs={{0,1},{1,0},{2,3},{3,2},{4,5},{5,4},{6,7},{7,6},{8,9},{9,8},{10,11... | collective-permute-start | bytes 196616 | tf_op jit(solution)/shard_map/ppermute | solution.py:408
  43.5 4.9 %collective-permute-start.14 = (f32[128,128]{1,0:T(8,128)S(1)}, f32[128,128]{1,0:T(8,128)S(1)}, u32[]{:S(2)}, u32[]{:S(2)}) collective-permute-start(f32[128,128]{1,0:T(8,128)S(1)} %get-tuple-element.42.refs_0_), channel_id=1, source_target_pairs={{0,2},{1,3},{2,0},{3,1},{4,6},{5,7},{6,4},{7,5},{8,10},{9,11},{10,... | collective-permute-start | bytes 196616 | tf_op jit(solution)/shard_map/ppermute | solution.py:408
  44.1 4.6 %collective-permute-start.15 = (f32[128,128]{1,0:T(8,128)S(1)}, f32[128,128]{1,0:T(8,128)S(1)}, u32[]{:S(2)}, u32[]{:S(2)}) collective-permute-start(f32[128,128]{1,0:T(8,128)S(1)} %get-tuple-element.42.refs_0_), channel_id=1, source_target_pairs={{0,3},{1,2},{2,1},{3,0},{4,7},{5,6},{6,5},{7,4},{8,11},{9,10},{10,... | collective-permute-start | bytes 196616 | tf_op jit(solution)/shard_map/ppermute | solution.py:408
  51.2 4.6 %collective-permute-start.16 = (f32[16,32]{1,0:T(8,128)S(1)}, f32[16,32]{1,0:T(8,128)S(1)}, u32[]{:S(2)}, u32[]{:S(2)}) collective-permute-start(f32[16,32]{1,0:T(8,128)S(1)} %get-tuple-element.45), channel_id=1, source_target_pairs={{0,4},{1,5},{2,6},{3,7},{4,0},{5,1},{6,2},{7,3},{8,12},{9,13},{10,... | collective-permute-start | bytes 6152 | tf_op jit(solution)/shard_map/ppermute | solution.py:408

commit v3 on v2

v3 whole, which is shorter than its diff:
```python
import functools
import math

import jax
import jax.numpy as jnp
from jax import lax
from jax.experimental import pallas as pl
from jax.experimental.pallas import tpu as pltpu
from jax.sharding import PartitionSpec as P

TY = 2
F32 = jnp.float32
BF16 = jnp.bfloat16


def call(kernel, outs, ins, scratch=(), places=None, grant=40 << 20, aliases=None):
    places = places or [pltpu.VMEM] * len(ins)
    return pl.pallas_call(
        kernel,
        out_shape=outs,
        in_specs=[pl.BlockSpec(memory_space=place) for place in places],
        out_specs=[pl.BlockSpec(memory_space=pltpu.VMEM)] * len(outs),
        scratch_shapes=scratch,
        input_output_aliases=aliases or {},
        compiler_params=pltpu.CompilerParams(vmem_limit_bytes=grant),
        cost_estimate=pl.CostEstimate(flops=0, bytes_accessed=0, transcendentals=0),
    )(*ins)


def toeplitz(tap_row, rows, cols, shift, sign=1):
    offsets = sign * (
        lax.broadcasted_iota(jnp.int32, (rows, cols), 1)
        - lax.broadcasted_iota(jnp.int32, (rows, cols), 0)
    )
    offsets = offsets + shift
    total = jnp.zeros((rows, cols), F32)
    for t in range(tap_row.shape[1]):
        total = jnp.where(offsets == t, tap_row[:, t : t + 1], total)
    return total


def contract(left, right, left_dim, right_dim):
    return lax.dot_general(
        left, right, (((left_dim,), (right_dim,)), ((), ())), preferred_element_type=F32
    )


def split(value):
    high = value.astype(BF16)
    return high, (value - high.astype(F32)).astype(BF16)


def turned(value, shift):
    return pltpu.roll(value, shift % value.shape[1], 1)


def device_at(index, count, shift, flip):
    return (index // 2 + shift) % (count // 2) * 2 + (index % 2 + flip) % 2


def put_rows(out_ref, at, first, size, rows_scr):
    _, frames, cols = out_ref.shape
    start = pl.multiple_of(first * frames, frames)
    block = rows_scr[pl.ds(start, size * frames), :].astype(BF16)
    out_ref[at : at + size] = block.reshape(size, frames, cols)


def put_anchor(out_ref, at, first, size, anchor_scr):
    _, frames, cols = out_ref.shape
    block = anchor_scr[pl.ds(pl.multiple_of(first, size), size), :].astype(BF16)
    out_ref[at : at + size // frames] = block.reshape(size // frames, frames, cols)


def put_omega(out_ref, at, omega):
    frames, cols = out_ref.shape[1], out_ref.shape[2]
    ranks = omega.shape[1]
    out_ref[at, :, 0:ranks] = omega
    out_ref[at, :, ranks:] = jnp.zeros((frames, cols - ranks), BF16)


def put_block(out_ref, at, dest, share, rows_scr, anchor_scr):
    put_rows(out_ref, at, dest * share, share, rows_scr)
    put_anchor(out_ref, at + share, dest * share, share, anchor_scr)


def filter_rows(x_of, halo_of, bx, bh, dy, frames, inner, centre_scr, rows_scr, anchor_scr):
    part, span = dy.shape
    cols = bx.shape[0]

    def mean(value_of):
        total = value_of(0)
        for f in range(1, frames):
            total = total + value_of(f)
        return (total * (1.0 / frames)).astype(BF16)

    def across(block, edge):
        value = contract(block, bx, 1, 0)
        return value if edge is None else value + contract(edge, bh, 0, 0)

    def rows_made(value):
        if part == span:
            return value
        centre_scr[...] = value
        return centre_scr[pl.ds(inner, part), :]

    anchor = mean(x_of)
    edge = None if halo_of is None else mean(halo_of)
    anchor32 = anchor.astype(F32)
    edge32 = None if edge is None else edge.astype(F32)
    high, low = split(across(anchor, edge))
    both = contract(dy, jnp.concatenate([high, low], axis=1), 1, 0)
    anchor_s = rows_made(anchor32) - both[:, :cols] - both[:, cols:]
    anchor_out = anchor_s.astype(BF16).astype(F32)
    anchor_scr[...] = anchor_out
    left_over = anchor_s - anchor_out
    for p in range(frames // 2):
        blocks, smooths = [], []
        for f in (2 * p, 2 * p + 1):
            block = (x_of(f) - anchor32).astype(BF16)
            edge = None if halo_of is None else (halo_of(f) - edge32).astype(BF16)
            smooths.append(across(block, edge).astype(BF16))
            blocks.append(rows_made(block.astype(F32)))
        both = contract(dy, jnp.concatenate(smooths, axis=1), 1, 0)
        for i, f in enumerate((2 * p, 2 * p + 1)):
            value = blocks[i] - both[:, i * cols : (i + 1) * cols] + left_over
            rows_scr[pl.ds(f, part, stride=frames), :] = value


def put_edges(out_ref, at, index, rows_scr, anchor_scr, share, frames, width):
    cols = out_ref.shape[2]
    packed = cols // (2 * width)
    groups = share // packed
    lane = lax.broadcasted_iota(jnp.int32, (frames, cols), 1) // (2 * width)
    start = pl.multiple_of(index * (share * frames), share * frames)
    for group in range(groups):
        tile = jnp.zeros((frames, cols), F32)
        for q in range(packed):
            begin = pl.multiple_of(start + (group * packed + q) * frames, frames)
            value = rows_scr[pl.ds(begin, frames), :]
            tile = jnp.where(lane == q, turned(value, width + 2 * width * q), tile)
        out_ref[at + group] = tile.astype(BF16)
    first = pl.multiple_of(index * share, share)
    tile = jnp.zeros((frames, cols), F32)
    for q in range(packed):
        value = jnp.concatenate(
            [
                anchor_scr[pl.ds(first + q, groups, stride=packed), :],
                jnp.zeros((frames - groups, cols), F32),
            ],
            axis=0,
        )
        tile = jnp.where(lane == q, turned(value, width + 2 * width * q), tile)
    out_ref[at + groups] = tile.astype(BF16)


def early_kernel(axis, side, count, x_ref, taps_hbm, *rest):
    out_ref, a_ref, b_ref, *scratch = rest
    taps_ref, centre_scr, rows_scr, anchor_scr, sem = scratch
    frames, rows, cols = x_ref.shape
    part, span = anchor_scr.shape[0], centre_scr.shape[0]
    share = part // 2
    radius = (taps_ref.shape[1] - 1) // 2
    copy = pltpu.make_async_copy(taps_hbm, taps_ref, sem)
    copy.start()
    me = lax.axis_index(axis)
    chip = device_at(me, count, count // 4, 0) // 2
    first = jnp.clip(chip * part - (span - part) // 2, 0, rows - span)
    first = pl.multiple_of(first, 16)
    inner = pl.multiple_of(chip * part - first, 16)
    copy.wait()
    taps = taps_ref[...].astype(F32)
    bx = toeplitz(taps, cols, cols, radius, -1).astype(BF16)
    dy = toeplitz(taps, part, span, radius - inner).astype(BF16)
    scratch = (centre_scr, rows_scr, anchor_scr)

    def x_of(f):
        return x_ref[f, pl.ds(first, span), :].astype(F32)

    filter_rows(x_of, None, bx, None, dy, frames, inner, *scratch)
    for h in range(2):
        put_block(out_ref, h * (share + share // frames), (me + h) % 2, share, rows_scr, anchor_scr)

    row = lax.broadcasted_iota(jnp.int32, (2 * radius, cols), 0)
    col = lax.broadcasted_iota(jnp.int32, (2 * radius, cols), 1)
    right = (row < radius) == (lax.axis_index(side) % 2 == 0)
    wanted = row % radius + jnp.where(right, cols - radius, 0)
    pick = jnp.where(col == wanted, 1.0, 0.0).astype(BF16)
    for f in range(frames):
        both = contract(pick, x_ref[f], 1, 1).astype(BF16)
        a_ref[f] = both[:radius]
        b_ref[f] = both[radius:]


def bands_kernel(side, space_ref, time_ref, bx_ref, bh_ref, dy_ref, lhs_ref):
    rows, cols = dy_ref.shape[0], bx_ref.shape[0]
    space, time = space_ref[...].astype(F32), time_ref[...].astype(F32)
    radius = (space.shape[1] - 1) // 2
    bx_ref[...] = toeplitz(space, cols, cols, radius, -1).astype(BF16)
    left = toeplitz(space, radius, cols, 0, -1)
    right = toeplitz(space, radius, cols, radius + cols, -1)
    odd = lax.axis_index(side) % 2 == 1
    bh_ref[0:radius] = jnp.where(odd, left, right).astype(BF16)
    bh_ref[radius:] = jnp.where(odd, right, left).astype(BF16)
    dy_ref[...] = toeplitz(space, rows, rows, radius).astype(BF16)
    all_frames = lhs_ref.shape[0]
    count = (lhs_ref.shape[1] - all_frames) // 2
    frames = all_frames // count
    band = toeplitz(time, all_frames, all_frames, radius)
    ids = lax.broadcasted_iota(jnp.int32, (all_frames, count), 0) // frames
    lane = lax.broadcasted_iota(jnp.int32, (all_frames, count), 1)
    sums = jnp.where(ids == lane, 1.0, 0.0)
    for j in range(count):
        piece = jnp.sum(band[:, j * frames : (j + 1) * frames], axis=1, keepdims=True)
        sums = jnp.where(lane == j, sums - piece, sums)
    high, low = split(sums)
    lhs_ref[:, 0:all_frames] = (-band).astype(BF16)
    lhs_ref[:, all_frames:] = jnp.concatenate([high.astype(F32), low.astype(F32)], 1).astype(BF16)


def spatial_kernel(axis, x_ref, a_ref, b_ref, bx_ref, bh_ref, dy_ref, om_ref, *rest):
    outs, edge_refs, (rows_scr, anchor_scr) = rest[:-4], rest[-4:-2], rest[-2:]
    frames, rows, cols = x_ref.shape
    radius = a_ref.shape[1]
    share = (outs[0].shape[0] - 1) * frames // (frames + 1)
    count = rows // share
    me = lax.axis_index(axis)

    def halo(f):
        return jnp.concatenate([a_ref[f].astype(F32), b_ref[f].astype(F32)], axis=0)

    scratch = (None, rows_scr, anchor_scr)
    filter_rows(
        lambda f: x_ref[f].astype(F32), halo, bx_ref[...], bh_ref[...], dy_ref[...], frames, 0, *scratch
    )
    early = count // 4
    for (shift, flips), out in zip(message_list(count), outs):
        for i, flip in enumerate(flips):
            dest = device_at(me, count, shift, flip)
            at = i * (share + share // frames + 1)
            put_block(out, at, dest, share, rows_scr, anchor_scr)
            put_omega(out, at + share + share // frames, om_ref[dest // (count // TY)])
    for h, out in enumerate(edge_refs):
        dest = device_at(me, count, early, h)
        put_edges(out, 0, dest, rows_scr, anchor_scr, share, frames, radius)
        put_omega(out, out.shape[0] - 1, om_ref[dest // (count // TY)])


def message_list(count):
    return [(c, (flip,)) for c in range(count // 2) if c != count // 4 for flip in range(2)]


def take_block(data_ref, anchor_ref, ref, at, src):
    share, count, frames, cols = data_ref.shape
    data_ref[:, src] = ref[at : at + share]
    anchor = ref[at + share : at + share + share // frames].reshape(share, cols)
    anchor_ref[pl.ds(src, share, stride=count), :] = anchor.astype(F32)


def take_edges(data_ref, anchor_ref, ref, src, width):
    share, count, frames, cols = data_ref.shape
    packed = cols // (2 * width)
    groups = share // packed
    lanes = lax.broadcasted_iota(jnp.int32, (frames, cols), 1)
    at_edge = (lanes < width) | (lanes >= cols - width)
    last = ref[groups].astype(F32)
    for q in range(packed):
        edge = turned(last, -(width + 2 * width * q))[:groups]
        where = pl.ds(src + q * count, groups, stride=count * packed)
        old = anchor_ref[where, :]
        anchor_ref[where, :] = jnp.where(at_edge[:groups], edge, old)
    for group in range(groups):
        tile = ref[group].astype(F32)
        for q in range(packed):
            r = group * packed + q
            edge = turned(tile, -(width + 2 * width * q))
            value = jnp.where(at_edge, edge, data_ref[r, src].astype(F32))
            data_ref[r, src] = value.astype(BF16)


def gather_kernel(axis, places, *refs):
    blocks, mains, (data_ref, anchor_ref, om_ref) = refs[:-5], refs[-5:-3], refs[-3:]
    share, count, frames, _ = data_ref.shape
    slots = share + share // frames
    me = lax.axis_index(axis)
    for (shift, flip), ref in zip(places, blocks):
        src = device_at(me, count, -shift, flip)
        take_block(data_ref, anchor_ref, ref, 0, src)
        om_ref[src] = ref[slots]
    for h, ref in enumerate(mains):
        take_block(data_ref, anchor_ref, ref, 0, device_at(me, count, -(count // 4), h))


def temporal_kernel(axis, width, places, *refs):
    blocks, edge_refs, lhs_ref = refs[3:-8], refs[-8:-6], refs[-6]
    data_ref, anchor_ref, om_ref, m_ref, gram_ref = refs[-5:]
    share, count, frames, cols = data_ref.shape
    all_frames = count * frames
    slots = share + share // frames
    me = lax.axis_index(axis)
    for (shift, flip), ref in zip(places, blocks):
        src = device_at(me, count, -shift, flip)
        take_block(data_ref, anchor_ref, ref, 0, src)
        om_ref[src] = ref[slots]
    for h, ref in enumerate(edge_refs):
        src = device_at(me, count, -(count // 4), h)
        take_edges(data_ref, anchor_ref, ref, src, width)
        om_ref[src] = ref[ref.shape[0] - 1]
    lhs = lhs_ref[...]
    gram = jnp.zeros((all_frames, all_frames), F32)
    for p in range(share // 2):
        blocks, feeds = [], []
        for r in (2 * p, 2 * p + 1):
            block = data_ref[r].reshape(all_frames, cols)
            anchor = anchor_ref[r * count : (r + 1) * count, :]
            blocks.append(block)
            feeds.append(
                jnp.concatenate([block, jnp.concatenate([anchor, anchor], 0).astype(BF16)], axis=0)
            )
        low = contract(lhs, jnp.concatenate(feeds, axis=1), 1, 0)
        value = (jnp.concatenate(blocks, axis=1).astype(F32) + low).astype(BF16)
        m_ref[2 * p] = value[:, :cols]
        m_ref[2 * p + 1] = value[:, cols:]
        gram = gram + contract(value, value, 1, 1)
    gram_ref[...] = gram


def exact(left, right, left_dim, right_dim):
    return lax.dot_general(
        left,
        right,
        (((left_dim,), (right_dim,)), ((), ())),
        precision=lax.Precision.HIGHEST,
        preferred_element_type=F32,
    )


def whiten(gram, *others):
    size = gram.shape[0]
    ids = lax.broadcasted_iota(jnp.int32, (size, 128), 0)
    work = [jnp.concatenate([gram, jnp.zeros((size, 128 - size), F32)], axis=1), *others]
    scale = jnp.zeros((size, 128), F32)
    panel = 8
    for start in range(0, size, panel):
        cols = [
            jnp.broadcast_to(work[0][:, j : j + 1], (size, 128)) for j in range(start, start + panel)
        ]
        for j in range(start, start + panel):
            inverse = 1.0 / cols[j - start][j : j + 1]
            factor = jnp.where(ids > j, cols[j - start] * inverse, 0.0)
            scale = jnp.where(ids == j, inverse, scale)
            for m in range(j - start + 1, panel):
                cols[m] = cols[m] - factor * cols[m][j : j + 1]
            for i in range(len(work)):
                value = work[i]
                width = value.shape[1]
                parts = [
                    value[:, c : c + 128] - factor * value[j : j + 1, c : c + 128]
                    for c in range(0, width, 128)
                ]
                work[i] = parts[0] if len(parts) == 1 else jnp.concatenate(parts, axis=1)
    scale = jnp.sqrt(scale)
    results = []
    for value in work[1:]:
        parts = [value[:, c : c + 128] * scale for c in range(0, value.shape[1], 128)]
        results.append(parts[0] if len(parts) == 1 else jnp.concatenate(parts, axis=1))
    return results


def factor_kernel(axis, count, ranks, pixels, om_ref, *refs):
    grams, (mix_ref, own_ref, send_ref) = refs[:-3], refs[-3:]
    frames = own_ref.shape[1]
    all_frames = grams[0].shape[0]
    me = lax.axis_index(axis)
    gram = grams[0][...]
    for other in grams[1:]:
        gram = gram + other[...]
    omega = om_ref[...].reshape(all_frames, om_ref.shape[2]).astype(F32).T[:ranks]
    sketch = exact(omega, gram, 1, 0)
    (load,) = whiten(exact(sketch, omega, 1, 1), sketch)
    back = exact(load, gram, 1, 0)
    mix, coef = whiten(exact(back, load, 1, 1), load, back)
    mix_ref[...] = mix * math.sqrt(pixels)
    ids = lax.broadcasted_iota(jnp.int32, (frames, all_frames), 0)
    lane = lax.broadcasted_iota(jnp.int32, (frames, all_frames), 1)
    for ref, who in ((own_ref, me), (send_ref, me ^ (count // TY))):
        pick = jnp.where(lane == ids + who * frames, 1.0, 0.0)
        ref[...] = jnp.zeros_like(ref)
        ref[me // (count // TY)] = exact(pick, coef, 1, 1)


def basis_kernel(m_ref, mix_ref, out_ref):
    share, _, cols = m_ref.shape
    ranks = mix_ref.shape[0]
    high, low = split(mix_ref[...])
    lhs = jnp.concatenate([high, low], axis=0)
    for p in range(share // 2):
        data = jnp.concatenate([m_ref[2 * p], m_ref[2 * p + 1]], axis=1)
        both = contract(lhs, data, 1, 0)
        value = both[:ranks] + both[ranks:]
        for i in range(2):
            out_ref[pl.ds(2 * p + i, ranks, stride=share), :] = value[:, i * cols : (i + 1) * cols]


def local(movie, omega, time_taps, space_taps):
    frames, rows, cols = movie.shape
    radius = (space_taps.shape[0] - 1) // 2
    count = lax.axis_size("tm")
    tiles = lax.axis_size("tile")
    ranks = omega.shape[2]
    share = rows // count
    all_frames = frames * count
    group = count // TY
    pixels = (rows // TY) * cols
    early = count // 4
    packed = cols // (2 * radius)
    slots = share + share // frames

    def shape(dims, dtype):
        return jax.ShapeDtypeStruct(dims, dtype)

    def swap(value, k):
        return lax.ppermute(value, "tm", [(i, i ^ k) for i in range(count)])

    def send(value, shift, flip):
        return lax.ppermute(value, "tm", [(i, device_at(i, count, shift, flip)) for i in range(count)])

    space_row, time_row = space_taps[None], time_taps[None]
    part = 2 * share
    span = part + 32
    main, side_a, side_b = call(
        functools.partial(early_kernel, "tm", "tile", count),
        [
            shape((2 * slots, frames, cols), BF16),
            *([shape((frames, radius, rows), BF16)] * 2),
        ],
        [movie, space_row],
        [
            pltpu.VMEM(space_row.shape, BF16),
            pltpu.VMEM((span, cols), F32),
            pltpu.VMEM((part * frames, cols), F32),
            pltpu.VMEM((part, cols), F32),
            pltpu.SemaphoreType.DMA,
        ],
        [pltpu.VMEM, pltpu.HBM],
    )
    main = send(main, early, 0)
    pairs = [(i, i ^ 1) for i in range(tiles)]
    side_a = lax.ppermute(side_a, "tile", pairs)
    pairs = [(i, i + 1) for i in range(1, tiles - 1, 2)]
    side_b = lax.ppermute(side_b, "tile", pairs + [(j, i) for i, j in pairs])
    bx, bh, dy, lhs = call(
        functools.partial(bands_kernel, "tile"),
        [
            shape((cols, cols), BF16),
            shape((2 * radius, cols), BF16),
            shape((rows, rows), BF16),
            shape((all_frames, all_frames + 2 * count), BF16),
        ],
        [space_row, time_row],
    )
    om = jnp.transpose(omega[:, 0], (0, 2, 1))
    listed = message_list(count)
    *parts, edges, edges_other = call(
        functools.partial(spatial_kernel, "tm"),
        [
            *[shape((len(flips) * (slots + 1), frames, cols), BF16) for _, flips in listed],
            *([shape((share // packed + 2, frames, cols), BF16)] * 2),
        ],
        [movie, side_a, side_b, bx, bh, dy, om],
        [pltpu.VMEM((rows * frames, cols), F32), pltpu.VMEM((rows, cols), F32)],
    )
    edges, edges_other = send(edges, early, 0), send(edges_other, early, 1)
    came = [
        send(value, shift, flips[0] if len(flips) == 1 else 0)
        for (shift, flips), value in zip(listed[2:], parts[2:])
    ]
    blocks = [parts[0], send(parts[1], 0, 1)]
    for (_, flips), value in zip(listed[2:], came):
        blocks += [value] if len(flips) == 1 else [value, swap(value[slots + 1 :], 1)]
    places = [(shift, flip) for shift, flips in listed for flip in flips]
    known = call(
        functools.partial(gather_kernel, "tm", places[:-2]),
        [
            shape((share, count, frames, cols), BF16),
            shape((share * count, cols), F32),
            shape((count, frames, cols), BF16),
        ],
        [*blocks[:-2], main, swap(main[slots:], 1)],
    )
    _, _, om_all, matrix, gram = call(
        functools.partial(temporal_kernel, "tm", radius, places[-2:]),
        [
            *[shape(value.shape, value.dtype) for value in known],
            shape((share, all_frames, cols), BF16),
            shape((all_frames, all_frames), F32),
        ],
        [*known, *blocks[-2:], edges, edges_other, lhs],
        aliases={0: 0, 1: 1, 2: 2},
    )
    grams = [gram] + [swap(gram, k) for k in range(1, group)]
    mix, coef_own, coef_send = call(
        functools.partial(factor_kernel, "tm", count, ranks, pixels),
        [shape((ranks, all_frames), F32), *([shape((TY, frames, ranks), F32)] * 2)],
        [om_all, *grams],
    )
    coef_other = swap(coef_send, group)
    (basis,) = call(basis_kernel, [shape((ranks * share, cols), F32)], [matrix, mix])
    coefficients = jnp.transpose(coef_own + coef_other, (0, 2, 1))[:, None]
    return basis.reshape(ranks, share, cols), coefficients


def solution(mesh):
    in_specs = (P("tm", None, "tile"), P(None, "tile", None, "tm"), P(), P())
    out_specs = (P(None, "tm", "tile"), P(None, "tile", None, "tm"))
    return jax.shard_map(local, mesh=mesh, in_specs=in_specs, out_specs=out_specs, check_vma=False)
```

time: 56.6 us -> 53.2 us (0.940)
  the two profiles are of different devices: /device:TPU:0 before, /device:TPU:4 now
where the time goes in v3:
time: 53.2 us; the launch traced here: 52.7 us
  waiting for transfers between devices  23.9 us (45%)
  starting transfers between devices  14.4 us (27%)
  Pallas kernels  11.1 us (21%)
  local copies, waits for them, and re-layouts  1.9 us (4%)
  between operations  0.75 us (1%)
  other arithmetic  0.61 us (1%)
    ppermute x8, waiting for transfers between devices, send(): lax.ppermute(value, 'tm', [(i, device_at(i, count, shift, flip)) for i in...  13.2 us
    pallas_call x7, Pallas kernels, call(): pl.pallas_call(kernel, out_shape=outs, in_specs=[pl.BlockSpec(memory_spac...  11.1 us
    ppermute x8, starting transfers between devices, send(): lax.ppermute(value, 'tm', [(i, device_at(i, count, shift, flip)) for i in...  8.07 us
    ppermute x5, waiting for transfers between devices, swap(): return lax.ppermute(value, 'tm', [(i, i ^ k) for i in range(count)])  7.27 us
    ppermute x1, waiting for transfers between devices, local(): side_b = lax.ppermute(side_b, 'tile', pairs + [(j, i) for i, j in pairs])  3.44 us
    ppermute x5, starting transfers between devices, swap(): return lax.ppermute(value, 'tm', [(i, i ^ k) for i in range(count)])  2.48 us
    ppermute x1, starting transfers between devices, local(): side_b = lax.ppermute(side_b, 'tile', pairs + [(j, i) for i, j in pairs])  2.37 us
    unnamed x10, local copies, waits for them, and re-layouts  1.89 us
  transfers between devices with their start and end apart: 15, of which 8 were waited for; matrix products, arithmetic and copies ran while one was open for 0% of the time, Pallas kernels for 10%

profile of v3, /device:TPU:4, one launch (start us, length us, event | category | flops | bytes accessed | tf_op | source)
XLA Modules:
  0.0 52.7 jit_solution(6812893604334156662)
XLA Ops:
  0.6 0.0 copy-start.3
  0.6 0.6 %copy-done.3 = bf16[17]{0:T(256)(128)(2,1)S(1)} copy-done((bf16[17]{0:T(256)(128)(2,1)S(1)}, bf16[17]{0:T(256)(128)(2,1)}, u32[]{:S(2)}) %copy-start.3) | copy-done | bytes 58
  1.3 0.0 copy-start
  1.3 1.2 %copy-done = bf16[16,256,128]{2,1,0:T(8,128)(2,1)S(1)} copy-done((bf16[16,256,128]{2,1,0:T(8,128)(2,1)S(1)}, bf16[16,256,128]{2,1,0:T(8,128)(2,1)}, u32[]{:S(2)}) %copy-start) | copy-done | bytes 1048600
  2.5 0.0 copy-start.4
  2.5 0.0 copy-start.1
  2.5 2.0 %shard_map.59 = (bf16[68,16,128]{2,1,0:T(8,128)(2,1)S(1)}, bf16[16,8,256]{2,1,0:T(8,128)(2,1)S(1)}, bf16[16,8,256]{2,1,0:T(8,128)(2,1)S(1)}) custom-call(bf16[16,256,128]{2,1,0:T(8,128)(2,1)S(1)} %copy-done, bf16[1,17]{1,0:T(2,128)(2,1)S(1)} %bitcast.13), custom_call_target="tpu_custom_call" | custom-call | tf_op jit(solution)/shard_map/pallas_call | solution.py:18
  4.5 0.0 copy-start.2
  4.5 2.7 %collective-permute-start.5 = (bf16[68,16,128]{2,1,0:T(8,128)(2,1)S(1)}, bf16[68,16,128]{2,1,0:T(8,128)(2,1)S(1)}, u32[]{:S(2)}, u32[]{:S(2)}) collective-permute-start(bf16[68,16,128]{2,1,0:T(8,128)(2,1)S(1)} %get-tuple-element.35), channel_id=1, source_target_pairs={{0,4},{1,5},{2,6},{3,7},{4,0},{5,1},{6,2},{7,3},{8,12},{9,13},{10,... | collective-permute-start | bytes 835592 | tf_op jit(solution)/shard_map/ppermute | solution.py:425
  7.2 1.5 %collective-permute-start = (bf16[16,8,256]{2,1,0:T(8,128)(2,1)S(1)}, bf16[16,8,256]{2,1,0:T(8,128)(2,1)S(1)}, u32[]{:S(2)}, u32[]{:S(2)}) collective-permute-start(bf16[16,8,256]{2,1,0:T(8,128)(2,1)S(1)} %get-tuple-element.26), channel_id=1, source_target_pairs={{0,8},{8,0},{16,24},{24,16},{1,9},{9,1},{17,25},{25,17},{2,10},{10... | collective-permute-start | bytes 196616 | tf_op jit(solution)/shard_map/ppermute | solution.py:448
  8.7 2.4 %collective-permute-start.1 = (bf16[16,8,256]{2,1,0:T(8,128)(2,1)S(1)}, bf16[16,8,256]{2,1,0:T(8,128)(2,1)S(1)}, u32[]{:S(2)}, u32[]{:S(2)}) collective-permute-start(bf16[16,8,256]{2,1,0:T(8,128)(2,1)S(1)} %get-tuple-element.27), channel_id=1, source_target_pairs={{8,16},{16,8},{9,17},{17,9},{10,18},{18,10},{11,19},{19,11},{12,20... | collective-permute-start | bytes 196616 | tf_op jit(solution)/shard_map/ppermute | solution.py:450
  11.1 0.0 copy-done.4
  11.1 1.2 %shard_map.60 = (bf16[128,128]{1,0:T(8,128)(2,1)S(1)}, bf16[16,128]{1,0:T(8,128)(2,1)S(1)}, bf16[256,256]{1,0:T(8,128)(2,1)S(1)}, bf16[128,144]{1,0:T(8,128)(2,1)S(1)}) custom-call(bf16[1,17]{1,0:T(2,128)(2,1)S(1)} %bitcast.14, bf16[1,17]{1,0:T(2,128)(2,1)S(1)} %bitcast.15), custom_call_target="tpu_custom_call" | custom-call | tf_op jit(solution)/shard_map/pallas_call | solution.py:18
  12.3 0.0 collective-permute-done.a_ref
  12.3 3.4 %collective-permute-done.1.b_ref = bf16[16,8,256]{2,1,0:T(8,128)(2,1)S(1)} collective-permute-done((bf16[16,8,256]{2,1,0:T(8,128)(2,1)S(1)}, bf16[16,8,256]{2,1,0:T(8,128)(2,1)S(1)}, u32[]{:S(2)}, u32[]{:S(2)}) %collective-permute-start.1) | collective-permute-done | bytes 65568 | tf_op jit(solution)/shard_map/ppermute | solution.py:450
  15.7 0.0 copy-done.1
  15.7 0.0 copy-done.2
  15.7 2.8 %shard_map.61 = (bf16[35,16,128]{2,1,0:T(8,128)(2,1)S(1)}, bf16[35,16,128]{2,1,0:T(8,128)(2,1)S(1)}, bf16[35,16,128]{2,1,0:T(8,128)(2,1)S(1)}, bf16[35,16,128]{2...) custom-call(bf16[16,256,128]{2,1,0:T(8,128)(2,1)S(1)} %copy-done.1, ...), custom_call_target="tpu_custom_call" | custom-call | tf_op jit(solution)/shard_map/pallas_call | solution.py:18
  18.6 0.1 collective-permute-start.2
  18.7 1.6 %collective-permute-start.3 = (bf16[35,16,128]{2,1,0:T(8,128)(2,1)S(1)}, bf16[35,16,128]{2,1,0:T(8,128)(2,1)S(1)}, u32[]{:S(2)}, u32[]{:S(2)}) collective-permute-start(bf16[35,16,128]{2,1,0:T(8,128)(2,1)S(1)} %get-tuple-element.33), channel_id=1, source_target_pairs={{0,2},{1,3},{2,4},{3,5},{4,6},{5,7},{6,0},{7,1},{8,10},{9,11},{10,... | collective-permute-start | bytes 430088 | tf_op jit(solution)/shard_map/ppermute | solution.py:425
  20.3 0.1 collective-permute-start.4
  20.4 3.5 %collective-permute-start.7 = (bf16[35,16,128]{2,1,0:T(8,128)(2,1)S(1)}, bf16[35,16,128]{2,1,0:T(8,128)(2,1)S(1)}, u32[]{:S(2)}, u32[]{:S(2)}) collective-permute-start(bf16[35,16,128]{2,1,0:T(8,128)(2,1)S(1)} %get-tuple-element.39), channel_id=1, source_target_pairs={{0,6},{1,7},{2,0},{3,1},{4,2},{5,3},{6,4},{7,5},{8,14},{9,15},{10,... | collective-permute-start | bytes 430088 | tf_op jit(solution)/shard_map/ppermute | solution.py:425
  23.9 0.0 collective-permute-done.5.refs_4_
  23.9 0.1 collective-permute-start.8
  24.0 0.0 collective-permute-done.2.refs_1_
  24.0 0.5 collective-permute-start.6
  24.6 2.7 %collective-permute-done.3.refs_2_ = bf16[35,16,128]{2,1,0:T(8,128)(2,1)S(1)} collective-permute-done((bf16[35,16,128]{2,1,0:T(8,128)(2,1)S(1)}, bf16[35,16,128]{2,1,0:T(8,128)(2,1)S(1)}, u32[]{:S(2)}, u32[]{:S(2)}) %collective-permute-start.3) | collective-permute-done | bytes 143392 | tf_op jit(solution)/shard_map/ppermute | solution.py:425
  27.2 0.0 collective-permute-start.9
  27.2 2.2 %collective-permute-done.4.refs_3_ = bf16[35,16,128]{2,1,0:T(8,128)(2,1)S(1)} collective-permute-done((bf16[35,16,128]{2,1,0:T(8,128)(2,1)S(1)}, bf16[35,16,128]{2,1,0:T(8,128)(2,1)S(1)}, u32[]{:S(2)}, u32[]{:S(2)}) %collective-permute-start.4) | collective-permute-done | bytes 143392 | tf_op jit(solution)/shard_map/ppermute | solution.py:425
  29.4 0.0 collective-permute-start.10
  29.4 0.0 collective-permute-done.6.refs_5_
  29.4 0.1 shard_map.62
  29.6 7.9 %collective-permute-done.9.refs_5_ = bf16[6,16,128]{2,1,0:T(8,128)(2,1)S(1)} collective-permute-done((bf16[6,16,128]{2,1,0:T(8,128)(2,1)S(1)}, bf16[6,16,128]{2,1,0:T(8,128)(2,1)S(1)}, u32[]{:S(2)}, u32[]{:S(2)}) %collective-permute-start.9) | collective-permute-done | bytes 24608 | tf_op jit(solution)/shard_map/ppermute | solution.py:425
  37.4 0.5 collective-permute-done.10.refs_6_
  37.9 0.0 collective-permute-done.7.refs_3_
  37.9 0.0 collective-permute-done.8.refs_4_
  37.9 1.1 %shard_map.63 = (bf16[32,8,16,128]{3,2,1,0:T(8,128)(2,1)S(1)}, f32[256,128]{1,0:T(8,128)S(1)}, bf16[8,16,128]{2,1,0:T(8,128)(2,1)S(1)}, bf16[32,128,128]{2,1,0:T(8,128)(2,1)S(1)}, f32[128,128]{1,0:T(8,128)S(1)}) custom-call(bf16[32,8,16,128]{3,2,1,0:T(8,128)(2,1)S(1)} %get-tuple-element.36.refs_0_, ...), custom_call_target="tpu_custom_call", output_to_operand_aliasing={{0}: (0, {}), {1}: (1, {}), {2}: (2, {})} | custom-call | tf_op jit(solution)/shard_map/pallas_call | solution.py:18
  39.1 0.1 collective-permute-start.13
  39.2 1.7 %collective-permute-start.12 = (f32[128,128]{1,0:T(8,128)S(1)}, f32[128,128]{1,0:T(8,128)S(1)}, u32[]{:S(2)}, u32[]{:S(2)}) collective-permute-start(f32[128,128]{1,0:T(8,128)S(1)} %get-tuple-element.46.refs_0_), channel_id=1, source_target_pairs={{0,2},{1,3},{2,0},{3,1},{4,6},{5,7},{6,4},{7,5},{8,10},{9,11},{10,... | collective-permute-start | bytes 196616 | tf_op jit(solution)/shard_map/ppermute | solution.py:422
  40.9 0.1 collective-permute-start.11
  41.0 2.2 %collective-permute-done.13.refs_3_ = f32[128,128]{1,0:T(8,128)S(1)} collective-permute-done((f32[128,128]{1,0:T(8,128)S(1)}, f32[128,128]{1,0:T(8,128)S(1)}, u32[]{:S(2)}, u32[]{:S(2)}) %collective-permute-start.13) | collective-permute-done | bytes 65568 | tf_op jit(solution)/shard_map/ppermute | solution.py:422
  43.2 1.7 %collective-permute-done.12.refs_2_ = f32[128,128]{1,0:T(8,128)S(1)} collective-permute-done((f32[128,128]{1,0:T(8,128)S(1)}, f32[128,128]{1,0:T(8,128)S(1)}, u32[]{:S(2)}, u32[]{:S(2)}) %collective-permute-start.12) | collective-permute-done | bytes 65568 | tf_op jit(solution)/shard_map/ppermute | solution.py:422
  44.9 0.0 collective-permute-done.11.refs_1_
  44.9 2.5 %shard_map.64 = (f32[32,128]{1,0:T(8,128)S(1)}, f32[2,16,32]{2,1,0:T(8,128)S(1)}, f32[2,16,32]{2,1,0:T(8,128)S(1)}) custom-call(bf16[8,16,128]{2,1,0:T(8,128)(2,1)S(1)} %get-tuple-element.45.om_ref, f32[128,128]{1,0:T(8,128)S(1)} %get-tuple-element.46.refs_0_, f32[128,128]{1,0:T(8,128)S(1)} %collective-permute-done.11.refs_1_, ...), custom_call_target="tpu_custom_call" | custom-call | tf_op jit(solution)/shard_map/pallas_call | solution.py:18
  47.4 0.0 collective-permute-start.14
  47.4 1.3 %shard_map.65 = f32[1024,128]{1,0:T(8,128)} custom-call(bf16[32,128,128]{2,1,0:T(8,128)(2,1)S(1)} %get-tuple-element.44.m_ref, f32[32,128]{1,0:T(8,128)S(1)} %get-tuple-element.47.mix_ref), custom_call_target="tpu_custom_call" | custom-call | tf_op jit(solution)/shard_map/pallas_call | solution.py:18
  48.7 3.4 %collective-permute-done.14 = f32[2,16,32]{2,1,0:T(8,128)S(1)} collective-permute-done((f32[2,16,32]{2,1,0:T(8,128)S(1)}, f32[2,16,32]{2,1,0:T(8,128)S(1)}, u32[]{:S(2)}, u32[]{:S(2)}) %collective-permute-start.14) | collective-permute-done | bytes 4128 | tf_op jit(solution)/shard_map/ppermute | solution.py:422
  52.1 0.6 %add_bitcast_fusion = f32[2,1,32,16]{2,3,1,0:T(8,128)} fusion(f32[2,16,32]{2,1,0:T(8,128)S(1)} %get-tuple-element.48, f32[2,16,32]{2,1,0:T(8,128)S(1)} %collective-permute-done.14), kind=kLoop, calls=%fused_computation | loop fusion | flops 1024 | bytes 12288
  (1 shorter events, 0.0 us)
Async XLA Ops:
  0.6 0.7 %copy-start.3 = (bf16[17]{0:T(256)(128)(2,1)S(1)}, bf16[17]{0:T(256)(128)(2,1)}, u32[]{:S(2)}) copy-start(bf16[17]{0:T(256)(128)(2,1)} %param.7) | copy-start | bytes 106
  1.3 1.2 %copy-start = (bf16[16,256,128]{2,1,0:T(8,128)(2,1)S(1)}, bf16[16,256,128]{2,1,0:T(8,128)(2,1)}, u32[]{:S(2)}) copy-start(bf16[16,256,128]{2,1,0:T(8,128)(2,1)} %x_ref.3) | copy-start | bytes 3145732
  2.5 8.6 %copy-start.4 = (bf16[17]{0:T(256)(128)(2,1)S(1)}, bf16[17]{0:T(256)(128)(2,1)}, u32[]{:S(2)}) copy-start(bf16[17]{0:T(256)(128)(2,1)} %param.6) | copy-start | bytes 106
  2.5 13.2 %copy-start.1 = (bf16[16,256,128]{2,1,0:T(8,128)(2,1)S(1)}, bf16[16,256,128]{2,1,0:T(8,128)(2,1)}, u32[]{:S(2)}) copy-start(bf16[16,256,128]{2,1,0:T(8,128)(2,1)} %x_ref.3) | copy-start | bytes 3145732
  4.5 11.2 %copy-start.2 = (bf16[2,1,32,16]{2,3,1,0:T(8,128)(2,1)S(1)}, bf16[2,1,32,16]{2,3,1,0:T(8,128)(2,1)}, u32[]{:S(2)}) copy-start(bf16[2,1,32,16]{2,3,1,0:T(8,128)(2,1)} %param.5) | copy-start | bytes 6148
  4.5 19.4 %collective-permute-start.5 = (bf16[68,16,128]{2,1,0:T(8,128)(2,1)S(1)}, bf16[68,16,128]{2,1,0:T(8,128)(2,1)S(1)}, u32[]{:S(2)}, u32[]{:S(2)}) collective-permute-start(bf16[68,16,128]{2,1,0:T(8,128)(2,1)S(1)} %get-tuple-element.35), channel_id=1, source_target_pairs={{0,4},{1,5},{2,6},{3,7},{4,0},{5,1},{6,2},{7,3},{8,12},{9,13},{10,... | collective-permute-start | bytes 835592 | tf_op jit(solution)/shard_map/ppermute | solution.py:425
  7.2 5.1 %collective-permute-start = (bf16[16,8,256]{2,1,0:T(8,128)(2,1)S(1)}, bf16[16,8,256]{2,1,0:T(8,128)(2,1)S(1)}, u32[]{:S(2)}, u32[]{:S(2)}) collective-permute-start(bf16[16,8,256]{2,1,0:T(8,128)(2,1)S(1)} %get-tuple-element.26), channel_id=1, source_target_pairs={{0,8},{8,0},{16,24},{24,16},{1,9},{9,1},{17,25},{25,17},{2,10},{10... | collective-permute-start | bytes 196616 | tf_op jit(solution)/shard_map/ppermute | solution.py:448
  8.7 7.0 %collective-permute-start.1 = (bf16[16,8,256]{2,1,0:T(8,128)(2,1)S(1)}, bf16[16,8,256]{2,1,0:T(8,128)(2,1)S(1)}, u32[]{:S(2)}, u32[]{:S(2)}) collective-permute-start(bf16[16,8,256]{2,1,0:T(8,128)(2,1)S(1)} %get-tuple-element.27), channel_id=1, source_target_pairs={{8,16},{16,8},{9,17},{17,9},{10,18},{18,10},{11,19},{19,11},{12,20... | collective-permute-start | bytes 196616 | tf_op jit(solution)/shard_map/ppermute | solution.py:450
  18.6 5.4 %collective-permute-start.2 = (bf16[35,16,128]{2,1,0:T(8,128)(2,1)S(1)}, bf16[35,16,128]{2,1,0:T(8,128)(2,1)S(1)}, u32[]{:S(2)}, u32[]{:S(2)}) collective-permute-start(bf16[35,16,128]{2,1,0:T(8,128)(2,1)S(1)} %get-tuple-element.32), channel_id=1, source_target_pairs={{0,1},{1,0},{2,3},{3,2},{4,5},{5,4},{6,7},{7,6},{8,9},{9,8},{10,11... | collective-permute-start | bytes 430088 | tf_op jit(solution)/shard_map/ppermute | solution.py:425
  18.7 8.6 %collective-permute-start.3 = (bf16[35,16,128]{2,1,0:T(8,128)(2,1)S(1)}, bf16[35,16,128]{2,1,0:T(8,128)(2,1)S(1)}, u32[]{:S(2)}, u32[]{:S(2)}) collective-permute-start(bf16[35,16,128]{2,1,0:T(8,128)(2,1)S(1)} %get-tuple-element.33), channel_id=1, source_target_pairs={{0,2},{1,3},{2,4},{3,5},{4,6},{5,7},{6,0},{7,1},{8,10},{9,11},{10,... | collective-permute-start | bytes 430088 | tf_op jit(solution)/shard_map/ppermute | solution.py:425
  20.3 9.1 %collective-permute-start.4 = (bf16[35,16,128]{2,1,0:T(8,128)(2,1)S(1)}, bf16[35,16,128]{2,1,0:T(8,128)(2,1)S(1)}, u32[]{:S(2)}, u32[]{:S(2)}) collective-permute-start(bf16[35,16,128]{2,1,0:T(8,128)(2,1)S(1)} %get-tuple-element.34), channel_id=1, source_target_pairs={{0,3},{1,2},{2,5},{3,4},{4,7},{5,6},{6,1},{7,0},{8,11},{9,10},{10,... | collective-permute-start | bytes 430088 | tf_op jit(solution)/shard_map/ppermute | solution.py:425
  20.4 17.5 %collective-permute-start.7 = (bf16[35,16,128]{2,1,0:T(8,128)(2,1)S(1)}, bf16[35,16,128]{2,1,0:T(8,128)(2,1)S(1)}, u32[]{:S(2)}, u32[]{:S(2)}) collective-permute-start(bf16[35,16,128]{2,1,0:T(8,128)(2,1)S(1)} %get-tuple-element.39), channel_id=1, source_target_pairs={{0,6},{1,7},{2,0},{3,1},{4,2},{5,3},{6,4},{7,5},{8,14},{9,15},{10,... | collective-permute-start | bytes 430088 | tf_op jit(solution)/shard_map/ppermute | solution.py:425
  23.9 14.0 %collective-permute-start.8 = (bf16[35,16,128]{2,1,0:T(8,128)(2,1)S(1)}, bf16[35,16,128]{2,1,0:T(8,128)(2,1)S(1)}, u32[]{:S(2)}, u32[]{:S(2)}) collective-permute-start(bf16[35,16,128]{2,1,0:T(8,128)(2,1)S(1)} %get-tuple-element.40), channel_id=1, source_target_pairs={{0,7},{1,6},{2,1},{3,0},{4,3},{5,2},{6,5},{7,4},{8,15},{9,14},{10,... | collective-permute-start | bytes 430088 | tf_op jit(solution)/shard_map/ppermute | solution.py:425
  24.0 5.4 %collective-permute-start.6 = (bf16[34,16,128]{2,1,0:T(8,128)(2,1)S(1)}, bf16[34,16,128]{2,1,0:T(8,128)(2,1)S(1)}, u32[]{:S(2)}, u32[]{:S(2)}) collective-permute-start(bf16[34,16,128]{2,1,0:T(8,128)(2,1)S(1)} %slice.4), channel_id=1, source_target_pairs={{0,1},{1,0},{2,3},{3,2},{4,5},{5,4},{6,7},{7,6},{8,9},{9,8},{10,11... | collective-permute-start | bytes 417800 | tf_op jit(solution)/shard_map/ppermute | solution.py:422
  27.2 10.2 %collective-permute-start.9 = (bf16[6,16,128]{2,1,0:T(8,128)(2,1)S(1)}, bf16[6,16,128]{2,1,0:T(8,128)(2,1)S(1)}, u32[]{:S(2)}, u32[]{:S(2)}) collective-permute-start(bf16[6,16,128]{2,1,0:T(8,128)(2,1)S(1)} %get-tuple-element.41), channel_id=1, source_target_pairs={{0,4},{1,5},{2,6},{3,7},{4,0},{5,1},{6,2},{7,3},{8,12},{9,13},{10,... | collective-permute-start | bytes 73736 | tf_op jit(solution)/shard_map/ppermute | solution.py:425
  29.4 8.5 %collective-permute-start.10 = (bf16[6,16,128]{2,1,0:T(8,128)(2,1)S(1)}, bf16[6,16,128]{2,1,0:T(8,128)(2,1)S(1)}, u32[]{:S(2)}, u32[]{:S(2)}) collective-permute-start(bf16[6,16,128]{2,1,0:T(8,128)(2,1)S(1)} %get-tuple-element.42), channel_id=1, source_target_pairs={{0,5},{1,4},{2,7},{3,6},{4,1},{5,0},{6,3},{7,2},{8,13},{9,12},{10,... | collective-permute-start | bytes 73736 | tf_op jit(solution)/shard_map/ppermute | solution.py:425
  39.1 4.2 %collective-permute-start.13 = (f32[128,128]{1,0:T(8,128)S(1)}, f32[128,128]{1,0:T(8,128)S(1)}, u32[]{:S(2)}, u32[]{:S(2)}) collective-permute-start(f32[128,128]{1,0:T(8,128)S(1)} %get-tuple-element.46.refs_0_), channel_id=1, source_target_pairs={{0,3},{1,2},{2,1},{3,0},{4,7},{5,6},{6,5},{7,4},{8,11},{9,10},{10,... | collective-permute-start | bytes 196616 | tf_op jit(solution)/shard_map/ppermute | solution.py:422
  39.2 5.8 %collective-permute-start.12 = (f32[128,128]{1,0:T(8,128)S(1)}, f32[128,128]{1,0:T(8,128)S(1)}, u32[]{:S(2)}, u32[]{:S(2)}) collective-permute-start(f32[128,128]{1,0:T(8,128)S(1)} %get-tuple-element.46.refs_0_), channel_id=1, source_target_pairs={{0,2},{1,3},{2,0},{3,1},{4,6},{5,7},{6,4},{7,5},{8,10},{9,11},{10,... | collective-permute-start | bytes 196616 | tf_op jit(solution)/shard_map/ppermute | solution.py:422
  40.9 4.1 %collective-permute-start.11 = (f32[128,128]{1,0:T(8,128)S(1)}, f32[128,128]{1,0:T(8,128)S(1)}, u32[]{:S(2)}, u32[]{:S(2)}) collective-permute-start(f32[128,128]{1,0:T(8,128)S(1)} %get-tuple-element.46.refs_0_), channel_id=1, source_target_pairs={{0,1},{1,0},{2,3},{3,2},{4,5},{5,4},{6,7},{7,6},{8,9},{9,8},{10,11... | collective-permute-start | bytes 196616 | tf_op jit(solution)/shard_map/ppermute | solution.py:422
  47.4 4.7 %collective-permute-start.14 = (f32[2,16,32]{2,1,0:T(8,128)S(1)}, f32[2,16,32]{2,1,0:T(8,128)S(1)}, u32[]{:S(2)}, u32[]{:S(2)}) collective-permute-start(f32[2,16,32]{2,1,0:T(8,128)S(1)} %get-tuple-element.49), channel_id=1, source_target_pairs={{0,4},{1,5},{2,6},{3,7},{4,0},{5,1},{6,2},{7,3},{8,12},{9,13},{10,... | collective-permute-start | bytes 12296 | tf_op jit(solution)/shard_map/ppermute | solution.py:422

commit v4 on v3

--- a/solution.py
+++ b/solution.py
@@ -154,7 +154,7 @@
 
 
 def early_kernel(axis, side, count, x_ref, taps_hbm, *rest):
-    out_ref, a_ref, b_ref, *scratch = rest
+    outs, (a_ref, b_ref), scratch = rest[:2], rest[2:4], rest[4:]
     taps_ref, centre_scr, rows_scr, anchor_scr, sem = scratch
     frames, rows, cols = x_ref.shape
     part, span = anchor_scr.shape[0], centre_scr.shape[0]
@@ -177,8 +177,8 @@
         return x_ref[f, pl.ds(first, span), :].astype(F32)
 
     filter_rows(x_of, None, bx, None, dy, frames, inner, *scratch)
-    for h in range(2):
-        put_block(out_ref, h * (share + share // frames), (me + h) % 2, share, rows_scr, anchor_scr)
+    for h, out_ref in enumerate(outs):
+        put_block(out_ref, 0, (me + h) % 2, share, rows_scr, anchor_scr)
 
     row = lax.broadcasted_iota(jnp.int32, (2 * radius, cols), 0)
     col = lax.broadcasted_iota(jnp.int32, (2 * radius, cols), 1)
@@ -191,11 +191,24 @@
         b_ref[f] = both[radius:]
 
 
-def bands_kernel(side, space_ref, time_ref, bx_ref, bh_ref, dy_ref, lhs_ref):
-    rows, cols = dy_ref.shape[0], bx_ref.shape[0]
+def prepare_kernel(side, x_ref, space_ref, time_ref, om_in, bh_ref, dy_ref, lhs_ref, om_ref, *rest):
+    anchor_ref, block_ref, smooth_ref = rest
+    om_ref[...] = om_in[...]
+    frames, rows, cols = x_ref.shape
     space, time = space_ref[...].astype(F32), time_ref[...].astype(F32)
     radius = (space.shape[1] - 1) // 2
-    bx_ref[...] = toeplitz(space, cols, cols, radius, -1).astype(BF16)
+    bx = toeplitz(space, cols, cols, radius, -1).astype(BF16)
+    total = jnp.zeros((rows, cols), F32)
+    for f in range(frames):
+        total = total + x_ref[f].astype(F32)
+    anchor = (total * (1.0 / frames)).astype(BF16)
+    anchor32 = anchor.astype(F32)
+    anchor_ref[...] = anchor32
+    smooth_ref[frames] = contract(anchor, bx, 1, 0)
+    for f in range(frames):
+        block = (x_ref[f].astype(F32) - anchor32).astype(BF16)
+        block_ref[f] = block
+        smooth_ref[f] = contract(block, bx, 1, 0)
     left = toeplitz(space, radius, cols, 0, -1)
     right = toeplitz(space, radius, cols, radius + cols, -1)
     odd = lax.axis_index(side) % 2 == 1
@@ -217,21 +230,40 @@
     lhs_ref[:, all_frames:] = jnp.concatenate([high.astype(F32), low.astype(F32)], 1).astype(BF16)
 
 
-def spatial_kernel(axis, x_ref, a_ref, b_ref, bx_ref, bh_ref, dy_ref, om_ref, *rest):
+def spatial_kernel(axis, a_ref, b_ref, bh_ref, dy_ref, om_ref, *rest):
+    (anchor_ref, block_ref, smooth_ref), rest = rest[:3], rest[3:]
     outs, edge_refs, (rows_scr, anchor_scr) = rest[:-4], rest[-4:-2], rest[-2:]
-    frames, rows, cols = x_ref.shape
+    frames, rows, cols = block_ref.shape
     radius = a_ref.shape[1]
     share = (outs[0].shape[0] - 1) * frames // (frames + 1)
     count = rows // share
     me = lax.axis_index(axis)
+    bh, dy = bh_ref[...], dy_ref[...]
 
     def halo(f):
         return jnp.concatenate([a_ref[f].astype(F32), b_ref[f].astype(F32)], axis=0)
 
-    scratch = (None, rows_scr, anchor_scr)
-    filter_rows(
-        lambda f: x_ref[f].astype(F32), halo, bx_ref[...], bh_ref[...], dy_ref[...], frames, 0, *scratch
-    )
+    def across(f, edge):
+        return smooth_ref[f] + contract(edge, bh, 0, 0)
+
+    total = halo(0)
+    for f in range(1, frames):
+        total = total + halo(f)
+    edge_anchor = (total * (1.0 / frames)).astype(BF16)
+    edge32 = edge_anchor.astype(F32)
+    high, low = split(across(frames, edge_anchor))
+    both = contract(dy, jnp.concatenate([high, low], axis=1), 1, 0)
+    anchor_s = anchor_ref[...] - both[:, :cols] - both[:, cols:]
+    anchor_out = anchor_s.astype(BF16).astype(F32)
+    anchor_scr[...] = anchor_out
+    left_over = anchor_s - anchor_out
+    for p in range(frames // 2):
+        pair = (2 * p, 2 * p + 1)
+        smooths = [across(f, (halo(f) - edge32).astype(BF16)).astype(BF16) for f in pair]
+        both = contract(dy, jnp.concatenate(smooths, axis=1), 1, 0)
+        for i, f in enumerate(pair):
+            value = block_ref[f].astype(F32) - both[:, i * cols : (i + 1) * cols] + left_over
+            rows_scr[pl.ds(f, rows, stride=frames), :] = value
     early = count // 4
     for (shift, flips), out in zip(message_list(count), outs):
         for i, flip in enumerate(flips):
@@ -339,7 +371,7 @@
     ids = lax.broadcasted_iota(jnp.int32, (size, 128), 0)
     work = [jnp.concatenate([gram, jnp.zeros((size, 128 - size), F32)], axis=1), *others]
     scale = jnp.zeros((size, 128), F32)
-    panel = 8
+    panel = 16
     for start in range(0, size, panel):
         cols = [
             jnp.broadcast_to(work[0][:, j : j + 1], (size, 128)) for j in range(start, start + panel)
@@ -427,10 +459,10 @@
     space_row, time_row = space_taps[None], time_taps[None]
     part = 2 * share
     span = part + 32
-    main, side_a, side_b = call(
+    *mains, side_a, side_b = call(
         functools.partial(early_kernel, "tm", "tile", count),
         [
-            shape((2 * slots, frames, cols), BF16),
+            *([shape((slots, frames, cols), BF16)] * 2),
             *([shape((frames, radius, rows), BF16)] * 2),
         ],
         [movie, space_row],
@@ -443,22 +475,25 @@
         ],
         [pltpu.VMEM, pltpu.HBM],
     )
-    main = send(main, early, 0)
+    mains = [send(value, early, h) for h, value in enumerate(mains)]
     pairs = [(i, i ^ 1) for i in range(tiles)]
     side_a = lax.ppermute(side_a, "tile", pairs)
     pairs = [(i, i + 1) for i in range(1, tiles - 1, 2)]
     side_b = lax.ppermute(side_b, "tile", pairs + [(j, i) for i, j in pairs])
-    bx, bh, dy, lhs = call(
-        functools.partial(bands_kernel, "tile"),
+    om = jnp.transpose(omega[:, 0], (0, 2, 1))
+    bh, dy, lhs, om, *prepared = call(
+        functools.partial(prepare_kernel, "tile"),
         [
-            shape((cols, cols), BF16),
             shape((2 * radius, cols), BF16),
             shape((rows, rows), BF16),
             shape((all_frames, all_frames + 2 * count), BF16),
+            shape(om.shape, om.dtype),
+            shape((rows, cols), F32),
+            shape(movie.shape, BF16),
+            shape((frames + 1, rows, cols), F32),
         ],
-        [space_row, time_row],
-    )
-    om = jnp.transpose(omega[:, 0], (0, 2, 1))
+        [movie, space_row, time_row, om],
+    )
     listed = message_list(count)
     *parts, edges, edges_other = call(
         functools.partial(spatial_kernel, "tm"),
@@ -466,17 +501,18 @@
             *[shape((len(flips) * (slots + 1), frames, cols), BF16) for _, flips in listed],
             *([shape((share // packed + 2, frames, cols), BF16)] * 2),
         ],
-        [movie, side_a, side_b, bx, bh, dy, om],
+        [side_a, side_b, bh, dy, om, *prepared],
         [pltpu.VMEM((rows * frames, cols), F32), pltpu.VMEM((rows, cols), F32)],
     )
-    edges, edges_other = send(edges, early, 0), send(edges_other, early, 1)
-    came = [
-        send(value, shift, flips[0] if len(flips) == 1 else 0)
-        for (shift, flips), value in zip(listed[2:], parts[2:])
+    def after(value, other):
+        return lax.optimization_barrier((value, other))[0]
+
+    parts[-2:] = [after(value, other) for value, other in zip(parts[-2:], mains)]
+    blocks = [parts[0]] + [
+        send(value, shift, flip) for (shift, (flip,)), value in zip(listed[1:], parts[1:])
     ]
-    blocks = [parts[0], send(parts[1], 0, 1)]
-    for (_, flips), value in zip(listed[2:], came):
-        blocks += [value] if len(flips) == 1 else [value, swap(value[slots + 1 :], 1)]
+    edges = send(after(edges, blocks[1]), early, 0)
+    edges_other = send(after(edges_other, blocks[1]), early, 1)
     places = [(shift, flip) for shift, flips in listed for flip in flips]
     known = call(
         functools.partial(gather_kernel, "tm", places[:-2]),
@@ -485,7 +521,7 @@
             shape((share * count, cols), F32),
             shape((count, frames, cols), BF16),
         ],
-        [*blocks[:-2], main, swap(main[slots:], 1)],
+        [*blocks[:-2], *mains],
     )
     _, _, om_all, matrix, gram = call(
         functools.partial(temporal_kernel, "tm", radius, places[-2:]),
@@ -497,7 +533,8 @@
         [*known, *blocks[-2:], edges, edges_other, lhs],
         aliases={0: 0, 1: 1, 2: 2},
     )
-    grams = [gram] + [swap(gram, k) for k in range(1, group)]
+    chips = [gram] + [swap(gram, k) for k in range(2, group, 2)]
+    grams = chips + [swap(value, 1) for value in chips]
     mix, coef_own, coef_send = call(
         functools.partial(factor_kernel, "tm", count, ranks, pixels),
         [shape((ranks, all_frames), F32), *([shape((TY, frames, ranks), F32)] * 2)],

time: 53.2 us -> 51.3 us (0.964)
  Pallas kernels: 11.1 us -> 9.75 us
  local copies, waits for them, and re-layouts: 1.9 us -> 3.22 us
  starting transfers between devices: 14.4 us -> 13.2 us
  waiting for transfers between devices: 23.9 us -> 23.3 us
    ppermute x5 -> x4, starting transfers between devices: 2.48 us -> 0.32 us  [swap(): return lax.ppermute(value, 'tm', [(i, i ^ k) for i in range(count)])]
    ppermute x1, waiting for transfers between devices: 3.44 us -> 1.91 us  [local(): side_b = lax.ppermute(side_b, 'tile', pairs + [(j, i) for i, j in pairs])]
    pallas_call x7, Pallas kernels: 11.1 us -> 9.75 us  [call(): pl.pallas_call(kernel, out_shape=outs, in_specs=[pl.BlockSpec(memory_spac...]
    ppermute x5 -> x4, waiting for transfers between devices: 7.27 us -> 8.64 us  [swap(): return lax.ppermute(value, 'tm', [(i, i ^ k) for i in range(count)])]
    unnamed x10 -> x8, local copies, waits for them, and re-layouts: 1.89 us -> 3.22 us
    ppermute x8 -> x9, starting transfers between devices: 8.07 us -> 9.04 us  [send(): lax.ppermute(value, 'tm', [(i, device_at(i, count, shift, flip)) for i in...]
    ppermute x8 -> x9, waiting for transfers between devices: 13.2 us -> 12.8 us  [send(): lax.ppermute(value, 'tm', [(i, device_at(i, count, shift, flip)) for i in...]
  transfers between devices with their start and end apart: 15 -> 15, of which waited for: 8 -> 8; matrix products, arithmetic and copies ran while one was open for 0% -> 0% of each run, Pallas kernels for 10% -> 9%
where the time goes in v4:
time: 51.3 us; the launch traced here: 50.9 us
  waiting for transfers between devices  23.3 us (45%)
  starting transfers between devices  13.2 us (26%)
  Pallas kernels  9.75 us (19%)
  local copies, waits for them, and re-layouts  3.22 us (6%)
  between operations  0.73 us (1%)
  other arithmetic  0.61 us (1%)
    ppermute x9, waiting for transfers between devices, send(): lax.ppermute(value, 'tm', [(i, device_at(i, count, shift, flip)) for i in...  12.8 us
    pallas_call x7, Pallas kernels, call(): pl.pallas_call(kernel, out_shape=outs, in_specs=[pl.BlockSpec(memory_spac...  9.75 us
    ppermute x9, starting transfers between devices, send(): lax.ppermute(value, 'tm', [(i, device_at(i, count, shift, flip)) for i in...  9.04 us
    ppermute x4, waiting for transfers between devices, swap(): return lax.ppermute(value, 'tm', [(i, i ^ k) for i in range(count)])  8.64 us
    unnamed x8, local copies, waits for them, and re-layouts  3.22 us
    ppermute x1, starting transfers between devices, local(): side_b = lax.ppermute(side_b, 'tile', pairs + [(j, i) for i, j in pairs])  2.37 us
    ppermute x1, waiting for transfers between devices, local(): side_b = lax.ppermute(side_b, 'tile', pairs + [(j, i) for i, j in pairs])  1.91 us
    ppermute x1, starting transfers between devices, local(): side_a = lax.ppermute(side_a, 'tile', pairs)  1.49 us
  transfers between devices with their start and end apart: 15, of which 8 were waited for; matrix products, arithmetic and copies ran while one was open for 0% of the time, Pallas kernels for 9%

profile of v4, /device:TPU:4, one launch (start us, length us, event | category | flops | bytes accessed | tf_op | source)
XLA Modules:
  0.0 50.9 jit_solution(5161157885857180854)
XLA Ops:
  0.6 0.0 copy-start
  0.6 1.2 %copy-done = bf16[16,256,128]{2,1,0:T(8,128)(2,1)S(1)} copy-done((bf16[16,256,128]{2,1,0:T(8,128)(2,1)S(1)}, bf16[16,256,128]{2,1,0:T(8,128)(2,1)}, u32[]{:S(2)}) %copy-start) | copy-done | bytes 1048600
  1.9 0.0 copy-start.2
  1.9 0.7 %copy-done.2 = bf16[17]{0:T(256)(128)(2,1)S(1)} copy-done((bf16[17]{0:T(256)(128)(2,1)S(1)}, bf16[17]{0:T(256)(128)(2,1)}, u32[]{:S(2)}) %copy-start.2) | copy-done | bytes 58
  2.5 2.0 %shard_map.59 = (bf16[34,16,128]{2,1,0:T(8,128)(2,1)S(1)}, bf16[34,16,128]{2,1,0:T(8,128)(2,1)S(1)}, bf16[16,8,256]{2,1,0:T(8,128)(2,1)S(1)}, bf16[16,8,256]{2,1,0:T(8,128)(2,1)S(1)}) custom-call(bf16[16,256,128]{2,1,0:T(8,128)(2,1)S(1)} %copy-done, bf16[1,17]{1,0:T(2,128)(2,1)S(1)} %bitcast.13), custom_call_target="tpu_custom_call" | custom-call | tf_op jit(solution)/shard_map/pallas_call | solution.py:18
  4.5 2.7 %collective-permute-start.5 = (bf16[34,16,128]{2,1,0:T(8,128)(2,1)S(1)}, bf16[34,16,128]{2,1,0:T(8,128)(2,1)S(1)}, u32[]{:S(2)}, u32[]{:S(2)}) collective-permute-start(bf16[34,16,128]{2,1,0:T(8,128)(2,1)S(1)} %get-tuple-element.46), channel_id=1, source_target_pairs={{0,4},{1,5},{2,6},{3,7},{4,0},{5,1},{6,2},{7,3},{8,12},{9,13},{10,... | collective-permute-start | bytes 417800 | tf_op jit(solution)/shard_map/ppermute | solution.py:457
  7.2 0.0 collective-permute-start.6
  7.2 1.5 %collective-permute-start = (bf16[16,8,256]{2,1,0:T(8,128)(2,1)S(1)}, bf16[16,8,256]{2,1,0:T(8,128)(2,1)S(1)}, u32[]{:S(2)}, u32[]{:S(2)}) collective-permute-start(bf16[16,8,256]{2,1,0:T(8,128)(2,1)S(1)} %get-tuple-element.34), channel_id=1, source_target_pairs={{0,8},{8,0},{16,24},{24,16},{1,9},{9,1},{17,25},{25,17},{2,10},{10... | collective-permute-start | bytes 196616 | tf_op jit(solution)/shard_map/ppermute | solution.py:480
  8.7 2.4 %collective-permute-start.1 = (bf16[16,8,256]{2,1,0:T(8,128)(2,1)S(1)}, bf16[16,8,256]{2,1,0:T(8,128)(2,1)S(1)}, u32[]{:S(2)}, u32[]{:S(2)}) collective-permute-start(bf16[16,8,256]{2,1,0:T(8,128)(2,1)S(1)} %get-tuple-element.35), channel_id=1, source_target_pairs={{8,16},{16,8},{9,17},{17,9},{10,18},{18,10},{11,19},{19,11},{12,20... | collective-permute-start | bytes 196616 | tf_op jit(solution)/shard_map/ppermute | solution.py:482
  11.1 0.0 copy-start.1
  11.1 0.7 %copy-done.1 = bf16[2,1,32,16]{2,3,1,0:T(8,128)(2,1)S(1)} copy-done((bf16[2,1,32,16]{2,3,1,0:T(8,128)(2,1)S(1)}, bf16[2,1,32,16]{2,3,1,0:T(8,128)(2,1)}, u32[]{:S(2)}) %copy-start.1) | copy-done | bytes 2072
  11.8 0.0 copy-start.3
  11.8 0.7 %copy-done.3 = bf16[17]{0:T(256)(128)(2,1)S(1)} copy-done((bf16[17]{0:T(256)(128)(2,1)S(1)}, bf16[17]{0:T(256)(128)(2,1)}, u32[]{:S(2)}) %copy-start.3) | copy-done | bytes 58
  12.4 1.4 %shard_map.60 = (bf16[16,128]{1,0:T(8,128)(2,1)S(1)}, bf16[256,256]{1,0:T(8,128)(2,1)S(1)}, bf16[128,144]{1,0:T(8,128)(2,1)S(1)}, bf16[2,16,32]{2,1,0:T(8,128)(2...) custom-call(bf16[16,256,128]{2,1,0:T(8,128)(2,1)S(1)} %copy-done, ...), custom_call_target="tpu_custom_call" | custom-call | tf_op jit(solution)/shard_map/pallas_call | solution.py:18
  13.8 0.0 collective-permute-done.a_ref
  13.8 1.9 %collective-permute-done.1.b_ref = bf16[16,8,256]{2,1,0:T(8,128)(2,1)S(1)} collective-permute-done((bf16[16,8,256]{2,1,0:T(8,128)(2,1)S(1)}, bf16[16,8,256]{2,1,0:T(8,128)(2,1)S(1)}, u32[]{:S(2)}, u32[]{:S(2)}) %collective-permute-start.1) | collective-permute-done | bytes 65568 | tf_op jit(solution)/shard_map/ppermute | solution.py:482
  15.7 1.6 %shard_map.61 = (bf16[35,16,128]{2,1,0:T(8,128)(2,1)S(1)}, bf16[35,16,128]{2,1,0:T(8,128)(2,1)S(1)}, bf16[35,16,128]{2,1,0:T(8,128)(2,1)S(1)}, bf16[35,16,128]{2...) custom-call(bf16[16,8,256]{2,1,0:T(8,128)(2,1)S(1)} %collective-perm, ...), custom_call_target="tpu_custom_call" | custom-call | tf_op jit(solution)/shard_map/pallas_call | solution.py:18
  17.4 0.1 collective-permute-start.2
  17.4 1.6 %collective-permute-start.3 = (bf16[35,16,128]{2,1,0:T(8,128)(2,1)S(1)}, bf16[35,16,128]{2,1,0:T(8,128)(2,1)S(1)}, u32[]{:S(2)}, u32[]{:S(2)}) collective-permute-start(bf16[35,16,128]{2,1,0:T(8,128)(2,1)S(1)} %get-tuple-element.44), channel_id=1, source_target_pairs={{0,2},{1,3},{2,4},{3,5},{4,6},{5,7},{6,0},{7,1},{8,10},{9,11},{10,... | collective-permute-start | bytes 430088 | tf_op jit(solution)/shard_map/ppermute | solution.py:457
  19.1 1.2 %collective-permute-start.4 = (bf16[35,16,128]{2,1,0:T(8,128)(2,1)S(1)}, bf16[35,16,128]{2,1,0:T(8,128)(2,1)S(1)}, u32[]{:S(2)}, u32[]{:S(2)}) collective-permute-start(bf16[35,16,128]{2,1,0:T(8,128)(2,1)S(1)} %get-tuple-element.45), channel_id=1, source_target_pairs={{0,3},{1,2},{2,5},{3,4},{4,7},{5,6},{6,1},{7,0},{8,11},{9,10},{10,... | collective-permute-start | bytes 430088 | tf_op jit(solution)/shard_map/ppermute | solution.py:457
  20.3 0.0 collective-permute-done.5.refs_4_
  20.3 0.0 collective-permute-done.6.refs_5_
  20.3 2.6 %collective-permute-start.8 = (bf16[35,16,128]{2,1,0:T(8,128)(2,1)S(1)}, bf16[35,16,128]{2,1,0:T(8,128)(2,1)S(1)}, u32[]{:S(2)}, u32[]{:S(2)}) collective-permute-start(bf16[35,16,128]{2,1,0:T(8,128)(2,1)S(1)} %get-tuple-element.54), channel_id=1, source_target_pairs={{0,7},{1,6},{2,1},{3,0},{4,3},{5,2},{6,5},{7,4},{8,15},{9,14},{10,... | collective-permute-start | bytes 430088 | tf_op jit(solution)/shard_map/ppermute | solution.py:457
  23.0 0.3 collective-permute-start.7
  23.3 0.0 collective-permute-done.2.refs_1_
  23.3 0.5 collective-permute-start.9
  23.8 2.2 %collective-permute-done.3.refs_2_ = bf16[35,16,128]{2,1,0:T(8,128)(2,1)S(1)} collective-permute-done((bf16[35,16,128]{2,1,0:T(8,128)(2,1)S(1)}, bf16[35,16,128]{2,1,0:T(8,128)(2,1)S(1)}, u32[]{:S(2)}, u32[]{:S(2)}) %collective-permute-start.3) | collective-permute-done | bytes 143392 | tf_op jit(solution)/shard_map/ppermute | solution.py:457
  26.0 0.0 collective-permute-start.10
  26.0 2.2 %collective-permute-done.4.refs_3_ = bf16[35,16,128]{2,1,0:T(8,128)(2,1)S(1)} collective-permute-done((bf16[35,16,128]{2,1,0:T(8,128)(2,1)S(1)}, bf16[35,16,128]{2,1,0:T(8,128)(2,1)S(1)}, u32[]{:S(2)}, u32[]{:S(2)}) %collective-permute-start.4) | collective-permute-done | bytes 143392 | tf_op jit(solution)/shard_map/ppermute | solution.py:457
  28.2 0.1 shard_map.62
  28.3 7.9 %collective-permute-done.9.refs_5_ = bf16[6,16,128]{2,1,0:T(8,128)(2,1)S(1)} collective-permute-done((bf16[6,16,128]{2,1,0:T(8,128)(2,1)S(1)}, bf16[6,16,128]{2,1,0:T(8,128)(2,1)S(1)}, u32[]{:S(2)}, u32[]{:S(2)}) %collective-permute-start.9) | collective-permute-done | bytes 24608 | tf_op jit(solution)/shard_map/ppermute | solution.py:457
  36.2 0.4 collective-permute-done.10.refs_6_
  36.7 0.0 collective-permute-done.8.refs_4_
  36.7 0.0 collective-permute-done.7.refs_3_
  36.7 1.2 %shard_map.63 = (bf16[32,8,16,128]{3,2,1,0:T(8,128)(2,1)S(1)}, f32[256,128]{1,0:T(8,128)S(1)}, bf16[8,16,128]{2,1,0:T(8,128)(2,1)S(1)}, bf16[32,128,128]{2,1,0:T(8,128)(2,1)S(1)}, f32[128,128]{1,0:T(8,128)S(1)}) custom-call(bf16[32,8,16,128]{3,2,1,0:T(8,128)(2,1)S(1)} %get-tuple-element.48.refs_0_, ...), custom_call_target="tpu_custom_call", output_to_operand_aliasing={{0}: (0, {}), {1}: (1, {}), {2}: (2, {})} | custom-call | tf_op jit(solution)/shard_map/pallas_call | solution.py:18
  37.8 0.1 collective-permute-start.11
  37.9 0.2 collective-permute-start.12
  38.1 4.1 %collective-permute-done.11.refs_1_ = f32[128,128]{1,0:T(8,128)S(1)} collective-permute-done((f32[128,128]{1,0:T(8,128)S(1)}, f32[128,128]{1,0:T(8,128)S(1)}, u32[]{:S(2)}, u32[]{:S(2)}) %collective-permute-start.11) | collective-permute-done | bytes 65568 | tf_op jit(solution)/shard_map/ppermute | solution.py:454
  42.2 0.0 collective-permute-start.13
  42.2 0.0 collective-permute-done.12.refs_2_
  42.2 1.2 %collective-permute-done.13.refs_3_ = f32[128,128]{1,0:T(8,128)S(1)} collective-permute-done((f32[128,128]{1,0:T(8,128)S(1)}, f32[128,128]{1,0:T(8,128)S(1)}, u32[]{:S(2)}, u32[]{:S(2)}) %collective-permute-start.13) | collective-permute-done | bytes 65568 | tf_op jit(solution)/shard_map/ppermute | solution.py:454
  43.4 2.2 %shard_map.64 = (f32[32,128]{1,0:T(8,128)S(1)}, f32[2,16,32]{2,1,0:T(8,128)S(1)}, f32[2,16,32]{2,1,0:T(8,128)S(1)}) custom-call(bf16[8,16,128]{2,1,0:T(8,128)(2,1)S(1)} %get-tuple-element.61.om_ref, f32[128,128]{1,0:T(8,128)S(1)} %get-tuple-element.62.refs_0_, f32[128,128]{1,0:T(8,128)S(1)} %collective-permute-done.11.refs_1_, ...), custom_call_target="tpu_custom_call" | custom-call | tf_op jit(solution)/shard_map/pallas_call | solution.py:18
  45.6 0.1 collective-permute-start.14
  45.7 1.3 %shard_map.65 = f32[1024,128]{1,0:T(8,128)} custom-call(bf16[32,128,128]{2,1,0:T(8,128)(2,1)S(1)} %get-tuple-element.60.m_ref, f32[32,128]{1,0:T(8,128)S(1)} %get-tuple-element.63.mix_ref), custom_call_target="tpu_custom_call" | custom-call | tf_op jit(solution)/shard_map/pallas_call | solution.py:18
  46.9 3.3 %collective-permute-done.14 = f32[2,16,32]{2,1,0:T(8,128)S(1)} collective-permute-done((f32[2,16,32]{2,1,0:T(8,128)S(1)}, f32[2,16,32]{2,1,0:T(8,128)S(1)}, u32[]{:S(2)}, u32[]{:S(2)}) %collective-permute-start.14) | collective-permute-done | bytes 4128 | tf_op jit(solution)/shard_map/ppermute | solution.py:454
  50.2 0.6 %add_bitcast_fusion = f32[2,1,32,16]{2,3,1,0:T(8,128)} fusion(f32[2,16,32]{2,1,0:T(8,128)S(1)} %get-tuple-element.64, f32[2,16,32]{2,1,0:T(8,128)S(1)} %collective-permute-done.14), kind=kLoop, calls=%fused_computation | loop fusion | flops 1024 | bytes 12288
Async XLA Ops:
  0.6 1.2 %copy-start = (bf16[16,256,128]{2,1,0:T(8,128)(2,1)S(1)}, bf16[16,256,128]{2,1,0:T(8,128)(2,1)}, u32[]{:S(2)}) copy-start(bf16[16,256,128]{2,1,0:T(8,128)(2,1)} %x_ref.3) | copy-start | bytes 3145732
  1.9 0.7 %copy-start.2 = (bf16[17]{0:T(256)(128)(2,1)S(1)}, bf16[17]{0:T(256)(128)(2,1)}, u32[]{:S(2)}) copy-start(bf16[17]{0:T(256)(128)(2,1)} %param.7) | copy-start | bytes 106
  4.5 15.8 %collective-permute-start.5 = (bf16[34,16,128]{2,1,0:T(8,128)(2,1)S(1)}, bf16[34,16,128]{2,1,0:T(8,128)(2,1)S(1)}, u32[]{:S(2)}, u32[]{:S(2)}) collective-permute-start(bf16[34,16,128]{2,1,0:T(8,128)(2,1)S(1)} %get-tuple-element.46), channel_id=1, source_target_pairs={{0,4},{1,5},{2,6},{3,7},{4,0},{5,1},{6,2},{7,3},{8,12},{9,13},{10,... | collective-permute-start | bytes 417800 | tf_op jit(solution)/shard_map/ppermute | solution.py:457
  7.2 13.1 %collective-permute-start.6 = (bf16[34,16,128]{2,1,0:T(8,128)(2,1)S(1)}, bf16[34,16,128]{2,1,0:T(8,128)(2,1)S(1)}, u32[]{:S(2)}, u32[]{:S(2)}) collective-permute-start(bf16[34,16,128]{2,1,0:T(8,128)(2,1)S(1)} %get-tuple-element.47), channel_id=1, source_target_pairs={{0,5},{1,4},{2,7},{3,6},{4,1},{5,0},{6,3},{7,2},{8,13},{9,12},{10,... | collective-permute-start | bytes 417800 | tf_op jit(solution)/shard_map/ppermute | solution.py:457
  7.2 6.6 %collective-permute-start = (bf16[16,8,256]{2,1,0:T(8,128)(2,1)S(1)}, bf16[16,8,256]{2,1,0:T(8,128)(2,1)S(1)}, u32[]{:S(2)}, u32[]{:S(2)}) collective-permute-start(bf16[16,8,256]{2,1,0:T(8,128)(2,1)S(1)} %get-tuple-element.34), channel_id=1, source_target_pairs={{0,8},{8,0},{16,24},{24,16},{1,9},{9,1},{17,25},{25,17},{2,10},{10... | collective-permute-start | bytes 196616 | tf_op jit(solution)/shard_map/ppermute | solution.py:480
  8.7 7.0 %collective-permute-start.1 = (bf16[16,8,256]{2,1,0:T(8,128)(2,1)S(1)}, bf16[16,8,256]{2,1,0:T(8,128)(2,1)S(1)}, u32[]{:S(2)}, u32[]{:S(2)}) collective-permute-start(bf16[16,8,256]{2,1,0:T(8,128)(2,1)S(1)} %get-tuple-element.35), channel_id=1, source_target_pairs={{8,16},{16,8},{9,17},{17,9},{10,18},{18,10},{11,19},{19,11},{12,20... | collective-permute-start | bytes 196616 | tf_op jit(solution)/shard_map/ppermute | solution.py:482
  11.1 0.7 %copy-start.1 = (bf16[2,1,32,16]{2,3,1,0:T(8,128)(2,1)S(1)}, bf16[2,1,32,16]{2,3,1,0:T(8,128)(2,1)}, u32[]{:S(2)}) copy-start(bf16[2,1,32,16]{2,3,1,0:T(8,128)(2,1)} %param.5) | copy-start | bytes 6148
  11.8 0.7 %copy-start.3 = (bf16[17]{0:T(256)(128)(2,1)S(1)}, bf16[17]{0:T(256)(128)(2,1)}, u32[]{:S(2)}) copy-start(bf16[17]{0:T(256)(128)(2,1)} %param.6) | copy-start | bytes 106
  17.4 5.9 %collective-permute-start.2 = (bf16[35,16,128]{2,1,0:T(8,128)(2,1)S(1)}, bf16[35,16,128]{2,1,0:T(8,128)(2,1)S(1)}, u32[]{:S(2)}, u32[]{:S(2)}) collective-permute-start(bf16[35,16,128]{2,1,0:T(8,128)(2,1)S(1)} %get-tuple-element.43), channel_id=1, source_target_pairs={{0,1},{1,0},{2,3},{3,2},{4,5},{5,4},{6,7},{7,6},{8,9},{9,8},{10,11... | collective-permute-start | bytes 430088 | tf_op jit(solution)/shard_map/ppermute | solution.py:457
  17.4 8.6 %collective-permute-start.3 = (bf16[35,16,128]{2,1,0:T(8,128)(2,1)S(1)}, bf16[35,16,128]{2,1,0:T(8,128)(2,1)S(1)}, u32[]{:S(2)}, u32[]{:S(2)}) collective-permute-start(bf16[35,16,128]{2,1,0:T(8,128)(2,1)S(1)} %get-tuple-element.44), channel_id=1, source_target_pairs={{0,2},{1,3},{2,4},{3,5},{4,6},{5,7},{6,0},{7,1},{8,10},{9,11},{10,... | collective-permute-start | bytes 430088 | tf_op jit(solution)/shard_map/ppermute | solution.py:457
  19.1 9.1 %collective-permute-start.4 = (bf16[35,16,128]{2,1,0:T(8,128)(2,1)S(1)}, bf16[35,16,128]{2,1,0:T(8,128)(2,1)S(1)}, u32[]{:S(2)}, u32[]{:S(2)}) collective-permute-start(bf16[35,16,128]{2,1,0:T(8,128)(2,1)S(1)} %get-tuple-element.45), channel_id=1, source_target_pairs={{0,3},{1,2},{2,5},{3,4},{4,7},{5,6},{6,1},{7,0},{8,11},{9,10},{10,... | collective-permute-start | bytes 430088 | tf_op jit(solution)/shard_map/ppermute | solution.py:457
  20.3 16.4 %collective-permute-start.8 = (bf16[35,16,128]{2,1,0:T(8,128)(2,1)S(1)}, bf16[35,16,128]{2,1,0:T(8,128)(2,1)S(1)}, u32[]{:S(2)}, u32[]{:S(2)}) collective-permute-start(bf16[35,16,128]{2,1,0:T(8,128)(2,1)S(1)} %get-tuple-element.54), channel_id=1, source_target_pairs={{0,7},{1,6},{2,1},{3,0},{4,3},{5,2},{6,5},{7,4},{8,15},{9,14},{10,... | collective-permute-start | bytes 430088 | tf_op jit(solution)/shard_map/ppermute | solution.py:457
  23.0 13.7 %collective-permute-start.7 = (bf16[35,16,128]{2,1,0:T(8,128)(2,1)S(1)}, bf16[35,16,128]{2,1,0:T(8,128)(2,1)S(1)}, u32[]{:S(2)}, u32[]{:S(2)}) collective-permute-start(bf16[35,16,128]{2,1,0:T(8,128)(2,1)S(1)} %get-tuple-element.52), channel_id=1, source_target_pairs={{0,6},{1,7},{2,0},{3,1},{4,2},{5,3},{6,4},{7,5},{8,14},{9,15},{10,... | collective-permute-start | bytes 430088 | tf_op jit(solution)/shard_map/ppermute | solution.py:457
  23.3 13.0 %collective-permute-start.9 = (bf16[6,16,128]{2,1,0:T(8,128)(2,1)S(1)}, bf16[6,16,128]{2,1,0:T(8,128)(2,1)S(1)}, u32[]{:S(2)}, u32[]{:S(2)}) collective-permute-start(bf16[6,16,128]{2,1,0:T(8,128)(2,1)S(1)} %get-tuple-element.56), channel_id=1, source_target_pairs={{0,4},{1,5},{2,6},{3,7},{4,0},{5,1},{6,2},{7,3},{8,12},{9,13},{10,... | collective-permute-start | bytes 73736 | tf_op jit(solution)/shard_map/ppermute | solution.py:457
  26.0 10.7 %collective-permute-start.10 = (bf16[6,16,128]{2,1,0:T(8,128)(2,1)S(1)}, bf16[6,16,128]{2,1,0:T(8,128)(2,1)S(1)}, u32[]{:S(2)}, u32[]{:S(2)}) collective-permute-start(bf16[6,16,128]{2,1,0:T(8,128)(2,1)S(1)} %get-tuple-element.58), channel_id=1, source_target_pairs={{0,5},{1,4},{2,7},{3,6},{4,1},{5,0},{6,3},{7,2},{8,13},{9,12},{10,... | collective-permute-start | bytes 73736 | tf_op jit(solution)/shard_map/ppermute | solution.py:457
  37.8 4.3 %collective-permute-start.11 = (f32[128,128]{1,0:T(8,128)S(1)}, f32[128,128]{1,0:T(8,128)S(1)}, u32[]{:S(2)}, u32[]{:S(2)}) collective-permute-start(f32[128,128]{1,0:T(8,128)S(1)} %get-tuple-element.62.refs_0_), channel_id=1, source_target_pairs={{0,2},{1,3},{2,0},{3,1},{4,6},{5,7},{6,4},{7,5},{8,10},{9,11},{10,... | collective-permute-start | bytes 196616 | tf_op jit(solution)/shard_map/ppermute | solution.py:454
  37.9 4.3 %collective-permute-start.12 = (f32[128,128]{1,0:T(8,128)S(1)}, f32[128,128]{1,0:T(8,128)S(1)}, u32[]{:S(2)}, u32[]{:S(2)}) collective-permute-start(f32[128,128]{1,0:T(8,128)S(1)} %get-tuple-element.62.refs_0_), channel_id=1, source_target_pairs={{0,1},{1,0},{2,3},{3,2},{4,5},{5,4},{6,7},{7,6},{8,9},{9,8},{10,11... | collective-permute-start | bytes 196616 | tf_op jit(solution)/shard_map/ppermute | solution.py:454
  42.2 1.3 %collective-permute-start.13 = (f32[128,128]{1,0:T(8,128)S(1)}, f32[128,128]{1,0:T(8,128)S(1)}, u32[]{:S(2)}, u32[]{:S(2)}) collective-permute-start(f32[128,128]{1,0:T(8,128)S(1)} %collective-permute-done.11.refs_1_), channel_id=1, source_target_pairs={{0,1},{1,0},{2,3},{3,2},{4,5},{5,4},{6,7},{7,6},{8,9},{9,8},{10,11... | collective-permute-start | bytes 196616 | tf_op jit(solution)/shard_map/ppermute | solution.py:454
  45.6 4.7 %collective-permute-start.14 = (f32[2,16,32]{2,1,0:T(8,128)S(1)}, f32[2,16,32]{2,1,0:T(8,128)S(1)}, u32[]{:S(2)}, u32[]{:S(2)}) collective-permute-start(f32[2,16,32]{2,1,0:T(8,128)S(1)} %get-tuple-element.65), channel_id=1, source_target_pairs={{0,4},{1,5},{2,6},{3,7},{4,0},{5,1},{6,2},{7,3},{8,12},{9,13},{10,... | collective-permute-start | bytes 12296 | tf_op jit(solution)/shard_map/ppermute | solution.py:454

commit v5 on v4

--- a/solution.py
+++ b/solution.py
@@ -126,8 +126,8 @@
             rows_scr[pl.ds(f, part, stride=frames), :] = value
 
 
-def put_edges(out_ref, at, index, rows_scr, anchor_scr, share, frames, width):
-    cols = out_ref.shape[2]
+def put_edges(out_ref, index, rows_scr, anchor_scr, share, width, omega):
+    _, frames, cols = out_ref.shape
     packed = cols // (2 * width)
     groups = share // packed
     lane = lax.broadcasted_iota(jnp.int32, (frames, cols), 1) // (2 * width)
@@ -138,36 +138,31 @@
             begin = pl.multiple_of(start + (group * packed + q) * frames, frames)
             value = rows_scr[pl.ds(begin, frames), :]
             tile = jnp.where(lane == q, turned(value, width + 2 * width * q), tile)
-        out_ref[at + group] = tile.astype(BF16)
+        out_ref[group] = tile.astype(BF16)
     first = pl.multiple_of(index * share, share)
-    tile = jnp.zeros((frames, cols), F32)
-    for q in range(packed):
-        value = jnp.concatenate(
-            [
-                anchor_scr[pl.ds(first + q, groups, stride=packed), :],
-                jnp.zeros((frames - groups, cols), F32),
-            ],
-            axis=0,
-        )
-        tile = jnp.where(lane == q, turned(value, width + 2 * width * q), tile)
-    out_ref[at + groups] = tile.astype(BF16)
-
-
-def early_kernel(axis, side, count, x_ref, taps_hbm, *rest):
+    ranks = omega.shape[1]
+    tile = jnp.concatenate([omega.astype(F32), jnp.zeros((frames, cols - ranks), F32)], axis=1)
+    for q in range(2):
+        at = ranks + 2 * width * q
+        value = anchor_scr[pl.ds(first + q, share // 2, stride=2), :]
+        if share // 2 < frames:
+            value = jnp.concatenate([value, jnp.zeros((frames - share // 2, cols), F32)], axis=0)
+        tile = jnp.where(lane == at // (2 * width), turned(value, width + at), tile)
+    out_ref[groups] = tile.astype(BF16)
+
+
+def early_kernel(axis, side, count, x_ref, taps_ref, *rest):
     outs, (a_ref, b_ref), scratch = rest[:2], rest[2:4], rest[4:]
-    taps_ref, centre_scr, rows_scr, anchor_scr, sem = scratch
+    centre_scr, rows_scr, anchor_scr = scratch
     frames, rows, cols = x_ref.shape
     part, span = anchor_scr.shape[0], centre_scr.shape[0]
     share = part // 2
     radius = (taps_ref.shape[1] - 1) // 2
-    copy = pltpu.make_async_copy(taps_hbm, taps_ref, sem)
-    copy.start()
     me = lax.axis_index(axis)
     chip = device_at(me, count, count // 4, 0) // 2
     first = jnp.clip(chip * part - (span - part) // 2, 0, rows - span)
     first = pl.multiple_of(first, 16)
     inner = pl.multiple_of(chip * part - first, 16)
-    copy.wait()
     taps = taps_ref[...].astype(F32)
     bx = toeplitz(taps, cols, cols, radius, -1).astype(BF16)
     dy = toeplitz(taps, part, span, radius - inner).astype(BF16)
@@ -273,8 +268,8 @@
             put_omega(out, at + share + share // frames, om_ref[dest // (count // TY)])
     for h, out in enumerate(edge_refs):
         dest = device_at(me, count, early, h)
-        put_edges(out, 0, dest, rows_scr, anchor_scr, share, frames, radius)
-        put_omega(out, out.shape[0] - 1, om_ref[dest // (count // TY)])
+        omega = om_ref[dest // (count // TY)]
+        put_edges(out, dest, rows_scr, anchor_scr, share, radius, omega)
 
 
 def message_list(count):
@@ -288,18 +283,18 @@
     anchor_ref[pl.ds(src, share, stride=count), :] = anchor.astype(F32)
 
 
-def take_edges(data_ref, anchor_ref, ref, src, width):
+def take_edges(data_ref, anchor_ref, ref, src, width, ranks):
     share, count, frames, cols = data_ref.shape
     packed = cols // (2 * width)
     groups = share // packed
     lanes = lax.broadcasted_iota(jnp.int32, (frames, cols), 1)
     at_edge = (lanes < width) | (lanes >= cols - width)
     last = ref[groups].astype(F32)
-    for q in range(packed):
-        edge = turned(last, -(width + 2 * width * q))[:groups]
-        where = pl.ds(src + q * count, groups, stride=count * packed)
+    for q in range(2):
+        edge = turned(last, -(width + ranks + 2 * width * q))[: share // 2]
+        where = pl.ds(src + q * count, share // 2, stride=2 * count)
         old = anchor_ref[where, :]
-        anchor_ref[where, :] = jnp.where(at_edge[:groups], edge, old)
+        anchor_ref[where, :] = jnp.where(at_edge[: share // 2], edge, old)
     for group in range(groups):
         tile = ref[group].astype(F32)
         for q in range(packed):
@@ -322,7 +317,7 @@
         take_block(data_ref, anchor_ref, ref, 0, device_at(me, count, -(count // 4), h))
 
 
-def temporal_kernel(axis, width, places, *refs):
+def temporal_kernel(axis, width, ranks, places, *refs):
     blocks, edge_refs, lhs_ref = refs[3:-8], refs[-8:-6], refs[-6]
     data_ref, anchor_ref, om_ref, m_ref, gram_ref = refs[-5:]
     share, count, frames, cols = data_ref.shape
@@ -335,7 +330,7 @@
         om_ref[src] = ref[slots]
     for h, ref in enumerate(edge_refs):
         src = device_at(me, count, -(count // 4), h)
-        take_edges(data_ref, anchor_ref, ref, src, width)
+        take_edges(data_ref, anchor_ref, ref, src, width, ranks)
         om_ref[src] = ref[ref.shape[0] - 1]
     lhs = lhs_ref[...]
     gram = jnp.zeros((all_frames, all_frames), F32)
@@ -399,7 +394,7 @@
 
 
 def factor_kernel(axis, count, ranks, pixels, om_ref, *refs):
-    grams, (mix_ref, own_ref, send_ref) = refs[:-3], refs[-3:]
+    grams, (mix_ref, own_ref, send_ref, coef_scr) = refs[:-4], refs[-4:]
     frames = own_ref.shape[1]
     all_frames = grams[0].shape[0]
     me = lax.axis_index(axis)
@@ -412,12 +407,11 @@
     back = exact(load, gram, 1, 0)
     mix, coef = whiten(exact(back, load, 1, 1), load, back)
     mix_ref[...] = mix * math.sqrt(pixels)
-    ids = lax.broadcasted_iota(jnp.int32, (frames, all_frames), 0)
-    lane = lax.broadcasted_iota(jnp.int32, (frames, all_frames), 1)
+    coef_scr[...] = coef.T
     for ref, who in ((own_ref, me), (send_ref, me ^ (count // TY))):
-        pick = jnp.where(lane == ids + who * frames, 1.0, 0.0)
         ref[...] = jnp.zeros_like(ref)
-        ref[me // (count // TY)] = exact(pick, coef, 1, 1)
+        start = pl.multiple_of(who * frames, frames)
+        ref[me // (count // TY)] = coef_scr[pl.ds(start, frames), :]
 
 
 def basis_kernel(m_ref, mix_ref, out_ref):
@@ -467,13 +461,10 @@
         ],
         [movie, space_row],
         [
-            pltpu.VMEM(space_row.shape, BF16),
             pltpu.VMEM((span, cols), F32),
             pltpu.VMEM((part * frames, cols), F32),
             pltpu.VMEM((part, cols), F32),
-            pltpu.SemaphoreType.DMA,
         ],
-        [pltpu.VMEM, pltpu.HBM],
     )
     mains = [send(value, early, h) for h, value in enumerate(mains)]
     pairs = [(i, i ^ 1) for i in range(tiles)]
@@ -499,15 +490,15 @@
         functools.partial(spatial_kernel, "tm"),
         [
             *[shape((len(flips) * (slots + 1), frames, cols), BF16) for _, flips in listed],
-            *([shape((share // packed + 2, frames, cols), BF16)] * 2),
+            *([shape((share // packed + 1, frames, cols), BF16)] * 2),
         ],
         [side_a, side_b, bh, dy, om, *prepared],
         [pltpu.VMEM((rows * frames, cols), F32), pltpu.VMEM((rows, cols), F32)],
     )
-    def after(value, other):
-        return lax.optimization_barrier((value, other))[0]
-
-    parts[-2:] = [after(value, other) for value, other in zip(parts[-2:], mains)]
+    def after(value, *others):
+        return lax.optimization_barrier((value, *others))[0]
+
+    parts[-1] = after(parts[-1], *mains)
     blocks = [parts[0]] + [
         send(value, shift, flip) for (shift, (flip,)), value in zip(listed[1:], parts[1:])
     ]
@@ -524,7 +515,7 @@
         [*blocks[:-2], *mains],
     )
     _, _, om_all, matrix, gram = call(
-        functools.partial(temporal_kernel, "tm", radius, places[-2:]),
+        functools.partial(temporal_kernel, "tm", radius, ranks, places[-2:]),
         [
             *[shape(value.shape, value.dtype) for value in known],
             shape((share, all_frames, cols), BF16),
@@ -539,6 +530,7 @@
         functools.partial(factor_kernel, "tm", count, ranks, pixels),
         [shape((ranks, all_frames), F32), *([shape((TY, frames, ranks), F32)] * 2)],
         [om_all, *grams],
+        [pltpu.VMEM((all_frames, ranks), F32)],
     )
     coef_other = swap(coef_send, group)
     (basis,) = call(basis_kernel, [shape((ranks * share, cols), F32)], [matrix, mix])

time: 51.3 us -> 50.7 us (0.988)
  transfers between devices with their start and end apart: 15 -> 15, of which waited for: 8 -> 9; matrix products, arithmetic and copies ran while one was open for 0% -> 0% of each run, Pallas kernels for 9% -> 9%
where the time goes in v5:
time: 50.7 us; the launch traced here: 50.5 us
  waiting for transfers between devices  23.2 us (46%)
  starting transfers between devices  13 us (26%)
  Pallas kernels  9.69 us (19%)
  local copies, waits for them, and re-layouts  3.22 us (6%)
  between operations  0.72 us (1%)
  other arithmetic  0.61 us (1%)
    ppermute x9, waiting for transfers between devices, send(): lax.ppermute(value, 'tm', [(i, device_at(i, count, shift, flip)) for i in...  12.7 us
    pallas_call x7, Pallas kernels, call(): pl.pallas_call(kernel, out_shape=outs, in_specs=[pl.BlockSpec(memory_spac...  9.69 us
    ppermute x9, starting transfers between devices, send(): lax.ppermute(value, 'tm', [(i, device_at(i, count, shift, flip)) for i in...  8.74 us
    ppermute x4, waiting for transfers between devices, swap(): return lax.ppermute(value, 'tm', [(i, i ^ k) for i in range(count)])  8.59 us
    unnamed x8, local copies, waits for them, and re-layouts  3.22 us
    ppermute x1, starting transfers between devices, local(): side_b = lax.ppermute(side_b, 'tile', pairs + [(j, i) for i, j in pairs])  2.37 us
    ppermute x1, waiting for transfers between devices, local(): side_b = lax.ppermute(side_b, 'tile', pairs + [(j, i) for i, j in pairs])  1.91 us
    ppermute x1, starting transfers between devices, local(): side_a = lax.ppermute(side_a, 'tile', pairs)  1.49 us
  transfers between devices with their start and end apart: 15, of which 9 were waited for; matrix products, arithmetic and copies ran while one was open for 0% of the time, Pallas kernels for 9%

profile of v5, /device:TPU:4, one launch (start us, length us, event | category | flops | bytes accessed | tf_op | source)
XLA Modules:
  0.0 50.5 jit_solution(10849799546582171863)
XLA Ops:
  0.6 0.0 copy-start
  0.6 1.2 %copy-done = bf16[16,256,128]{2,1,0:T(8,128)(2,1)S(1)} copy-done((bf16[16,256,128]{2,1,0:T(8,128)(2,1)S(1)}, bf16[16,256,128]{2,1,0:T(8,128)(2,1)}, u32[]{:S(2)}) %copy-start) | copy-done | bytes 1048600
  1.9 0.0 copy-start.2
  1.9 0.7 %copy-done.2 = bf16[17]{0:T(256)(128)(2,1)S(1)} copy-done((bf16[17]{0:T(256)(128)(2,1)S(1)}, bf16[17]{0:T(256)(128)(2,1)}, u32[]{:S(2)}) %copy-start.2) | copy-done | bytes 58
  2.5 2.0 %shard_map.59 = (bf16[34,16,128]{2,1,0:T(8,128)(2,1)S(1)}, bf16[34,16,128]{2,1,0:T(8,128)(2,1)S(1)}, bf16[16,8,256]{2,1,0:T(8,128)(2,1)S(1)}, bf16[16,8,256]{2,1,0:T(8,128)(2,1)S(1)}) custom-call(bf16[16,256,128]{2,1,0:T(8,128)(2,1)S(1)} %copy-done, bf16[1,17]{1,0:T(2,128)(2,1)S(1)} %bitcast.13), custom_call_target="tpu_custom_call" | custom-call | tf_op jit(solution)/shard_map/pallas_call | solution.py:18
  4.5 2.6 %collective-permute-start.5 = (bf16[34,16,128]{2,1,0:T(8,128)(2,1)S(1)}, bf16[34,16,128]{2,1,0:T(8,128)(2,1)S(1)}, u32[]{:S(2)}, u32[]{:S(2)}) collective-permute-start(bf16[34,16,128]{2,1,0:T(8,128)(2,1)S(1)} %get-tuple-element.45), channel_id=1, source_target_pairs={{0,4},{1,5},{2,6},{3,7},{4,0},{5,1},{6,2},{7,3},{8,12},{9,13},{10,... | collective-permute-start | bytes 417800 | tf_op jit(solution)/shard_map/ppermute | solution.py:451
  7.1 0.0 collective-permute-start.6
  7.1 1.5 %collective-permute-start = (bf16[16,8,256]{2,1,0:T(8,128)(2,1)S(1)}, bf16[16,8,256]{2,1,0:T(8,128)(2,1)S(1)}, u32[]{:S(2)}, u32[]{:S(2)}) collective-permute-start(bf16[16,8,256]{2,1,0:T(8,128)(2,1)S(1)} %get-tuple-element.33), channel_id=1, source_target_pairs={{0,8},{8,0},{16,24},{24,16},{1,9},{9,1},{17,25},{25,17},{2,10},{10... | collective-permute-start | bytes 196616 | tf_op jit(solution)/shard_map/ppermute | solution.py:471
  8.6 2.4 %collective-permute-start.1 = (bf16[16,8,256]{2,1,0:T(8,128)(2,1)S(1)}, bf16[16,8,256]{2,1,0:T(8,128)(2,1)S(1)}, u32[]{:S(2)}, u32[]{:S(2)}) collective-permute-start(bf16[16,8,256]{2,1,0:T(8,128)(2,1)S(1)} %get-tuple-element.34), channel_id=1, source_target_pairs={{8,16},{16,8},{9,17},{17,9},{10,18},{18,10},{11,19},{19,11},{12,20... | collective-permute-start | bytes 196616 | tf_op jit(solution)/shard_map/ppermute | solution.py:473
  11.0 0.0 copy-start.1
  11.0 0.7 %copy-done.1 = bf16[2,1,32,16]{2,3,1,0:T(8,128)(2,1)S(1)} copy-done((bf16[2,1,32,16]{2,3,1,0:T(8,128)(2,1)S(1)}, bf16[2,1,32,16]{2,3,1,0:T(8,128)(2,1)}, u32[]{:S(2)}) %copy-start.1) | copy-done | bytes 2072
  11.7 0.0 copy-start.3
  11.7 0.7 %copy-done.3 = bf16[17]{0:T(256)(128)(2,1)S(1)} copy-done((bf16[17]{0:T(256)(128)(2,1)S(1)}, bf16[17]{0:T(256)(128)(2,1)}, u32[]{:S(2)}) %copy-start.3) | copy-done | bytes 58
  12.3 1.4 %shard_map.60 = (bf16[16,128]{1,0:T(8,128)(2,1)S(1)}, bf16[256,256]{1,0:T(8,128)(2,1)S(1)}, bf16[128,144]{1,0:T(8,128)(2,1)S(1)}, bf16[2,16,32]{2,1,0:T(8,128)(2...) custom-call(bf16[16,256,128]{2,1,0:T(8,128)(2,1)S(1)} %copy-done, ...), custom_call_target="tpu_custom_call" | custom-call | tf_op jit(solution)/shard_map/pallas_call | solution.py:18
  13.7 0.0 collective-permute-done.a_ref
  13.7 1.9 %collective-permute-done.1.b_ref = bf16[16,8,256]{2,1,0:T(8,128)(2,1)S(1)} collective-permute-done((bf16[16,8,256]{2,1,0:T(8,128)(2,1)S(1)}, bf16[16,8,256]{2,1,0:T(8,128)(2,1)S(1)}, u32[]{:S(2)}, u32[]{:S(2)}) %collective-permute-start.1) | collective-permute-done | bytes 65568 | tf_op jit(solution)/shard_map/ppermute | solution.py:473
  15.6 1.7 %shard_map.61 = (bf16[35,16,128]{2,1,0:T(8,128)(2,1)S(1)}, bf16[35,16,128]{2,1,0:T(8,128)(2,1)S(1)}, bf16[35,16,128]{2,1,0:T(8,128)(2,1)S(1)}, bf16[35,16,128]{2...) custom-call(bf16[16,8,256]{2,1,0:T(8,128)(2,1)S(1)} %collective-perm, ...), custom_call_target="tpu_custom_call" | custom-call | tf_op jit(solution)/shard_map/pallas_call | solution.py:18
  17.4 0.1 collective-permute-start.2
  17.4 1.6 %collective-permute-start.3 = (bf16[35,16,128]{2,1,0:T(8,128)(2,1)S(1)}, bf16[35,16,128]{2,1,0:T(8,128)(2,1)S(1)}, u32[]{:S(2)}, u32[]{:S(2)}) collective-permute-start(bf16[35,16,128]{2,1,0:T(8,128)(2,1)S(1)} %get-tuple-element.43), channel_id=1, source_target_pairs={{0,2},{1,3},{2,4},{3,5},{4,6},{5,7},{6,0},{7,1},{8,10},{9,11},{10,... | collective-permute-start | bytes 430088 | tf_op jit(solution)/shard_map/ppermute | solution.py:451
  19.1 1.2 %collective-permute-start.4 = (bf16[35,16,128]{2,1,0:T(8,128)(2,1)S(1)}, bf16[35,16,128]{2,1,0:T(8,128)(2,1)S(1)}, u32[]{:S(2)}, u32[]{:S(2)}) collective-permute-start(bf16[35,16,128]{2,1,0:T(8,128)(2,1)S(1)} %get-tuple-element.44), channel_id=1, source_target_pairs={{0,3},{1,2},{2,5},{3,4},{4,7},{5,6},{6,1},{7,0},{8,11},{9,10},{10,... | collective-permute-start | bytes 430088 | tf_op jit(solution)/shard_map/ppermute | solution.py:451
  20.3 0.0 collective-permute-done.5.refs_4_
  20.3 2.3 %collective-permute-start.7 = (bf16[35,16,128]{2,1,0:T(8,128)(2,1)S(1)}, bf16[35,16,128]{2,1,0:T(8,128)(2,1)S(1)}, u32[]{:S(2)}, u32[]{:S(2)}) collective-permute-start(bf16[35,16,128]{2,1,0:T(8,128)(2,1)S(1)} %get-tuple-element.50), channel_id=1, source_target_pairs={{0,6},{1,7},{2,0},{3,1},{4,2},{5,3},{6,4},{7,5},{8,14},{9,15},{10,... | collective-permute-start | bytes 430088 | tf_op jit(solution)/shard_map/ppermute | solution.py:451
  22.7 0.0 collective-permute-done.6.refs_5_
  22.7 0.2 collective-permute-start.8
  22.9 0.0 collective-permute-done.2.refs_1_
  22.9 0.6 %collective-permute-start.9 = (bf16[5,16,128]{2,1,0:T(8,128)(2,1)S(1)}, bf16[5,16,128]{2,1,0:T(8,128)(2,1)S(1)}, u32[]{:S(2)}, u32[]{:S(2)}) collective-permute-start(bf16[5,16,128]{2,1,0:T(8,128)(2,1)S(1)} %get-tuple-element.54), channel_id=1, source_target_pairs={{0,4},{1,5},{2,6},{3,7},{4,0},{5,1},{6,2},{7,3},{8,12},{9,13},{10,... | collective-permute-start | bytes 61448 | tf_op jit(solution)/shard_map/ppermute | solution.py:451
  23.5 2.5 %collective-permute-done.3.refs_2_ = bf16[35,16,128]{2,1,0:T(8,128)(2,1)S(1)} collective-permute-done((bf16[35,16,128]{2,1,0:T(8,128)(2,1)S(1)}, bf16[35,16,128]{2,1,0:T(8,128)(2,1)S(1)}, u32[]{:S(2)}, u32[]{:S(2)}) %collective-permute-start.3) | collective-permute-done | bytes 143392 | tf_op jit(solution)/shard_map/ppermute | solution.py:451
  26.0 0.0 collective-permute-start.10
  26.0 2.2 %collective-permute-done.4.refs_3_ = bf16[35,16,128]{2,1,0:T(8,128)(2,1)S(1)} collective-permute-done((bf16[35,16,128]{2,1,0:T(8,128)(2,1)S(1)}, bf16[35,16,128]{2,1,0:T(8,128)(2,1)S(1)}, u32[]{:S(2)}, u32[]{:S(2)}) %collective-permute-start.4) | collective-permute-done | bytes 143392 | tf_op jit(solution)/shard_map/ppermute | solution.py:451
  28.2 0.1 shard_map.62
  28.3 3.3 %collective-permute-done.7.refs_3_ = bf16[35,16,128]{2,1,0:T(8,128)(2,1)S(1)} collective-permute-done((bf16[35,16,128]{2,1,0:T(8,128)(2,1)S(1)}, bf16[35,16,128]{2,1,0:T(8,128)(2,1)S(1)}, u32[]{:S(2)}, u32[]{:S(2)}) %collective-permute-start.7) | collective-permute-done | bytes 143392 | tf_op jit(solution)/shard_map/ppermute | solution.py:451
  31.6 4.4 %collective-permute-done.9.refs_5_ = bf16[5,16,128]{2,1,0:T(8,128)(2,1)S(1)} collective-permute-done((bf16[5,16,128]{2,1,0:T(8,128)(2,1)S(1)}, bf16[5,16,128]{2,1,0:T(8,128)(2,1)S(1)}, u32[]{:S(2)}, u32[]{:S(2)}) %collective-permute-start.9) | collective-permute-done | bytes 20512 | tf_op jit(solution)/shard_map/ppermute | solution.py:451
  36.0 0.3 collective-permute-done.10.refs_6_
  36.3 0.0 collective-permute-done.8.refs_4_
  36.3 1.1 %shard_map.63 = (bf16[32,8,16,128]{3,2,1,0:T(8,128)(2,1)S(1)}, f32[256,128]{1,0:T(8,128)S(1)}, bf16[8,16,128]{2,1,0:T(8,128)(2,1)S(1)}, bf16[32,128,128]{2,1,0:T(8,128)(2,1)S(1)}, f32[128,128]{1,0:T(8,128)S(1)}) custom-call(bf16[32,8,16,128]{3,2,1,0:T(8,128)(2,1)S(1)} %get-tuple-element.47.refs_0_, ...), custom_call_target="tpu_custom_call", output_to_operand_aliasing={{0}: (0, {}), {1}: (1, {}), {2}: (2, {})} | custom-call | tf_op jit(solution)/shard_map/pallas_call | solution.py:18
  37.5 0.1 collective-permute-start.11
  37.5 0.2 collective-permute-start.12
  37.7 4.1 %collective-permute-done.11.refs_1_ = f32[128,128]{1,0:T(8,128)S(1)} collective-permute-done((f32[128,128]{1,0:T(8,128)S(1)}, f32[128,128]{1,0:T(8,128)S(1)}, u32[]{:S(2)}, u32[]{:S(2)}) %collective-permute-start.11) | collective-permute-done | bytes 65568 | tf_op jit(solution)/shard_map/ppermute | solution.py:448
  41.8 0.0 collective-permute-start.13
  41.8 0.0 collective-permute-done.12.refs_2_
  41.8 1.2 %collective-permute-done.13.refs_3_ = f32[128,128]{1,0:T(8,128)S(1)} collective-permute-done((f32[128,128]{1,0:T(8,128)S(1)}, f32[128,128]{1,0:T(8,128)S(1)}, u32[]{:S(2)}, u32[]{:S(2)}) %collective-permute-start.13) | collective-permute-done | bytes 65568 | tf_op jit(solution)/shard_map/ppermute | solution.py:448
  43.0 2.1 %shard_map.64 = (f32[32,128]{1,0:T(8,128)S(1)}, f32[2,16,32]{2,1,0:T(8,128)S(1)}, f32[2,16,32]{2,1,0:T(8,128)S(1)}) custom-call(bf16[8,16,128]{2,1,0:T(8,128)(2,1)S(1)} %get-tuple-element.59.om_ref, f32[128,128]{1,0:T(8,128)S(1)} %get-tuple-element.60.refs_0_, f32[128,128]{1,0:T(8,128)S(1)} %collective-permute-done.11.refs_1_, ...), custom_call_target="tpu_custom_call" | custom-call | tf_op jit(solution)/shard_map/pallas_call | solution.py:18
  45.1 0.2 collective-permute-start.14
  45.3 1.3 %shard_map.65 = f32[1024,128]{1,0:T(8,128)} custom-call(bf16[32,128,128]{2,1,0:T(8,128)(2,1)S(1)} %get-tuple-element.58.m_ref, f32[32,128]{1,0:T(8,128)S(1)} %get-tuple-element.61.mix_ref), custom_call_target="tpu_custom_call" | custom-call | tf_op jit(solution)/shard_map/pallas_call | solution.py:18
  46.6 3.3 %collective-permute-done.14 = f32[2,16,32]{2,1,0:T(8,128)S(1)} collective-permute-done((f32[2,16,32]{2,1,0:T(8,128)S(1)}, f32[2,16,32]{2,1,0:T(8,128)S(1)}, u32[]{:S(2)}, u32[]{:S(2)}) %collective-permute-start.14) | collective-permute-done | bytes 4128 | tf_op jit(solution)/shard_map/ppermute | solution.py:448
  49.8 0.6 %add_bitcast_fusion = f32[2,1,32,16]{2,3,1,0:T(8,128)} fusion(f32[2,16,32]{2,1,0:T(8,128)S(1)} %get-tuple-element.62, f32[2,16,32]{2,1,0:T(8,128)S(1)} %collective-permute-done.14), kind=kLoop, calls=%fused_computation | loop fusion | flops 1024 | bytes 12288
Async XLA Ops:
  0.6 1.2 %copy-start = (bf16[16,256,128]{2,1,0:T(8,128)(2,1)S(1)}, bf16[16,256,128]{2,1,0:T(8,128)(2,1)}, u32[]{:S(2)}) copy-start(bf16[16,256,128]{2,1,0:T(8,128)(2,1)} %x_ref.3) | copy-start | bytes 3145732
  1.9 0.7 %copy-start.2 = (bf16[17]{0:T(256)(128)(2,1)S(1)}, bf16[17]{0:T(256)(128)(2,1)}, u32[]{:S(2)}) copy-start(bf16[17]{0:T(256)(128)(2,1)} %param.7) | copy-start | bytes 106
  4.5 15.9 %collective-permute-start.5 = (bf16[34,16,128]{2,1,0:T(8,128)(2,1)S(1)}, bf16[34,16,128]{2,1,0:T(8,128)(2,1)S(1)}, u32[]{:S(2)}, u32[]{:S(2)}) collective-permute-start(bf16[34,16,128]{2,1,0:T(8,128)(2,1)S(1)} %get-tuple-element.45), channel_id=1, source_target_pairs={{0,4},{1,5},{2,6},{3,7},{4,0},{5,1},{6,2},{7,3},{8,12},{9,13},{10,... | collective-permute-start | bytes 417800 | tf_op jit(solution)/shard_map/ppermute | solution.py:451
  7.1 15.6 %collective-permute-start.6 = (bf16[34,16,128]{2,1,0:T(8,128)(2,1)S(1)}, bf16[34,16,128]{2,1,0:T(8,128)(2,1)S(1)}, u32[]{:S(2)}, u32[]{:S(2)}) collective-permute-start(bf16[34,16,128]{2,1,0:T(8,128)(2,1)S(1)} %get-tuple-element.46), channel_id=1, source_target_pairs={{0,5},{1,4},{2,7},{3,6},{4,1},{5,0},{6,3},{7,2},{8,13},{9,12},{10,... | collective-permute-start | bytes 417800 | tf_op jit(solution)/shard_map/ppermute | solution.py:451
  7.1 6.6 %collective-permute-start = (bf16[16,8,256]{2,1,0:T(8,128)(2,1)S(1)}, bf16[16,8,256]{2,1,0:T(8,128)(2,1)S(1)}, u32[]{:S(2)}, u32[]{:S(2)}) collective-permute-start(bf16[16,8,256]{2,1,0:T(8,128)(2,1)S(1)} %get-tuple-element.33), channel_id=1, source_target_pairs={{0,8},{8,0},{16,24},{24,16},{1,9},{9,1},{17,25},{25,17},{2,10},{10... | collective-permute-start | bytes 196616 | tf_op jit(solution)/shard_map/ppermute | solution.py:471
  8.6 7.0 %collective-permute-start.1 = (bf16[16,8,256]{2,1,0:T(8,128)(2,1)S(1)}, bf16[16,8,256]{2,1,0:T(8,128)(2,1)S(1)}, u32[]{:S(2)}, u32[]{:S(2)}) collective-permute-start(bf16[16,8,256]{2,1,0:T(8,128)(2,1)S(1)} %get-tuple-element.34), channel_id=1, source_target_pairs={{8,16},{16,8},{9,17},{17,9},{10,18},{18,10},{11,19},{19,11},{12,20... | collective-permute-start | bytes 196616 | tf_op jit(solution)/shard_map/ppermute | solution.py:473
  11.0 0.7 %copy-start.1 = (bf16[2,1,32,16]{2,3,1,0:T(8,128)(2,1)S(1)}, bf16[2,1,32,16]{2,3,1,0:T(8,128)(2,1)}, u32[]{:S(2)}) copy-start(bf16[2,1,32,16]{2,3,1,0:T(8,128)(2,1)} %param.5) | copy-start | bytes 6148
  11.7 0.7 %copy-start.3 = (bf16[17]{0:T(256)(128)(2,1)S(1)}, bf16[17]{0:T(256)(128)(2,1)}, u32[]{:S(2)}) copy-start(bf16[17]{0:T(256)(128)(2,1)} %param.6) | copy-start | bytes 106
  17.4 5.5 %collective-permute-start.2 = (bf16[35,16,128]{2,1,0:T(8,128)(2,1)S(1)}, bf16[35,16,128]{2,1,0:T(8,128)(2,1)S(1)}, u32[]{:S(2)}, u32[]{:S(2)}) collective-permute-start(bf16[35,16,128]{2,1,0:T(8,128)(2,1)S(1)} %get-tuple-element.42), channel_id=1, source_target_pairs={{0,1},{1,0},{2,3},{3,2},{4,5},{5,4},{6,7},{7,6},{8,9},{9,8},{10,11... | collective-permute-start | bytes 430088 | tf_op jit(solution)/shard_map/ppermute | solution.py:451
  17.4 8.6 %collective-permute-start.3 = (bf16[35,16,128]{2,1,0:T(8,128)(2,1)S(1)}, bf16[35,16,128]{2,1,0:T(8,128)(2,1)S(1)}, u32[]{:S(2)}, u32[]{:S(2)}) collective-permute-start(bf16[35,16,128]{2,1,0:T(8,128)(2,1)S(1)} %get-tuple-element.43), channel_id=1, source_target_pairs={{0,2},{1,3},{2,4},{3,5},{4,6},{5,7},{6,0},{7,1},{8,10},{9,11},{10,... | collective-permute-start | bytes 430088 | tf_op jit(solution)/shard_map/ppermute | solution.py:451
  19.1 9.1 %collective-permute-start.4 = (bf16[35,16,128]{2,1,0:T(8,128)(2,1)S(1)}, bf16[35,16,128]{2,1,0:T(8,128)(2,1)S(1)}, u32[]{:S(2)}, u32[]{:S(2)}) collective-permute-start(bf16[35,16,128]{2,1,0:T(8,128)(2,1)S(1)} %get-tuple-element.44), channel_id=1, source_target_pairs={{0,3},{1,2},{2,5},{3,4},{4,7},{5,6},{6,1},{7,0},{8,11},{9,10},{10,... | collective-permute-start | bytes 430088 | tf_op jit(solution)/shard_map/ppermute | solution.py:451
  20.3 11.3 %collective-permute-start.7 = (bf16[35,16,128]{2,1,0:T(8,128)(2,1)S(1)}, bf16[35,16,128]{2,1,0:T(8,128)(2,1)S(1)}, u32[]{:S(2)}, u32[]{:S(2)}) collective-permute-start(bf16[35,16,128]{2,1,0:T(8,128)(2,1)S(1)} %get-tuple-element.50), channel_id=1, source_target_pairs={{0,6},{1,7},{2,0},{3,1},{4,2},{5,3},{6,4},{7,5},{8,14},{9,15},{10,... | collective-permute-start | bytes 430088 | tf_op jit(solution)/shard_map/ppermute | solution.py:451
  22.7 13.6 %collective-permute-start.8 = (bf16[35,16,128]{2,1,0:T(8,128)(2,1)S(1)}, bf16[35,16,128]{2,1,0:T(8,128)(2,1)S(1)}, u32[]{:S(2)}, u32[]{:S(2)}) collective-permute-start(bf16[35,16,128]{2,1,0:T(8,128)(2,1)S(1)} %get-tuple-element.52), channel_id=1, source_target_pairs={{0,7},{1,6},{2,1},{3,0},{4,3},{5,2},{6,5},{7,4},{8,15},{9,14},{10,... | collective-permute-start | bytes 430088 | tf_op jit(solution)/shard_map/ppermute | solution.py:451
  22.9 13.1 %collective-permute-start.9 = (bf16[5,16,128]{2,1,0:T(8,128)(2,1)S(1)}, bf16[5,16,128]{2,1,0:T(8,128)(2,1)S(1)}, u32[]{:S(2)}, u32[]{:S(2)}) collective-permute-start(bf16[5,16,128]{2,1,0:T(8,128)(2,1)S(1)} %get-tuple-element.54), channel_id=1, source_target_pairs={{0,4},{1,5},{2,6},{3,7},{4,0},{5,1},{6,2},{7,3},{8,12},{9,13},{10,... | collective-permute-start | bytes 61448 | tf_op jit(solution)/shard_map/ppermute | solution.py:451
  26.0 10.3 %collective-permute-start.10 = (bf16[5,16,128]{2,1,0:T(8,128)(2,1)S(1)}, bf16[5,16,128]{2,1,0:T(8,128)(2,1)S(1)}, u32[]{:S(2)}, u32[]{:S(2)}) collective-permute-start(bf16[5,16,128]{2,1,0:T(8,128)(2,1)S(1)} %get-tuple-element.56), channel_id=1, source_target_pairs={{0,5},{1,4},{2,7},{3,6},{4,1},{5,0},{6,3},{7,2},{8,13},{9,12},{10,... | collective-permute-start | bytes 61448 | tf_op jit(solution)/shard_map/ppermute | solution.py:451
  37.5 4.3 %collective-permute-start.11 = (f32[128,128]{1,0:T(8,128)S(1)}, f32[128,128]{1,0:T(8,128)S(1)}, u32[]{:S(2)}, u32[]{:S(2)}) collective-permute-start(f32[128,128]{1,0:T(8,128)S(1)} %get-tuple-element.60.refs_0_), channel_id=1, source_target_pairs={{0,2},{1,3},{2,0},{3,1},{4,6},{5,7},{6,4},{7,5},{8,10},{9,11},{10,... | collective-permute-start | bytes 196616 | tf_op jit(solution)/shard_map/ppermute | solution.py:448
  37.5 4.3 %collective-permute-start.12 = (f32[128,128]{1,0:T(8,128)S(1)}, f32[128,128]{1,0:T(8,128)S(1)}, u32[]{:S(2)}, u32[]{:S(2)}) collective-permute-start(f32[128,128]{1,0:T(8,128)S(1)} %get-tuple-element.60.refs_0_), channel_id=1, source_target_pairs={{0,1},{1,0},{2,3},{3,2},{4,5},{5,4},{6,7},{7,6},{8,9},{9,8},{10,11... | collective-permute-start | bytes 196616 | tf_op jit(solution)/shard_map/ppermute | solution.py:448
  41.8 1.3 %collective-permute-start.13 = (f32[128,128]{1,0:T(8,128)S(1)}, f32[128,128]{1,0:T(8,128)S(1)}, u32[]{:S(2)}, u32[]{:S(2)}) collective-permute-start(f32[128,128]{1,0:T(8,128)S(1)} %collective-permute-done.11.refs_1_), channel_id=1, source_target_pairs={{0,1},{1,0},{2,3},{3,2},{4,5},{5,4},{6,7},{7,6},{8,9},{9,8},{10,11... | collective-permute-start | bytes 196616 | tf_op jit(solution)/shard_map/ppermute | solution.py:448
  45.1 4.7 %collective-permute-start.14 = (f32[2,16,32]{2,1,0:T(8,128)S(1)}, f32[2,16,32]{2,1,0:T(8,128)S(1)}, u32[]{:S(2)}, u32[]{:S(2)}) collective-permute-start(f32[2,16,32]{2,1,0:T(8,128)S(1)} %get-tuple-element.63), channel_id=1, source_target_pairs={{0,4},{1,5},{2,6},{3,7},{4,0},{5,1},{6,2},{7,3},{8,12},{9,13},{10,... | collective-permute-start | bytes 12296 | tf_op jit(solution)/shard_map/ppermute | solution.py:448

commit v6 on v5

--- a/solution.py
+++ b/solution.py
@@ -81,49 +81,6 @@
 def put_block(out_ref, at, dest, share, rows_scr, anchor_scr):
     put_rows(out_ref, at, dest * share, share, rows_scr)
     put_anchor(out_ref, at + share, dest * share, share, anchor_scr)
-
-
-def filter_rows(x_of, halo_of, bx, bh, dy, frames, inner, centre_scr, rows_scr, anchor_scr):
-    part, span = dy.shape
-    cols = bx.shape[0]
-
-    def mean(value_of):
-        total = value_of(0)
-        for f in range(1, frames):
-            total = total + value_of(f)
-        return (total * (1.0 / frames)).astype(BF16)
-
-    def across(block, edge):
-        value = contract(block, bx, 1, 0)
-        return value if edge is None else value + contract(edge, bh, 0, 0)
-
-    def rows_made(value):
-        if part == span:
-            return value
-        centre_scr[...] = value
-        return centre_scr[pl.ds(inner, part), :]
-
-    anchor = mean(x_of)
-    edge = None if halo_of is None else mean(halo_of)
-    anchor32 = anchor.astype(F32)
-    edge32 = None if edge is None else edge.astype(F32)
-    high, low = split(across(anchor, edge))
-    both = contract(dy, jnp.concatenate([high, low], axis=1), 1, 0)
-    anchor_s = rows_made(anchor32) - both[:, :cols] - both[:, cols:]
-    anchor_out = anchor_s.astype(BF16).astype(F32)
-    anchor_scr[...] = anchor_out
-    left_over = anchor_s - anchor_out
-    for p in range(frames // 2):
-        blocks, smooths = [], []
-        for f in (2 * p, 2 * p + 1):
-            block = (x_of(f) - anchor32).astype(BF16)
-            edge = None if halo_of is None else (halo_of(f) - edge32).astype(BF16)
-            smooths.append(across(block, edge).astype(BF16))
-            blocks.append(rows_made(block.astype(F32)))
-        both = contract(dy, jnp.concatenate(smooths, axis=1), 1, 0)
-        for i, f in enumerate((2 * p, 2 * p + 1)):
-            value = blocks[i] - both[:, i * cols : (i + 1) * cols] + left_over
-            rows_scr[pl.ds(f, part, stride=frames), :] = value
 
 
 def put_edges(out_ref, index, rows_scr, anchor_scr, share, width, omega):
@@ -166,12 +123,33 @@
     taps = taps_ref[...].astype(F32)
     bx = toeplitz(taps, cols, cols, radius, -1).astype(BF16)
     dy = toeplitz(taps, part, span, radius - inner).astype(BF16)
-    scratch = (centre_scr, rows_scr, anchor_scr)
-
-    def x_of(f):
-        return x_ref[f, pl.ds(first, span), :].astype(F32)
-
-    filter_rows(x_of, None, bx, None, dy, frames, inner, *scratch)
+    middle = pl.multiple_of(chip * part, part)
+    total = jnp.zeros((span, cols), F32)
+    for f in range(frames):
+        total = total + x_ref[f, pl.ds(first, span), :].astype(F32)
+    anchor = (total * (1.0 / frames)).astype(BF16)
+    anchor32 = anchor.astype(F32)
+    centre_scr[...] = anchor32
+    centre = centre_scr[pl.ds(inner, part), :]
+    blocks = [anchor]
+    for f in range(frames):
+        blocks.append((x_ref[f, pl.ds(first, span), :].astype(F32) - anchor32).astype(BF16))
+    smooth = contract(jnp.concatenate(blocks, axis=0), bx, 1, 0)
+    high, low = split(smooth[:span])
+    both = contract(dy, jnp.concatenate([high, low], axis=1), 1, 0)
+    anchor_s = centre - both[:, :cols] - both[:, cols:]
+    anchor_out = anchor_s.astype(BF16).astype(F32)
+    anchor_scr[...] = anchor_out
+    left_over = anchor_s - anchor_out
+    for p in range(frames // 2):
+        pair = (2 * p, 2 * p + 1)
+        smooths = [smooth[(f + 1) * span : (f + 2) * span].astype(BF16) for f in pair]
+        both = contract(dy, jnp.concatenate(smooths, axis=1), 1, 0)
+        for i, f in enumerate(pair):
+            block = x_ref[f, pl.ds(middle, part), :].astype(F32) - centre
+            block = block.astype(BF16).astype(F32)
+            value = block - both[:, i * cols : (i + 1) * cols] + left_over
+            rows_scr[pl.ds(f, part, stride=frames), :] = value
     for h, out_ref in enumerate(outs):
         put_block(out_ref, 0, (me + h) % 2, share, rows_scr, anchor_scr)
 
@@ -318,8 +296,8 @@
 
 
 def temporal_kernel(axis, width, ranks, places, *refs):
-    blocks, edge_refs, lhs_ref = refs[3:-8], refs[-8:-6], refs[-6]
-    data_ref, anchor_ref, om_ref, m_ref, gram_ref = refs[-5:]
+    blocks, edge_refs, lhs_ref = refs[3:-9], refs[-9:-7], refs[-7]
+    data_ref, anchor_ref, om_ref, m_ref, gram_ref, turned_ref = refs[-6:]
     share, count, frames, cols = data_ref.shape
     all_frames = count * frames
     slots = share + share // frames
@@ -349,6 +327,8 @@
         m_ref[2 * p + 1] = value[:, cols:]
         gram = gram + contract(value, value, 1, 1)
     gram_ref[...] = gram
+    omega = om_ref[...].reshape(all_frames, cols).astype(F32)
+    turned_ref[...] = omega.T[:ranks]
 
 
 def exact(left, right, left_dim, right_dim):
@@ -401,7 +381,7 @@
     gram = grams[0][...]
     for other in grams[1:]:
         gram = gram + other[...]
-    omega = om_ref[...].reshape(all_frames, om_ref.shape[2]).astype(F32).T[:ranks]
+    omega = om_ref[...]
     sketch = exact(omega, gram, 1, 0)
     (load,) = whiten(exact(sketch, omega, 1, 1), sketch)
     back = exact(load, gram, 1, 0)
@@ -514,12 +494,13 @@
         ],
         [*blocks[:-2], *mains],
     )
-    _, _, om_all, matrix, gram = call(
+    *_, matrix, gram, om_all = call(
         functools.partial(temporal_kernel, "tm", radius, ranks, places[-2:]),
         [
             *[shape(value.shape, value.dtype) for value in known],
             shape((share, all_frames, cols), BF16),
             shape((all_frames, all_frames), F32),
+            shape((ranks, all_frames), F32),
         ],
         [*known, *blocks[-2:], edges, edges_other, lhs],
         aliases={0: 0, 1: 1, 2: 2},

time: 50.7 us -> 49.6 us (0.978)
  Pallas kernels: 9.69 us -> 8.63 us
    pallas_call x7, Pallas kernels: 9.69 us -> 8.63 us  [call(): pl.pallas_call(kernel, out_shape=outs, in_specs=[pl.BlockSpec(memory_spac...]
where the time goes in v6:
time: 49.6 us; the launch traced here: 49.4 us
  waiting for transfers between devices  23.2 us (47%)
  starting transfers between devices  13 us (26%)
  Pallas kernels  8.63 us (17%)
  local copies, waits for them, and re-layouts  3.22 us (6%)
  between operations  0.72 us (1%)
  other arithmetic  0.61 us (1%)
    ppermute x9, waiting for transfers between devices, send(): lax.ppermute(value, 'tm', [(i, device_at(i, count, shift, flip)) for i in...  12.7 us
    ppermute x9, starting transfers between devices, send(): lax.ppermute(value, 'tm', [(i, device_at(i, count, shift, flip)) for i in...  8.74 us
    pallas_call x7, Pallas kernels, call(): pl.pallas_call(kernel, out_shape=outs, in_specs=[pl.BlockSpec(memory_spac...  8.63 us
    ppermute x4, waiting for transfers between devices, swap(): return lax.ppermute(value, 'tm', [(i, i ^ k) for i in range(count)])  8.59 us
    unnamed x8, local copies, waits for them, and re-layouts  3.22 us
    ppermute x1, starting transfers between devices, local(): side_b = lax.ppermute(side_b, 'tile', pairs + [(j, i) for i, j in pairs])  2.37 us
    ppermute x1, waiting for transfers between devices, local(): side_b = lax.ppermute(side_b, 'tile', pairs + [(j, i) for i, j in pairs])  1.91 us
    ppermute x1, starting transfers between devices, local(): side_a = lax.ppermute(side_a, 'tile', pairs)  1.49 us
  transfers between devices with their start and end apart: 15, of which 9 were waited for; matrix products, arithmetic and copies ran while one was open for 0% of the time, Pallas kernels for 9%

profile of v6, /device:TPU:4, one launch (start us, length us, event | category | flops | bytes accessed | tf_op | source)
XLA Modules:
  0.0 49.4 jit_solution(559890395045395021)
XLA Ops:
  0.6 0.0 copy-start
  0.6 1.2 %copy-done = bf16[16,256,128]{2,1,0:T(8,128)(2,1)S(1)} copy-done((bf16[16,256,128]{2,1,0:T(8,128)(2,1)S(1)}, bf16[16,256,128]{2,1,0:T(8,128)(2,1)}, u32[]{:S(2)}) %copy-start) | copy-done | bytes 1048600
  1.9 0.0 copy-start.2
  1.9 0.7 %copy-done.2 = bf16[17]{0:T(256)(128)(2,1)S(1)} copy-done((bf16[17]{0:T(256)(128)(2,1)S(1)}, bf16[17]{0:T(256)(128)(2,1)}, u32[]{:S(2)}) %copy-start.2) | copy-done | bytes 58
  2.5 1.0 %shard_map.59 = (bf16[34,16,128]{2,1,0:T(8,128)(2,1)S(1)}, bf16[34,16,128]{2,1,0:T(8,128)(2,1)S(1)}, bf16[16,8,256]{2,1,0:T(8,128)(2,1)S(1)}, bf16[16,8,256]{2,1,0:T(8,128)(2,1)S(1)}) custom-call(bf16[16,256,128]{2,1,0:T(8,128)(2,1)S(1)} %copy-done, bf16[1,17]{1,0:T(2,128)(2,1)S(1)} %bitcast.13), custom_call_target="tpu_custom_call" | custom-call | tf_op jit(solution)/shard_map/pallas_call | solution.py:18
  3.5 2.6 %collective-permute-start.5 = (bf16[34,16,128]{2,1,0:T(8,128)(2,1)S(1)}, bf16[34,16,128]{2,1,0:T(8,128)(2,1)S(1)}, u32[]{:S(2)}, u32[]{:S(2)}) collective-permute-start(bf16[34,16,128]{2,1,0:T(8,128)(2,1)S(1)} %get-tuple-element.45), channel_id=1, source_target_pairs={{0,4},{1,5},{2,6},{3,7},{4,0},{5,1},{6,2},{7,3},{8,12},{9,13},{10,... | collective-permute-start | bytes 417800 | tf_op jit(solution)/shard_map/ppermute | solution.py:431
  6.1 0.0 collective-permute-start.6
  6.1 1.5 %collective-permute-start = (bf16[16,8,256]{2,1,0:T(8,128)(2,1)S(1)}, bf16[16,8,256]{2,1,0:T(8,128)(2,1)S(1)}, u32[]{:S(2)}, u32[]{:S(2)}) collective-permute-start(bf16[16,8,256]{2,1,0:T(8,128)(2,1)S(1)} %get-tuple-element.33), channel_id=1, source_target_pairs={{0,8},{8,0},{16,24},{24,16},{1,9},{9,1},{17,25},{25,17},{2,10},{10... | collective-permute-start | bytes 196616 | tf_op jit(solution)/shard_map/ppermute | solution.py:451
  7.6 2.4 %collective-permute-start.1 = (bf16[16,8,256]{2,1,0:T(8,128)(2,1)S(1)}, bf16[16,8,256]{2,1,0:T(8,128)(2,1)S(1)}, u32[]{:S(2)}, u32[]{:S(2)}) collective-permute-start(bf16[16,8,256]{2,1,0:T(8,128)(2,1)S(1)} %get-tuple-element.34), channel_id=1, source_target_pairs={{8,16},{16,8},{9,17},{17,9},{10,18},{18,10},{11,19},{19,11},{12,20... | collective-permute-start | bytes 196616 | tf_op jit(solution)/shard_map/ppermute | solution.py:453
  10.0 0.0 copy-start.1
  10.0 0.7 %copy-done.1 = bf16[2,1,32,16]{2,3,1,0:T(8,128)(2,1)S(1)} copy-done((bf16[2,1,32,16]{2,3,1,0:T(8,128)(2,1)S(1)}, bf16[2,1,32,16]{2,3,1,0:T(8,128)(2,1)}, u32[]{:S(2)}) %copy-start.1) | copy-done | bytes 2072
  10.7 0.0 copy-start.3
  10.7 0.7 %copy-done.3 = bf16[17]{0:T(256)(128)(2,1)S(1)} copy-done((bf16[17]{0:T(256)(128)(2,1)S(1)}, bf16[17]{0:T(256)(128)(2,1)}, u32[]{:S(2)}) %copy-start.3) | copy-done | bytes 58
  11.4 1.4 %shard_map.60 = (bf16[16,128]{1,0:T(8,128)(2,1)S(1)}, bf16[256,256]{1,0:T(8,128)(2,1)S(1)}, bf16[128,144]{1,0:T(8,128)(2,1)S(1)}, bf16[2,16,32]{2,1,0:T(8,128)(2...) custom-call(bf16[16,256,128]{2,1,0:T(8,128)(2,1)S(1)} %copy-done, ...), custom_call_target="tpu_custom_call" | custom-call | tf_op jit(solution)/shard_map/pallas_call | solution.py:18
  12.7 0.0 collective-permute-done.a_ref
  12.8 1.9 %collective-permute-done.1.b_ref = bf16[16,8,256]{2,1,0:T(8,128)(2,1)S(1)} collective-permute-done((bf16[16,8,256]{2,1,0:T(8,128)(2,1)S(1)}, bf16[16,8,256]{2,1,0:T(8,128)(2,1)S(1)}, u32[]{:S(2)}, u32[]{:S(2)}) %collective-permute-start.1) | collective-permute-done | bytes 65568 | tf_op jit(solution)/shard_map/ppermute | solution.py:453
  14.7 1.7 %shard_map.61 = (bf16[35,16,128]{2,1,0:T(8,128)(2,1)S(1)}, bf16[35,16,128]{2,1,0:T(8,128)(2,1)S(1)}, bf16[35,16,128]{2,1,0:T(8,128)(2,1)S(1)}, bf16[35,16,128]{2...) custom-call(bf16[16,8,256]{2,1,0:T(8,128)(2,1)S(1)} %collective-perm, ...), custom_call_target="tpu_custom_call" | custom-call | tf_op jit(solution)/shard_map/pallas_call | solution.py:18
  16.4 0.1 collective-permute-start.2
  16.4 1.6 %collective-permute-start.3 = (bf16[35,16,128]{2,1,0:T(8,128)(2,1)S(1)}, bf16[35,16,128]{2,1,0:T(8,128)(2,1)S(1)}, u32[]{:S(2)}, u32[]{:S(2)}) collective-permute-start(bf16[35,16,128]{2,1,0:T(8,128)(2,1)S(1)} %get-tuple-element.43), channel_id=1, source_target_pairs={{0,2},{1,3},{2,4},{3,5},{4,6},{5,7},{6,0},{7,1},{8,10},{9,11},{10,... | collective-permute-start | bytes 430088 | tf_op jit(solution)/shard_map/ppermute | solution.py:431
  18.1 1.2 %collective-permute-start.4 = (bf16[35,16,128]{2,1,0:T(8,128)(2,1)S(1)}, bf16[35,16,128]{2,1,0:T(8,128)(2,1)S(1)}, u32[]{:S(2)}, u32[]{:S(2)}) collective-permute-start(bf16[35,16,128]{2,1,0:T(8,128)(2,1)S(1)} %get-tuple-element.44), channel_id=1, source_target_pairs={{0,3},{1,2},{2,5},{3,4},{4,7},{5,6},{6,1},{7,0},{8,11},{9,10},{10,... | collective-permute-start | bytes 430088 | tf_op jit(solution)/shard_map/ppermute | solution.py:431
  19.3 0.0 collective-permute-done.5.refs_4_
  19.3 2.4 %collective-permute-start.7 = (bf16[35,16,128]{2,1,0:T(8,128)(2,1)S(1)}, bf16[35,16,128]{2,1,0:T(8,128)(2,1)S(1)}, u32[]{:S(2)}, u32[]{:S(2)}) collective-permute-start(bf16[35,16,128]{2,1,0:T(8,128)(2,1)S(1)} %get-tuple-element.50), channel_id=1, source_target_pairs={{0,6},{1,7},{2,0},{3,1},{4,2},{5,3},{6,4},{7,5},{8,14},{9,15},{10,... | collective-permute-start | bytes 430088 | tf_op jit(solution)/shard_map/ppermute | solution.py:431
  21.7 0.0 collective-permute-done.6.refs_5_
  21.7 0.2 collective-permute-start.8
  21.9 0.0 collective-permute-done.2.refs_1_
  21.9 0.6 %collective-permute-start.9 = (bf16[5,16,128]{2,1,0:T(8,128)(2,1)S(1)}, bf16[5,16,128]{2,1,0:T(8,128)(2,1)S(1)}, u32[]{:S(2)}, u32[]{:S(2)}) collective-permute-start(bf16[5,16,128]{2,1,0:T(8,128)(2,1)S(1)} %get-tuple-element.54), channel_id=1, source_target_pairs={{0,4},{1,5},{2,6},{3,7},{4,0},{5,1},{6,2},{7,3},{8,12},{9,13},{10,... | collective-permute-start | bytes 61448 | tf_op jit(solution)/shard_map/ppermute | solution.py:431
  22.5 2.5 %collective-permute-done.3.refs_2_ = bf16[35,16,128]{2,1,0:T(8,128)(2,1)S(1)} collective-permute-done((bf16[35,16,128]{2,1,0:T(8,128)(2,1)S(1)}, bf16[35,16,128]{2,1,0:T(8,128)(2,1)S(1)}, u32[]{:S(2)}, u32[]{:S(2)}) %collective-permute-start.3) | collective-permute-done | bytes 143392 | tf_op jit(solution)/shard_map/ppermute | solution.py:431
  25.0 0.0 collective-permute-start.10
  25.0 2.2 %collective-permute-done.4.refs_3_ = bf16[35,16,128]{2,1,0:T(8,128)(2,1)S(1)} collective-permute-done((bf16[35,16,128]{2,1,0:T(8,128)(2,1)S(1)}, bf16[35,16,128]{2,1,0:T(8,128)(2,1)S(1)}, u32[]{:S(2)}, u32[]{:S(2)}) %collective-permute-start.4) | collective-permute-done | bytes 143392 | tf_op jit(solution)/shard_map/ppermute | solution.py:431
  27.2 0.1 shard_map.62
  27.3 3.3 %collective-permute-done.7.refs_3_ = bf16[35,16,128]{2,1,0:T(8,128)(2,1)S(1)} collective-permute-done((bf16[35,16,128]{2,1,0:T(8,128)(2,1)S(1)}, bf16[35,16,128]{2,1,0:T(8,128)(2,1)S(1)}, u32[]{:S(2)}, u32[]{:S(2)}) %collective-permute-start.7) | collective-permute-done | bytes 143392 | tf_op jit(solution)/shard_map/ppermute | solution.py:431
  30.6 4.4 %collective-permute-done.9.refs_5_ = bf16[5,16,128]{2,1,0:T(8,128)(2,1)S(1)} collective-permute-done((bf16[5,16,128]{2,1,0:T(8,128)(2,1)S(1)}, bf16[5,16,128]{2,1,0:T(8,128)(2,1)S(1)}, u32[]{:S(2)}, u32[]{:S(2)}) %collective-permute-start.9) | collective-permute-done | bytes 20512 | tf_op jit(solution)/shard_map/ppermute | solution.py:431
  35.0 0.3 collective-permute-done.10.refs_6_
  35.3 0.0 collective-permute-done.8.refs_4_
  35.3 1.1 %shard_map.63 = (bf16[32,8,16,128]{3,2,1,0:T(8,128)(2,1)S(1)}, f32[256,128]{1,0:T(8,128)S(1)}, bf16[8,16,128]{2,1,0:T(8,128)(2,1)S(1)}, bf16[32,128,128]{2,1,0:T...) custom-call(bf16[32,8,16,128]{3,2,1,0:T(8,128)(2,1)S(1)} %get-tuple-, ...), custom_call_target="tpu_custom_call", output_to_operand_aliasing={{0}: (0, {}), {1}: (1, {}), {2}: (2, {})} | custom-call | tf_op jit(solution)/shard_map/pallas_call | solution.py:18
  36.5 0.1 collective-permute-start.11
  36.5 0.2 collective-permute-start.12
  36.7 4.1 %collective-permute-done.11.refs_1_ = f32[128,128]{1,0:T(8,128)S(1)} collective-permute-done((f32[128,128]{1,0:T(8,128)S(1)}, f32[128,128]{1,0:T(8,128)S(1)}, u32[]{:S(2)}, u32[]{:S(2)}) %collective-permute-start.11) | collective-permute-done | bytes 65568 | tf_op jit(solution)/shard_map/ppermute | solution.py:428
  40.8 0.0 collective-permute-start.13
  40.8 0.0 collective-permute-done.12.refs_2_
  40.8 1.2 %collective-permute-done.13.refs_3_ = f32[128,128]{1,0:T(8,128)S(1)} collective-permute-done((f32[128,128]{1,0:T(8,128)S(1)}, f32[128,128]{1,0:T(8,128)S(1)}, u32[]{:S(2)}, u32[]{:S(2)}) %collective-permute-start.13) | collective-permute-done | bytes 65568 | tf_op jit(solution)/shard_map/ppermute | solution.py:428
  42.0 2.0 %shard_map.64 = (f32[32,128]{1,0:T(8,128)S(1)}, f32[2,16,32]{2,1,0:T(8,128)S(1)}, f32[2,16,32]{2,1,0:T(8,128)S(1)}) custom-call(f32[32,128]{1,0:T(8,128)S(1)} %get-tuple-element.59.om_ref, f32[128,128]{1,0:T(8,128)S(1)} %get-tuple-element.60.refs_0_, f32[128,128]{1,0:T(8,128)S(1)} %collective-permute-done.11.refs_1_, ...), custom_call_target="tpu_custom_call" | custom-call | tf_op jit(solution)/shard_map/pallas_call | solution.py:18
  44.1 0.2 collective-permute-start.14
  44.2 1.3 %shard_map.65 = f32[1024,128]{1,0:T(8,128)} custom-call(bf16[32,128,128]{2,1,0:T(8,128)(2,1)S(1)} %get-tuple-element.58.m_ref, f32[32,128]{1,0:T(8,128)S(1)} %get-tuple-element.61.mix_ref), custom_call_target="tpu_custom_call" | custom-call | tf_op jit(solution)/shard_map/pallas_call | solution.py:18
  45.5 3.3 %collective-permute-done.14 = f32[2,16,32]{2,1,0:T(8,128)S(1)} collective-permute-done((f32[2,16,32]{2,1,0:T(8,128)S(1)}, f32[2,16,32]{2,1,0:T(8,128)S(1)}, u32[]{:S(2)}, u32[]{:S(2)}) %collective-permute-start.14) | collective-permute-done | bytes 4128 | tf_op jit(solution)/shard_map/ppermute | solution.py:428
  48.8 0.6 %add_bitcast_fusion = f32[2,1,32,16]{2,3,1,0:T(8,128)} fusion(f32[2,16,32]{2,1,0:T(8,128)S(1)} %get-tuple-element.62, f32[2,16,32]{2,1,0:T(8,128)S(1)} %collective-permute-done.14), kind=kLoop, calls=%fused_computation | loop fusion | flops 1024 | bytes 12288
Async XLA Ops:
  0.6 1.2 %copy-start = (bf16[16,256,128]{2,1,0:T(8,128)(2,1)S(1)}, bf16[16,256,128]{2,1,0:T(8,128)(2,1)}, u32[]{:S(2)}) copy-start(bf16[16,256,128]{2,1,0:T(8,128)(2,1)} %x_ref.3) | copy-start | bytes 3145732
  1.9 0.7 %copy-start.2 = (bf16[17]{0:T(256)(128)(2,1)S(1)}, bf16[17]{0:T(256)(128)(2,1)}, u32[]{:S(2)}) copy-start(bf16[17]{0:T(256)(128)(2,1)} %param.7) | copy-start | bytes 106
  3.5 15.8 %collective-permute-start.5 = (bf16[34,16,128]{2,1,0:T(8,128)(2,1)S(1)}, bf16[34,16,128]{2,1,0:T(8,128)(2,1)S(1)}, u32[]{:S(2)}, u32[]{:S(2)}) collective-permute-start(bf16[34,16,128]{2,1,0:T(8,128)(2,1)S(1)} %get-tuple-element.45), channel_id=1, source_target_pairs={{0,4},{1,5},{2,6},{3,7},{4,0},{5,1},{6,2},{7,3},{8,12},{9,13},{10,... | collective-permute-start | bytes 417800 | tf_op jit(solution)/shard_map/ppermute | solution.py:431
  6.1 15.5 %collective-permute-start.6 = (bf16[34,16,128]{2,1,0:T(8,128)(2,1)S(1)}, bf16[34,16,128]{2,1,0:T(8,128)(2,1)S(1)}, u32[]{:S(2)}, u32[]{:S(2)}) collective-permute-start(bf16[34,16,128]{2,1,0:T(8,128)(2,1)S(1)} %get-tuple-element.46), channel_id=1, source_target_pairs={{0,5},{1,4},{2,7},{3,6},{4,1},{5,0},{6,3},{7,2},{8,13},{9,12},{10,... | collective-permute-start | bytes 417800 | tf_op jit(solution)/shard_map/ppermute | solution.py:431
  6.1 6.6 %collective-permute-start = (bf16[16,8,256]{2,1,0:T(8,128)(2,1)S(1)}, bf16[16,8,256]{2,1,0:T(8,128)(2,1)S(1)}, u32[]{:S(2)}, u32[]{:S(2)}) collective-permute-start(bf16[16,8,256]{2,1,0:T(8,128)(2,1)S(1)} %get-tuple-element.33), channel_id=1, source_target_pairs={{0,8},{8,0},{16,24},{24,16},{1,9},{9,1},{17,25},{25,17},{2,10},{10... | collective-permute-start | bytes 196616 | tf_op jit(solution)/shard_map/ppermute | solution.py:451
  7.6 7.0 %collective-permute-start.1 = (bf16[16,8,256]{2,1,0:T(8,128)(2,1)S(1)}, bf16[16,8,256]{2,1,0:T(8,128)(2,1)S(1)}, u32[]{:S(2)}, u32[]{:S(2)}) collective-permute-start(bf16[16,8,256]{2,1,0:T(8,128)(2,1)S(1)} %get-tuple-element.34), channel_id=1, source_target_pairs={{8,16},{16,8},{9,17},{17,9},{10,18},{18,10},{11,19},{19,11},{12,20... | collective-permute-start | bytes 196616 | tf_op jit(solution)/shard_map/ppermute | solution.py:453
  10.0 0.7 %copy-start.1 = (bf16[2,1,32,16]{2,3,1,0:T(8,128)(2,1)S(1)}, bf16[2,1,32,16]{2,3,1,0:T(8,128)(2,1)}, u32[]{:S(2)}) copy-start(bf16[2,1,32,16]{2,3,1,0:T(8,128)(2,1)} %param.5) | copy-start | bytes 6148
  10.7 0.7 %copy-start.3 = (bf16[17]{0:T(256)(128)(2,1)S(1)}, bf16[17]{0:T(256)(128)(2,1)}, u32[]{:S(2)}) copy-start(bf16[17]{0:T(256)(128)(2,1)} %param.6) | copy-start | bytes 106
  16.4 5.6 %collective-permute-start.2 = (bf16[35,16,128]{2,1,0:T(8,128)(2,1)S(1)}, bf16[35,16,128]{2,1,0:T(8,128)(2,1)S(1)}, u32[]{:S(2)}, u32[]{:S(2)}) collective-permute-start(bf16[35,16,128]{2,1,0:T(8,128)(2,1)S(1)} %get-tuple-element.42), channel_id=1, source_target_pairs={{0,1},{1,0},{2,3},{3,2},{4,5},{5,4},{6,7},{7,6},{8,9},{9,8},{10,11... | collective-permute-start | bytes 430088 | tf_op jit(solution)/shard_map/ppermute | solution.py:431
  16.4 8.6 %collective-permute-start.3 = (bf16[35,16,128]{2,1,0:T(8,128)(2,1)S(1)}, bf16[35,16,128]{2,1,0:T(8,128)(2,1)S(1)}, u32[]{:S(2)}, u32[]{:S(2)}) collective-permute-start(bf16[35,16,128]{2,1,0:T(8,128)(2,1)S(1)} %get-tuple-element.43), channel_id=1, source_target_pairs={{0,2},{1,3},{2,4},{3,5},{4,6},{5,7},{6,0},{7,1},{8,10},{9,11},{10,... | collective-permute-start | bytes 430088 | tf_op jit(solution)/shard_map/ppermute | solution.py:431
  18.1 9.1 %collective-permute-start.4 = (bf16[35,16,128]{2,1,0:T(8,128)(2,1)S(1)}, bf16[35,16,128]{2,1,0:T(8,128)(2,1)S(1)}, u32[]{:S(2)}, u32[]{:S(2)}) collective-permute-start(bf16[35,16,128]{2,1,0:T(8,128)(2,1)S(1)} %get-tuple-element.44), channel_id=1, source_target_pairs={{0,3},{1,2},{2,5},{3,4},{4,7},{5,6},{6,1},{7,0},{8,11},{9,10},{10,... | collective-permute-start | bytes 430088 | tf_op jit(solution)/shard_map/ppermute | solution.py:431
  19.3 11.3 %collective-permute-start.7 = (bf16[35,16,128]{2,1,0:T(8,128)(2,1)S(1)}, bf16[35,16,128]{2,1,0:T(8,128)(2,1)S(1)}, u32[]{:S(2)}, u32[]{:S(2)}) collective-permute-start(bf16[35,16,128]{2,1,0:T(8,128)(2,1)S(1)} %get-tuple-element.50), channel_id=1, source_target_pairs={{0,6},{1,7},{2,0},{3,1},{4,2},{5,3},{6,4},{7,5},{8,14},{9,15},{10,... | collective-permute-start | bytes 430088 | tf_op jit(solution)/shard_map/ppermute | solution.py:431
  21.7 13.6 %collective-permute-start.8 = (bf16[35,16,128]{2,1,0:T(8,128)(2,1)S(1)}, bf16[35,16,128]{2,1,0:T(8,128)(2,1)S(1)}, u32[]{:S(2)}, u32[]{:S(2)}) collective-permute-start(bf16[35,16,128]{2,1,0:T(8,128)(2,1)S(1)} %get-tuple-element.52), channel_id=1, source_target_pairs={{0,7},{1,6},{2,1},{3,0},{4,3},{5,2},{6,5},{7,4},{8,15},{9,14},{10,... | collective-permute-start | bytes 430088 | tf_op jit(solution)/shard_map/ppermute | solution.py:431
  21.9 13.1 %collective-permute-start.9 = (bf16[5,16,128]{2,1,0:T(8,128)(2,1)S(1)}, bf16[5,16,128]{2,1,0:T(8,128)(2,1)S(1)}, u32[]{:S(2)}, u32[]{:S(2)}) collective-permute-start(bf16[5,16,128]{2,1,0:T(8,128)(2,1)S(1)} %get-tuple-element.54), channel_id=1, source_target_pairs={{0,4},{1,5},{2,6},{3,7},{4,0},{5,1},{6,2},{7,3},{8,12},{9,13},{10,... | collective-permute-start | bytes 61448 | tf_op jit(solution)/shard_map/ppermute | solution.py:431
  25.0 10.3 %collective-permute-start.10 = (bf16[5,16,128]{2,1,0:T(8,128)(2,1)S(1)}, bf16[5,16,128]{2,1,0:T(8,128)(2,1)S(1)}, u32[]{:S(2)}, u32[]{:S(2)}) collective-permute-start(bf16[5,16,128]{2,1,0:T(8,128)(2,1)S(1)} %get-tuple-element.56), channel_id=1, source_target_pairs={{0,5},{1,4},{2,7},{3,6},{4,1},{5,0},{6,3},{7,2},{8,13},{9,12},{10,... | collective-permute-start | bytes 61448 | tf_op jit(solution)/shard_map/ppermute | solution.py:431
  36.5 4.3 %collective-permute-start.11 = (f32[128,128]{1,0:T(8,128)S(1)}, f32[128,128]{1,0:T(8,128)S(1)}, u32[]{:S(2)}, u32[]{:S(2)}) collective-permute-start(f32[128,128]{1,0:T(8,128)S(1)} %get-tuple-element.60.refs_0_), channel_id=1, source_target_pairs={{0,2},{1,3},{2,0},{3,1},{4,6},{5,7},{6,4},{7,5},{8,10},{9,11},{10,... | collective-permute-start | bytes 196616 | tf_op jit(solution)/shard_map/ppermute | solution.py:428
  36.5 4.3 %collective-permute-start.12 = (f32[128,128]{1,0:T(8,128)S(1)}, f32[128,128]{1,0:T(8,128)S(1)}, u32[]{:S(2)}, u32[]{:S(2)}) collective-permute-start(f32[128,128]{1,0:T(8,128)S(1)} %get-tuple-element.60.refs_0_), channel_id=1, source_target_pairs={{0,1},{1,0},{2,3},{3,2},{4,5},{5,4},{6,7},{7,6},{8,9},{9,8},{10,11... | collective-permute-start | bytes 196616 | tf_op jit(solution)/shard_map/ppermute | solution.py:428
  40.8 1.3 %collective-permute-start.13 = (f32[128,128]{1,0:T(8,128)S(1)}, f32[128,128]{1,0:T(8,128)S(1)}, u32[]{:S(2)}, u32[]{:S(2)}) collective-permute-start(f32[128,128]{1,0:T(8,128)S(1)} %collective-permute-done.11.refs_1_), channel_id=1, source_target_pairs={{0,1},{1,0},{2,3},{3,2},{4,5},{5,4},{6,7},{7,6},{8,9},{9,8},{10,11... | collective-permute-start | bytes 196616 | tf_op jit(solution)/shard_map/ppermute | solution.py:428
  44.1 4.7 %collective-permute-start.14 = (f32[2,16,32]{2,1,0:T(8,128)S(1)}, f32[2,16,32]{2,1,0:T(8,128)S(1)}, u32[]{:S(2)}, u32[]{:S(2)}) collective-permute-start(f32[2,16,32]{2,1,0:T(8,128)S(1)} %get-tuple-element.63), channel_id=1, source_target_pairs={{0,4},{1,5},{2,6},{3,7},{4,0},{5,1},{6,2},{7,3},{8,12},{9,13},{10,... | collective-permute-start | bytes 12296 | tf_op jit(solution)/shard_map/ppermute | solution.py:428

commit v7 on v6

--- a/solution.py
+++ b/solution.py
@@ -205,7 +205,7 @@
 
 def spatial_kernel(axis, a_ref, b_ref, bh_ref, dy_ref, om_ref, *rest):
     (anchor_ref, block_ref, smooth_ref), rest = rest[:3], rest[3:]
-    outs, edge_refs, (rows_scr, anchor_scr) = rest[:-4], rest[-4:-2], rest[-2:]
+    outs, edge_refs, (rows_scr, anchor_scr, smooth_scr) = rest[:-5], rest[-5:-3], rest[-3:]
     frames, rows, cols = block_ref.shape
     radius = a_ref.shape[1]
     share = (outs[0].shape[0] - 1) * frames // (frames + 1)
@@ -224,6 +224,8 @@
         total = total + halo(f)
     edge_anchor = (total * (1.0 / frames)).astype(BF16)
     edge32 = edge_anchor.astype(F32)
+    for f in range(frames):
+        smooth_scr[f] = across(f, (halo(f) - edge32).astype(BF16)).astype(BF16)
     high, low = split(across(frames, edge_anchor))
     both = contract(dy, jnp.concatenate([high, low], axis=1), 1, 0)
     anchor_s = anchor_ref[...] - both[:, :cols] - both[:, cols:]
@@ -232,8 +234,7 @@
     left_over = anchor_s - anchor_out
     for p in range(frames // 2):
         pair = (2 * p, 2 * p + 1)
-        smooths = [across(f, (halo(f) - edge32).astype(BF16)).astype(BF16) for f in pair]
-        both = contract(dy, jnp.concatenate(smooths, axis=1), 1, 0)
+        both = contract(dy, jnp.concatenate([smooth_scr[f] for f in pair], axis=1), 1, 0)
         for i, f in enumerate(pair):
             value = block_ref[f].astype(F32) - both[:, i * cols : (i + 1) * cols] + left_over
             rows_scr[pl.ds(f, rows, stride=frames), :] = value
@@ -353,7 +354,7 @@
         ]
         for j in range(start, start + panel):
             inverse = 1.0 / cols[j - start][j : j + 1]
-            factor = jnp.where(ids > j, cols[j - start] * inverse, 0.0)
+            factor = jnp.where(ids > j, cols[j - start], 0.0) * inverse
             scale = jnp.where(ids == j, inverse, scale)
             for m in range(j - start + 1, panel):
                 cols[m] = cols[m] - factor * cols[m][j : j + 1]
@@ -430,7 +431,7 @@
     def send(value, shift, flip):
         return lax.ppermute(value, "tm", [(i, device_at(i, count, shift, flip)) for i in range(count)])
 
-    space_row, time_row = space_taps[None], time_taps[None]
+    space_row, time_row = space_taps.astype(F32)[None], time_taps[None]
     part = 2 * share
     span = part + 32
     *mains, side_a, side_b = call(
@@ -473,7 +474,11 @@
             *([shape((share // packed + 1, frames, cols), BF16)] * 2),
         ],
         [side_a, side_b, bh, dy, om, *prepared],
-        [pltpu.VMEM((rows * frames, cols), F32), pltpu.VMEM((rows, cols), F32)],
+        [
+            pltpu.VMEM((rows * frames, cols), F32),
+            pltpu.VMEM((rows, cols), F32),
+            pltpu.VMEM(movie.shape, BF16),
+        ],
     )
     def after(value, *others):
         return lax.optimization_barrier((value, *others))[0]

time: 49.6 us -> 49.6 us (level)
  other arithmetic: 0.61 us -> 1.27 us
  local copies, waits for them, and re-layouts: 3.22 us -> 2.57 us
    broadcast_in_dim x0 -> x1, other arithmetic: none -> 0.66 us  [local(): space_row, time_row = (space_taps.astype(F32)[None], time_taps[None])]
    unnamed x8 -> x6, local copies, waits for them, and re-layouts: 3.22 us -> 2.57 us
where the time goes in v7:
time: 49.6 us; the launch traced here: 49.3 us
  waiting for transfers between devices  23.2 us (47%)
  starting transfers between devices  13 us (26%)
  Pallas kernels  8.55 us (17%)
  local copies, waits for them, and re-layouts  2.57 us (5%)
  other arithmetic  1.27 us (3%)
  between operations  0.72 us (1%)
    ppermute x9, waiting for transfers between devices, send(): lax.ppermute(value, 'tm', [(i, device_at(i, count, shift, flip)) for i in...  12.7 us
    ppermute x9, starting transfers between devices, send(): lax.ppermute(value, 'tm', [(i, device_at(i, count, shift, flip)) for i in...  8.74 us
    ppermute x4, waiting for transfers between devices, swap(): return lax.ppermute(value, 'tm', [(i, i ^ k) for i in range(count)])  8.59 us
    pallas_call x7, Pallas kernels, call(): pl.pallas_call(kernel, out_shape=outs, in_specs=[pl.BlockSpec(memory_spac...  8.55 us
    unnamed x6, local copies, waits for them, and re-layouts  2.57 us
    ppermute x1, starting transfers between devices, local(): side_b = lax.ppermute(side_b, 'tile', pairs + [(j, i) for i, j in pairs])  2.38 us
    ppermute x1, waiting for transfers between devices, local(): side_b = lax.ppermute(side_b, 'tile', pairs + [(j, i) for i, j in pairs])  1.95 us
    ppermute x1, starting transfers between devices, local(): side_a = lax.ppermute(side_a, 'tile', pairs)  1.49 us
  transfers between devices with their start and end apart: 15, of which 9 were waited for; matrix products, arithmetic and copies ran while one was open for 0% of the time, Pallas kernels for 9%

profile of v7, /device:TPU:4, one launch (start us, length us, event | category | flops | bytes accessed | tf_op | source)
XLA Modules:
  0.0 49.3 jit_solution(11572632950721054556)
XLA Ops:
  0.6 0.7 %bitcast_convert_fusion.taps_ref.space_ref = f32[1,17]{1,0:T(1,128)S(1)} fusion(bf16[17]{0:T(256)(128)(2,1)} %param.7), kind=kLoop, calls=%fused_computation.1 | loop fusion | flops 17 | bytes 102 | tf_op jit(solution)/shard_map/broadcast_in_dim | solution.py:434
  1.3 0.0 copy-start
  1.3 1.2 %copy-done = bf16[16,256,128]{2,1,0:T(8,128)(2,1)S(1)} copy-done((bf16[16,256,128]{2,1,0:T(8,128)(2,1)S(1)}, bf16[16,256,128]{2,1,0:T(8,128)(2,1)}, u32[]{:S(2)}) %copy-start) | copy-done | bytes 1048600
  2.5 1.0 %shard_map.59 = (bf16[34,16,128]{2,1,0:T(8,128)(2,1)S(1)}, bf16[34,16,128]{2,1,0:T(8,128)(2,1)S(1)}, bf16[16,8,256]{2,1,0:T(8,128)(2,1)S(1)}, bf16[16,8,256]{2,1,0:T(8,128)(2,1)S(1)}) custom-call(bf16[16,256,128]{2,1,0:T(8,128)(2,1)S(1)} %copy-done, f32[1,17]{1,0:T(1,128)S(1)} %bitcast_convert_fusion.taps_ref.space_ref), custom_call_target="tpu_custom_call" | custom-call | tf_op jit(solution)/shard_map/pallas_call | solution.py:18
  3.5 2.6 %collective-permute-start.5 = (bf16[34,16,128]{2,1,0:T(8,128)(2,1)S(1)}, bf16[34,16,128]{2,1,0:T(8,128)(2,1)S(1)}, u32[]{:S(2)}, u32[]{:S(2)}) collective-permute-start(bf16[34,16,128]{2,1,0:T(8,128)(2,1)S(1)} %get-tuple-element.45), channel_id=1, source_target_pairs={{0,4},{1,5},{2,6},{3,7},{4,0},{5,1},{6,2},{7,3},{8,12},{9,13},{10,... | collective-permute-start | bytes 417800 | tf_op jit(solution)/shard_map/ppermute | solution.py:432
  6.1 0.0 collective-permute-start.6
  6.1 1.5 %collective-permute-start = (bf16[16,8,256]{2,1,0:T(8,128)(2,1)S(1)}, bf16[16,8,256]{2,1,0:T(8,128)(2,1)S(1)}, u32[]{:S(2)}, u32[]{:S(2)}) collective-permute-start(bf16[16,8,256]{2,1,0:T(8,128)(2,1)S(1)} %get-tuple-element.33), channel_id=1, source_target_pairs={{0,8},{8,0},{16,24},{24,16},{1,9},{9,1},{17,25},{25,17},{2,10},{10... | collective-permute-start | bytes 196616 | tf_op jit(solution)/shard_map/ppermute | solution.py:452
  7.6 2.4 %collective-permute-start.1 = (bf16[16,8,256]{2,1,0:T(8,128)(2,1)S(1)}, bf16[16,8,256]{2,1,0:T(8,128)(2,1)S(1)}, u32[]{:S(2)}, u32[]{:S(2)}) collective-permute-start(bf16[16,8,256]{2,1,0:T(8,128)(2,1)S(1)} %get-tuple-element.34), channel_id=1, source_target_pairs={{8,16},{16,8},{9,17},{17,9},{10,18},{18,10},{11,19},{19,11},{12,20... | collective-permute-start | bytes 196616 | tf_op jit(solution)/shard_map/ppermute | solution.py:454
  10.0 0.0 copy-start.1
  10.0 0.7 %copy-done.1 = bf16[2,1,32,16]{2,3,1,0:T(8,128)(2,1)S(1)} copy-done((bf16[2,1,32,16]{2,3,1,0:T(8,128)(2,1)S(1)}, bf16[2,1,32,16]{2,3,1,0:T(8,128)(2,1)}, u32[]{:S(2)}) %copy-start.1) | copy-done | bytes 2072
  10.7 0.0 copy-start.2
  10.7 0.7 %copy-done.2 = bf16[17]{0:T(256)(128)(2,1)S(1)} copy-done((bf16[17]{0:T(256)(128)(2,1)S(1)}, bf16[17]{0:T(256)(128)(2,1)}, u32[]{:S(2)}) %copy-start.2) | copy-done | bytes 58
  11.3 1.3 %shard_map.60 = (bf16[16,128]{1,0:T(8,128)(2,1)S(1)}, bf16[256,256]{1,0:T(8,128)(2,1)S(1)}, bf16[128,144]{1,0:T(8,128)(2,1)S(1)}, bf16[2,16,32]{2,1,0:T(8,128)(2...) custom-call(bf16[16,256,128]{2,1,0:T(8,128)(2,1)S(1)} %copy-done, ...), custom_call_target="tpu_custom_call" | custom-call | tf_op jit(solution)/shard_map/pallas_call | solution.py:18
  12.7 0.0 collective-permute-done.a_ref
  12.7 1.9 %collective-permute-done.1.b_ref = bf16[16,8,256]{2,1,0:T(8,128)(2,1)S(1)} collective-permute-done((bf16[16,8,256]{2,1,0:T(8,128)(2,1)S(1)}, bf16[16,8,256]{2,1,0:T(8,128)(2,1)S(1)}, u32[]{:S(2)}, u32[]{:S(2)}) %collective-permute-start.1) | collective-permute-done | bytes 65568 | tf_op jit(solution)/shard_map/ppermute | solution.py:454
  14.6 1.7 %shard_map.61 = (bf16[35,16,128]{2,1,0:T(8,128)(2,1)S(1)}, bf16[35,16,128]{2,1,0:T(8,128)(2,1)S(1)}, bf16[35,16,128]{2,1,0:T(8,128)(2,1)S(1)}, bf16[35,16,128]{2...) custom-call(bf16[16,8,256]{2,1,0:T(8,128)(2,1)S(1)} %collective-perm, ...), custom_call_target="tpu_custom_call" | custom-call | tf_op jit(solution)/shard_map/pallas_call | solution.py:18
  16.3 0.1 collective-permute-start.2
  16.4 1.6 %collective-permute-start.3 = (bf16[35,16,128]{2,1,0:T(8,128)(2,1)S(1)}, bf16[35,16,128]{2,1,0:T(8,128)(2,1)S(1)}, u32[]{:S(2)}, u32[]{:S(2)}) collective-permute-start(bf16[35,16,128]{2,1,0:T(8,128)(2,1)S(1)} %get-tuple-element.43), channel_id=1, source_target_pairs={{0,2},{1,3},{2,4},{3,5},{4,6},{5,7},{6,0},{7,1},{8,10},{9,11},{10,... | collective-permute-start | bytes 430088 | tf_op jit(solution)/shard_map/ppermute | solution.py:432
  18.1 1.2 %collective-permute-start.4 = (bf16[35,16,128]{2,1,0:T(8,128)(2,1)S(1)}, bf16[35,16,128]{2,1,0:T(8,128)(2,1)S(1)}, u32[]{:S(2)}, u32[]{:S(2)}) collective-permute-start(bf16[35,16,128]{2,1,0:T(8,128)(2,1)S(1)} %get-tuple-element.44), channel_id=1, source_target_pairs={{0,3},{1,2},{2,5},{3,4},{4,7},{5,6},{6,1},{7,0},{8,11},{9,10},{10,... | collective-permute-start | bytes 430088 | tf_op jit(solution)/shard_map/ppermute | solution.py:432
  19.3 0.0 collective-permute-done.5.refs_4_
  19.3 2.4 %collective-permute-start.7 = (bf16[35,16,128]{2,1,0:T(8,128)(2,1)S(1)}, bf16[35,16,128]{2,1,0:T(8,128)(2,1)S(1)}, u32[]{:S(2)}, u32[]{:S(2)}) collective-permute-start(bf16[35,16,128]{2,1,0:T(8,128)(2,1)S(1)} %get-tuple-element.50), channel_id=1, source_target_pairs={{0,6},{1,7},{2,0},{3,1},{4,2},{5,3},{6,4},{7,5},{8,14},{9,15},{10,... | collective-permute-start | bytes 430088 | tf_op jit(solution)/shard_map/ppermute | solution.py:432
  21.7 0.0 collective-permute-done.6.refs_5_
  21.7 0.2 collective-permute-start.8
  21.9 0.0 collective-permute-done.2.refs_1_
  21.9 0.6 %collective-permute-start.9 = (bf16[5,16,128]{2,1,0:T(8,128)(2,1)S(1)}, bf16[5,16,128]{2,1,0:T(8,128)(2,1)S(1)}, u32[]{:S(2)}, u32[]{:S(2)}) collective-permute-start(bf16[5,16,128]{2,1,0:T(8,128)(2,1)S(1)} %get-tuple-element.54), channel_id=1, source_target_pairs={{0,4},{1,5},{2,6},{3,7},{4,0},{5,1},{6,2},{7,3},{8,12},{9,13},{10,... | collective-permute-start | bytes 61448 | tf_op jit(solution)/shard_map/ppermute | solution.py:432
  22.5 2.5 %collective-permute-done.3.refs_2_ = bf16[35,16,128]{2,1,0:T(8,128)(2,1)S(1)} collective-permute-done((bf16[35,16,128]{2,1,0:T(8,128)(2,1)S(1)}, bf16[35,16,128]{2,1,0:T(8,128)(2,1)S(1)}, u32[]{:S(2)}, u32[]{:S(2)}) %collective-permute-start.3) | collective-permute-done | bytes 143392 | tf_op jit(solution)/shard_map/ppermute | solution.py:432
  25.0 0.0 collective-permute-start.10
  25.0 2.2 %collective-permute-done.4.refs_3_ = bf16[35,16,128]{2,1,0:T(8,128)(2,1)S(1)} collective-permute-done((bf16[35,16,128]{2,1,0:T(8,128)(2,1)S(1)}, bf16[35,16,128]{2,1,0:T(8,128)(2,1)S(1)}, u32[]{:S(2)}, u32[]{:S(2)}) %collective-permute-start.4) | collective-permute-done | bytes 143392 | tf_op jit(solution)/shard_map/ppermute | solution.py:432
  27.2 0.1 shard_map.62
  27.3 3.3 %collective-permute-done.7.refs_3_ = bf16[35,16,128]{2,1,0:T(8,128)(2,1)S(1)} collective-permute-done((bf16[35,16,128]{2,1,0:T(8,128)(2,1)S(1)}, bf16[35,16,128]{2,1,0:T(8,128)(2,1)S(1)}, u32[]{:S(2)}, u32[]{:S(2)}) %collective-permute-start.7) | collective-permute-done | bytes 143392 | tf_op jit(solution)/shard_map/ppermute | solution.py:432
  30.6 4.4 %collective-permute-done.9.refs_5_ = bf16[5,16,128]{2,1,0:T(8,128)(2,1)S(1)} collective-permute-done((bf16[5,16,128]{2,1,0:T(8,128)(2,1)S(1)}, bf16[5,16,128]{2,1,0:T(8,128)(2,1)S(1)}, u32[]{:S(2)}, u32[]{:S(2)}) %collective-permute-start.9) | collective-permute-done | bytes 20512 | tf_op jit(solution)/shard_map/ppermute | solution.py:432
  35.0 0.3 collective-permute-done.10.refs_6_
  35.3 0.0 collective-permute-done.8.refs_4_
  35.3 1.1 %shard_map.63 = (bf16[32,8,16,128]{3,2,1,0:T(8,128)(2,1)S(1)}, f32[256,128]{1,0:T(8,128)S(1)}, bf16[8,16,128]{2,1,0:T(8,128)(2,1)S(1)}, bf16[32,128,128]{2,1,0:T...) custom-call(bf16[32,8,16,128]{3,2,1,0:T(8,128)(2,1)S(1)} %get-tuple-, ...), custom_call_target="tpu_custom_call", output_to_operand_aliasing={{0}: (0, {}), {1}: (1, {}), {2}: (2, {})} | custom-call | tf_op jit(solution)/shard_map/pallas_call | solution.py:18
  36.4 0.1 collective-permute-start.11
  36.5 0.2 collective-permute-start.12
  36.7 4.1 %collective-permute-done.11.refs_1_ = f32[128,128]{1,0:T(8,128)S(1)} collective-permute-done((f32[128,128]{1,0:T(8,128)S(1)}, f32[128,128]{1,0:T(8,128)S(1)}, u32[]{:S(2)}, u32[]{:S(2)}) %collective-permute-start.11) | collective-permute-done | bytes 65568 | tf_op jit(solution)/shard_map/ppermute | solution.py:429
  40.8 0.0 collective-permute-start.13
  40.8 0.0 collective-permute-done.12.refs_2_
  40.8 1.2 %collective-permute-done.13.refs_3_ = f32[128,128]{1,0:T(8,128)S(1)} collective-permute-done((f32[128,128]{1,0:T(8,128)S(1)}, f32[128,128]{1,0:T(8,128)S(1)}, u32[]{:S(2)}, u32[]{:S(2)}) %collective-permute-start.13) | collective-permute-done | bytes 65568 | tf_op jit(solution)/shard_map/ppermute | solution.py:429
  42.0 2.0 %shard_map.64 = (f32[32,128]{1,0:T(8,128)S(1)}, f32[2,16,32]{2,1,0:T(8,128)S(1)}, f32[2,16,32]{2,1,0:T(8,128)S(1)}) custom-call(f32[32,128]{1,0:T(8,128)S(1)} %get-tuple-element.59.om_ref, f32[128,128]{1,0:T(8,128)S(1)} %get-tuple-element.60.refs_0_, f32[128,128]{1,0:T(8,128)S(1)} %collective-permute-done.11.refs_1_, ...), custom_call_target="tpu_custom_call" | custom-call | tf_op jit(solution)/shard_map/pallas_call | solution.py:18
  44.0 0.2 collective-permute-start.14
  44.2 1.3 %shard_map.65 = f32[1024,128]{1,0:T(8,128)} custom-call(bf16[32,128,128]{2,1,0:T(8,128)(2,1)S(1)} %get-tuple-element.58.m_ref, f32[32,128]{1,0:T(8,128)S(1)} %get-tuple-element.61.mix_ref), custom_call_target="tpu_custom_call" | custom-call | tf_op jit(solution)/shard_map/pallas_call | solution.py:18
  45.5 3.3 %collective-permute-done.14 = f32[2,16,32]{2,1,0:T(8,128)S(1)} collective-permute-done((f32[2,16,32]{2,1,0:T(8,128)S(1)}, f32[2,16,32]{2,1,0:T(8,128)S(1)}, u32[]{:S(2)}, u32[]{:S(2)}) %collective-permute-start.14) | collective-permute-done | bytes 4128 | tf_op jit(solution)/shard_map/ppermute | solution.py:429
  48.7 0.6 %add_bitcast_fusion = f32[2,1,32,16]{2,3,1,0:T(8,128)} fusion(f32[2,16,32]{2,1,0:T(8,128)S(1)} %get-tuple-element.62, f32[2,16,32]{2,1,0:T(8,128)S(1)} %collective-permute-done.14), kind=kLoop, calls=%fused_computation | loop fusion | flops 1024 | bytes 12288
Async XLA Ops:
  1.3 1.2 %copy-start = (bf16[16,256,128]{2,1,0:T(8,128)(2,1)S(1)}, bf16[16,256,128]{2,1,0:T(8,128)(2,1)}, u32[]{:S(2)}) copy-start(bf16[16,256,128]{2,1,0:T(8,128)(2,1)} %x_ref.3) | copy-start | bytes 3145732
  3.5 15.8 %collective-permute-start.5 = (bf16[34,16,128]{2,1,0:T(8,128)(2,1)S(1)}, bf16[34,16,128]{2,1,0:T(8,128)(2,1)S(1)}, u32[]{:S(2)}, u32[]{:S(2)}) collective-permute-start(bf16[34,16,128]{2,1,0:T(8,128)(2,1)S(1)} %get-tuple-element.45), channel_id=1, source_target_pairs={{0,4},{1,5},{2,6},{3,7},{4,0},{5,1},{6,2},{7,3},{8,12},{9,13},{10,... | collective-permute-start | bytes 417800 | tf_op jit(solution)/shard_map/ppermute | solution.py:432
  6.1 15.6 %collective-permute-start.6 = (bf16[34,16,128]{2,1,0:T(8,128)(2,1)S(1)}, bf16[34,16,128]{2,1,0:T(8,128)(2,1)S(1)}, u32[]{:S(2)}, u32[]{:S(2)}) collective-permute-start(bf16[34,16,128]{2,1,0:T(8,128)(2,1)S(1)} %get-tuple-element.46), channel_id=1, source_target_pairs={{0,5},{1,4},{2,7},{3,6},{4,1},{5,0},{6,3},{7,2},{8,13},{9,12},{10,... | collective-permute-start | bytes 417800 | tf_op jit(solution)/shard_map/ppermute | solution.py:432
  6.1 6.6 %collective-permute-start = (bf16[16,8,256]{2,1,0:T(8,128)(2,1)S(1)}, bf16[16,8,256]{2,1,0:T(8,128)(2,1)S(1)}, u32[]{:S(2)}, u32[]{:S(2)}) collective-permute-start(bf16[16,8,256]{2,1,0:T(8,128)(2,1)S(1)} %get-tuple-element.33), channel_id=1, source_target_pairs={{0,8},{8,0},{16,24},{24,16},{1,9},{9,1},{17,25},{25,17},{2,10},{10... | collective-permute-start | bytes 196616 | tf_op jit(solution)/shard_map/ppermute | solution.py:452
  7.6 7.0 %collective-permute-start.1 = (bf16[16,8,256]{2,1,0:T(8,128)(2,1)S(1)}, bf16[16,8,256]{2,1,0:T(8,128)(2,1)S(1)}, u32[]{:S(2)}, u32[]{:S(2)}) collective-permute-start(bf16[16,8,256]{2,1,0:T(8,128)(2,1)S(1)} %get-tuple-element.34), channel_id=1, source_target_pairs={{8,16},{16,8},{9,17},{17,9},{10,18},{18,10},{11,19},{19,11},{12,20... | collective-permute-start | bytes 196616 | tf_op jit(solution)/shard_map/ppermute | solution.py:454
  10.0 0.7 %copy-start.1 = (bf16[2,1,32,16]{2,3,1,0:T(8,128)(2,1)S(1)}, bf16[2,1,32,16]{2,3,1,0:T(8,128)(2,1)}, u32[]{:S(2)}) copy-start(bf16[2,1,32,16]{2,3,1,0:T(8,128)(2,1)} %param.5) | copy-start | bytes 6148
  10.7 0.7 %copy-start.2 = (bf16[17]{0:T(256)(128)(2,1)S(1)}, bf16[17]{0:T(256)(128)(2,1)}, u32[]{:S(2)}) copy-start(bf16[17]{0:T(256)(128)(2,1)} %param.6) | copy-start | bytes 106
  16.3 5.5 %collective-permute-start.2 = (bf16[35,16,128]{2,1,0:T(8,128)(2,1)S(1)}, bf16[35,16,128]{2,1,0:T(8,128)(2,1)S(1)}, u32[]{:S(2)}, u32[]{:S(2)}) collective-permute-start(bf16[35,16,128]{2,1,0:T(8,128)(2,1)S(1)} %get-tuple-element.42), channel_id=1, source_target_pairs={{0,1},{1,0},{2,3},{3,2},{4,5},{5,4},{6,7},{7,6},{8,9},{9,8},{10,11... | collective-permute-start | bytes 430088 | tf_op jit(solution)/shard_map/ppermute | solution.py:432
  16.4 8.6 %collective-permute-start.3 = (bf16[35,16,128]{2,1,0:T(8,128)(2,1)S(1)}, bf16[35,16,128]{2,1,0:T(8,128)(2,1)S(1)}, u32[]{:S(2)}, u32[]{:S(2)}) collective-permute-start(bf16[35,16,128]{2,1,0:T(8,128)(2,1)S(1)} %get-tuple-element.43), channel_id=1, source_target_pairs={{0,2},{1,3},{2,4},{3,5},{4,6},{5,7},{6,0},{7,1},{8,10},{9,11},{10,... | collective-permute-start | bytes 430088 | tf_op jit(solution)/shard_map/ppermute | solution.py:432
  18.1 9.1 %collective-permute-start.4 = (bf16[35,16,128]{2,1,0:T(8,128)(2,1)S(1)}, bf16[35,16,128]{2,1,0:T(8,128)(2,1)S(1)}, u32[]{:S(2)}, u32[]{:S(2)}) collective-permute-start(bf16[35,16,128]{2,1,0:T(8,128)(2,1)S(1)} %get-tuple-element.44), channel_id=1, source_target_pairs={{0,3},{1,2},{2,5},{3,4},{4,7},{5,6},{6,1},{7,0},{8,11},{9,10},{10,... | collective-permute-start | bytes 430088 | tf_op jit(solution)/shard_map/ppermute | solution.py:432
  19.3 11.3 %collective-permute-start.7 = (bf16[35,16,128]{2,1,0:T(8,128)(2,1)S(1)}, bf16[35,16,128]{2,1,0:T(8,128)(2,1)S(1)}, u32[]{:S(2)}, u32[]{:S(2)}) collective-permute-start(bf16[35,16,128]{2,1,0:T(8,128)(2,1)S(1)} %get-tuple-element.50), channel_id=1, source_target_pairs={{0,6},{1,7},{2,0},{3,1},{4,2},{5,3},{6,4},{7,5},{8,14},{9,15},{10,... | collective-permute-start | bytes 430088 | tf_op jit(solution)/shard_map/ppermute | solution.py:432
  21.7 13.6 %collective-permute-start.8 = (bf16[35,16,128]{2,1,0:T(8,128)(2,1)S(1)}, bf16[35,16,128]{2,1,0:T(8,128)(2,1)S(1)}, u32[]{:S(2)}, u32[]{:S(2)}) collective-permute-start(bf16[35,16,128]{2,1,0:T(8,128)(2,1)S(1)} %get-tuple-element.52), channel_id=1, source_target_pairs={{0,7},{1,6},{2,1},{3,0},{4,3},{5,2},{6,5},{7,4},{8,15},{9,14},{10,... | collective-permute-start | bytes 430088 | tf_op jit(solution)/shard_map/ppermute | solution.py:432
  21.9 13.1 %collective-permute-start.9 = (bf16[5,16,128]{2,1,0:T(8,128)(2,1)S(1)}, bf16[5,16,128]{2,1,0:T(8,128)(2,1)S(1)}, u32[]{:S(2)}, u32[]{:S(2)}) collective-permute-start(bf16[5,16,128]{2,1,0:T(8,128)(2,1)S(1)} %get-tuple-element.54), channel_id=1, source_target_pairs={{0,4},{1,5},{2,6},{3,7},{4,0},{5,1},{6,2},{7,3},{8,12},{9,13},{10,... | collective-permute-start | bytes 61448 | tf_op jit(solution)/shard_map/ppermute | solution.py:432
  25.0 10.3 %collective-permute-start.10 = (bf16[5,16,128]{2,1,0:T(8,128)(2,1)S(1)}, bf16[5,16,128]{2,1,0:T(8,128)(2,1)S(1)}, u32[]{:S(2)}, u32[]{:S(2)}) collective-permute-start(bf16[5,16,128]{2,1,0:T(8,128)(2,1)S(1)} %get-tuple-element.56), channel_id=1, source_target_pairs={{0,5},{1,4},{2,7},{3,6},{4,1},{5,0},{6,3},{7,2},{8,13},{9,12},{10,... | collective-permute-start | bytes 61448 | tf_op jit(solution)/shard_map/ppermute | solution.py:432
  36.4 4.3 %collective-permute-start.11 = (f32[128,128]{1,0:T(8,128)S(1)}, f32[128,128]{1,0:T(8,128)S(1)}, u32[]{:S(2)}, u32[]{:S(2)}) collective-permute-start(f32[128,128]{1,0:T(8,128)S(1)} %get-tuple-element.60.refs_0_), channel_id=1, source_target_pairs={{0,2},{1,3},{2,0},{3,1},{4,6},{5,7},{6,4},{7,5},{8,10},{9,11},{10,... | collective-permute-start | bytes 196616 | tf_op jit(solution)/shard_map/ppermute | solution.py:429
  36.5 4.3 %collective-permute-start.12 = (f32[128,128]{1,0:T(8,128)S(1)}, f32[128,128]{1,0:T(8,128)S(1)}, u32[]{:S(2)}, u32[]{:S(2)}) collective-permute-start(f32[128,128]{1,0:T(8,128)S(1)} %get-tuple-element.60.refs_0_), channel_id=1, source_target_pairs={{0,1},{1,0},{2,3},{3,2},{4,5},{5,4},{6,7},{7,6},{8,9},{9,8},{10,11... | collective-permute-start | bytes 196616 | tf_op jit(solution)/shard_map/ppermute | solution.py:429
  40.8 1.3 %collective-permute-start.13 = (f32[128,128]{1,0:T(8,128)S(1)}, f32[128,128]{1,0:T(8,128)S(1)}, u32[]{:S(2)}, u32[]{:S(2)}) collective-permute-start(f32[128,128]{1,0:T(8,128)S(1)} %collective-permute-done.11.refs_1_), channel_id=1, source_target_pairs={{0,1},{1,0},{2,3},{3,2},{4,5},{5,4},{6,7},{7,6},{8,9},{9,8},{10,11... | collective-permute-start | bytes 196616 | tf_op jit(solution)/shard_map/ppermute | solution.py:429
  44.0 4.7 %collective-permute-start.14 = (f32[2,16,32]{2,1,0:T(8,128)S(1)}, f32[2,16,32]{2,1,0:T(8,128)S(1)}, u32[]{:S(2)}, u32[]{:S(2)}) collective-permute-start(f32[2,16,32]{2,1,0:T(8,128)S(1)} %get-tuple-element.63), channel_id=1, source_target_pairs={{0,4},{1,5},{2,6},{3,7},{4,0},{5,1},{6,2},{7,3},{8,12},{9,13},{10,... | collective-permute-start | bytes 12296 | tf_op jit(solution)/shard_map/ppermute | solution.py:429

commit v8 on v6

--- a/solution.py
+++ b/solution.py
@@ -353,7 +353,7 @@
         ]
         for j in range(start, start + panel):
             inverse = 1.0 / cols[j - start][j : j + 1]
-            factor = jnp.where(ids > j, cols[j - start] * inverse, 0.0)
+            factor = jnp.where(ids > j, cols[j - start], 0.0) * inverse
             scale = jnp.where(ids == j, inverse, scale)
             for m in range(j - start + 1, panel):
                 cols[m] = cols[m] - factor * cols[m][j : j + 1]

time: 49.6 us -> 49.6 us (level)
  no operation moved by 1% of the time
where the time goes in v8:
time: 49.6 us; the launch traced here: 49.4 us
  waiting for transfers between devices  23.2 us (47%)
  starting transfers between devices  13 us (26%)
  Pallas kernels  8.6 us (17%)
  local copies, waits for them, and re-layouts  3.22 us (6%)
  between operations  0.72 us (1%)
  other arithmetic  0.61 us (1%)
    ppermute x9, waiting for transfers between devices, send(): lax.ppermute(value, 'tm', [(i, device_at(i, count, shift, flip)) for i in...  12.7 us
    ppermute x9, starting transfers between devices, send(): lax.ppermute(value, 'tm', [(i, device_at(i, count, shift, flip)) for i in...  8.74 us
    pallas_call x7, Pallas kernels, call(): pl.pallas_call(kernel, out_shape=outs, in_specs=[pl.BlockSpec(memory_spac...  8.6 us
    ppermute x4, waiting for transfers between devices, swap(): return lax.ppermute(value, 'tm', [(i, i ^ k) for i in range(count)])  8.59 us
    unnamed x8, local copies, waits for them, and re-layouts  3.22 us
    ppermute x1, starting transfers between devices, local(): side_b = lax.ppermute(side_b, 'tile', pairs + [(j, i) for i, j in pairs])  2.37 us
    ppermute x1, waiting for transfers between devices, local(): side_b = lax.ppermute(side_b, 'tile', pairs + [(j, i) for i, j in pairs])  1.91 us
    ppermute x1, starting transfers between devices, local(): side_a = lax.ppermute(side_a, 'tile', pairs)  1.49 us
  transfers between devices with their start and end apart: 15, of which 9 were waited for; matrix products, arithmetic and copies ran while one was open for 0% of the time, Pallas kernels for 9%

profile of v8, /device:TPU:4, one launch (start us, length us, event | category | flops | bytes accessed | tf_op | source)
XLA Modules:
  0.0 49.4 jit_solution(6090576070316980842)
XLA Ops:
  0.6 0.0 copy-start
  0.6 1.2 %copy-done = bf16[16,256,128]{2,1,0:T(8,128)(2,1)S(1)} copy-done((bf16[16,256,128]{2,1,0:T(8,128)(2,1)S(1)}, bf16[16,256,128]{2,1,0:T(8,128)(2,1)}, u32[]{:S(2)}) %copy-start) | copy-done | bytes 1048600
  1.9 0.0 copy-start.2
  1.9 0.7 %copy-done.2 = bf16[17]{0:T(256)(128)(2,1)S(1)} copy-done((bf16[17]{0:T(256)(128)(2,1)S(1)}, bf16[17]{0:T(256)(128)(2,1)}, u32[]{:S(2)}) %copy-start.2) | copy-done | bytes 58
  2.5 1.0 %shard_map.59 = (bf16[34,16,128]{2,1,0:T(8,128)(2,1)S(1)}, bf16[34,16,128]{2,1,0:T(8,128)(2,1)S(1)}, bf16[16,8,256]{2,1,0:T(8,128)(2,1)S(1)}, bf16[16,8,256]{2,1,0:T(8,128)(2,1)S(1)}) custom-call(bf16[16,256,128]{2,1,0:T(8,128)(2,1)S(1)} %copy-done, bf16[1,17]{1,0:T(2,128)(2,1)S(1)} %bitcast.13), custom_call_target="tpu_custom_call" | custom-call | tf_op jit(solution)/shard_map/pallas_call | solution.py:18
  3.5 2.6 %collective-permute-start.5 = (bf16[34,16,128]{2,1,0:T(8,128)(2,1)S(1)}, bf16[34,16,128]{2,1,0:T(8,128)(2,1)S(1)}, u32[]{:S(2)}, u32[]{:S(2)}) collective-permute-start(bf16[34,16,128]{2,1,0:T(8,128)(2,1)S(1)} %get-tuple-element.45), channel_id=1, source_target_pairs={{0,4},{1,5},{2,6},{3,7},{4,0},{5,1},{6,2},{7,3},{8,12},{9,13},{10,... | collective-permute-start | bytes 417800 | tf_op jit(solution)/shard_map/ppermute | solution.py:431
  6.1 0.0 collective-permute-start.6
  6.1 1.5 %collective-permute-start = (bf16[16,8,256]{2,1,0:T(8,128)(2,1)S(1)}, bf16[16,8,256]{2,1,0:T(8,128)(2,1)S(1)}, u32[]{:S(2)}, u32[]{:S(2)}) collective-permute-start(bf16[16,8,256]{2,1,0:T(8,128)(2,1)S(1)} %get-tuple-element.33), channel_id=1, source_target_pairs={{0,8},{8,0},{16,24},{24,16},{1,9},{9,1},{17,25},{25,17},{2,10},{10... | collective-permute-start | bytes 196616 | tf_op jit(solution)/shard_map/ppermute | solution.py:451
  7.6 2.4 %collective-permute-start.1 = (bf16[16,8,256]{2,1,0:T(8,128)(2,1)S(1)}, bf16[16,8,256]{2,1,0:T(8,128)(2,1)S(1)}, u32[]{:S(2)}, u32[]{:S(2)}) collective-permute-start(bf16[16,8,256]{2,1,0:T(8,128)(2,1)S(1)} %get-tuple-element.34), channel_id=1, source_target_pairs={{8,16},{16,8},{9,17},{17,9},{10,18},{18,10},{11,19},{19,11},{12,20... | collective-permute-start | bytes 196616 | tf_op jit(solution)/shard_map/ppermute | solution.py:453
  10.0 0.0 copy-start.1
  10.0 0.7 %copy-done.1 = bf16[2,1,32,16]{2,3,1,0:T(8,128)(2,1)S(1)} copy-done((bf16[2,1,32,16]{2,3,1,0:T(8,128)(2,1)S(1)}, bf16[2,1,32,16]{2,3,1,0:T(8,128)(2,1)}, u32[]{:S(2)}) %copy-start.1) | copy-done | bytes 2072
  10.7 0.0 copy-start.3
  10.7 0.7 %copy-done.3 = bf16[17]{0:T(256)(128)(2,1)S(1)} copy-done((bf16[17]{0:T(256)(128)(2,1)S(1)}, bf16[17]{0:T(256)(128)(2,1)}, u32[]{:S(2)}) %copy-start.3) | copy-done | bytes 58
  11.4 1.4 %shard_map.60 = (bf16[16,128]{1,0:T(8,128)(2,1)S(1)}, bf16[256,256]{1,0:T(8,128)(2,1)S(1)}, bf16[128,144]{1,0:T(8,128)(2,1)S(1)}, bf16[2,16,32]{2,1,0:T(8,128)(2...) custom-call(bf16[16,256,128]{2,1,0:T(8,128)(2,1)S(1)} %copy-done, ...), custom_call_target="tpu_custom_call" | custom-call | tf_op jit(solution)/shard_map/pallas_call | solution.py:18
  12.7 0.0 collective-permute-done.a_ref
  12.8 1.9 %collective-permute-done.1.b_ref = bf16[16,8,256]{2,1,0:T(8,128)(2,1)S(1)} collective-permute-done((bf16[16,8,256]{2,1,0:T(8,128)(2,1)S(1)}, bf16[16,8,256]{2,1,0:T(8,128)(2,1)S(1)}, u32[]{:S(2)}, u32[]{:S(2)}) %collective-permute-start.1) | collective-permute-done | bytes 65568 | tf_op jit(solution)/shard_map/ppermute | solution.py:453
  14.7 1.7 %shard_map.61 = (bf16[35,16,128]{2,1,0:T(8,128)(2,1)S(1)}, bf16[35,16,128]{2,1,0:T(8,128)(2,1)S(1)}, bf16[35,16,128]{2,1,0:T(8,128)(2,1)S(1)}, bf16[35,16,128]{2...) custom-call(bf16[16,8,256]{2,1,0:T(8,128)(2,1)S(1)} %collective-perm, ...), custom_call_target="tpu_custom_call" | custom-call | tf_op jit(solution)/shard_map/pallas_call | solution.py:18
  16.4 0.1 collective-permute-start.2
  16.4 1.6 %collective-permute-start.3 = (bf16[35,16,128]{2,1,0:T(8,128)(2,1)S(1)}, bf16[35,16,128]{2,1,0:T(8,128)(2,1)S(1)}, u32[]{:S(2)}, u32[]{:S(2)}) collective-permute-start(bf16[35,16,128]{2,1,0:T(8,128)(2,1)S(1)} %get-tuple-element.43), channel_id=1, source_target_pairs={{0,2},{1,3},{2,4},{3,5},{4,6},{5,7},{6,0},{7,1},{8,10},{9,11},{10,... | collective-permute-start | bytes 430088 | tf_op jit(solution)/shard_map/ppermute | solution.py:431
  18.1 1.2 %collective-permute-start.4 = (bf16[35,16,128]{2,1,0:T(8,128)(2,1)S(1)}, bf16[35,16,128]{2,1,0:T(8,128)(2,1)S(1)}, u32[]{:S(2)}, u32[]{:S(2)}) collective-permute-start(bf16[35,16,128]{2,1,0:T(8,128)(2,1)S(1)} %get-tuple-element.44), channel_id=1, source_target_pairs={{0,3},{1,2},{2,5},{3,4},{4,7},{5,6},{6,1},{7,0},{8,11},{9,10},{10,... | collective-permute-start | bytes 430088 | tf_op jit(solution)/shard_map/ppermute | solution.py:431
  19.3 0.0 collective-permute-done.5.refs_4_
  19.3 2.4 %collective-permute-start.7 = (bf16[35,16,128]{2,1,0:T(8,128)(2,1)S(1)}, bf16[35,16,128]{2,1,0:T(8,128)(2,1)S(1)}, u32[]{:S(2)}, u32[]{:S(2)}) collective-permute-start(bf16[35,16,128]{2,1,0:T(8,128)(2,1)S(1)} %get-tuple-element.50), channel_id=1, source_target_pairs={{0,6},{1,7},{2,0},{3,1},{4,2},{5,3},{6,4},{7,5},{8,14},{9,15},{10,... | collective-permute-start | bytes 430088 | tf_op jit(solution)/shard_map/ppermute | solution.py:431
  21.7 0.0 collective-permute-done.6.refs_5_
  21.7 0.2 collective-permute-start.8
  21.9 0.0 collective-permute-done.2.refs_1_
  21.9 0.6 %collective-permute-start.9 = (bf16[5,16,128]{2,1,0:T(8,128)(2,1)S(1)}, bf16[5,16,128]{2,1,0:T(8,128)(2,1)S(1)}, u32[]{:S(2)}, u32[]{:S(2)}) collective-permute-start(bf16[5,16,128]{2,1,0:T(8,128)(2,1)S(1)} %get-tuple-element.54), channel_id=1, source_target_pairs={{0,4},{1,5},{2,6},{3,7},{4,0},{5,1},{6,2},{7,3},{8,12},{9,13},{10,... | collective-permute-start | bytes 61448 | tf_op jit(solution)/shard_map/ppermute | solution.py:431
  22.5 2.5 %collective-permute-done.3.refs_2_ = bf16[35,16,128]{2,1,0:T(8,128)(2,1)S(1)} collective-permute-done((bf16[35,16,128]{2,1,0:T(8,128)(2,1)S(1)}, bf16[35,16,128]{2,1,0:T(8,128)(2,1)S(1)}, u32[]{:S(2)}, u32[]{:S(2)}) %collective-permute-start.3) | collective-permute-done | bytes 143392 | tf_op jit(solution)/shard_map/ppermute | solution.py:431
  25.0 0.0 collective-permute-start.10
  25.0 2.2 %collective-permute-done.4.refs_3_ = bf16[35,16,128]{2,1,0:T(8,128)(2,1)S(1)} collective-permute-done((bf16[35,16,128]{2,1,0:T(8,128)(2,1)S(1)}, bf16[35,16,128]{2,1,0:T(8,128)(2,1)S(1)}, u32[]{:S(2)}, u32[]{:S(2)}) %collective-permute-start.4) | collective-permute-done | bytes 143392 | tf_op jit(solution)/shard_map/ppermute | solution.py:431
  27.2 0.1 shard_map.62
  27.3 3.3 %collective-permute-done.7.refs_3_ = bf16[35,16,128]{2,1,0:T(8,128)(2,1)S(1)} collective-permute-done((bf16[35,16,128]{2,1,0:T(8,128)(2,1)S(1)}, bf16[35,16,128]{2,1,0:T(8,128)(2,1)S(1)}, u32[]{:S(2)}, u32[]{:S(2)}) %collective-permute-start.7) | collective-permute-done | bytes 143392 | tf_op jit(solution)/shard_map/ppermute | solution.py:431
  30.6 4.4 %collective-permute-done.9.refs_5_ = bf16[5,16,128]{2,1,0:T(8,128)(2,1)S(1)} collective-permute-done((bf16[5,16,128]{2,1,0:T(8,128)(2,1)S(1)}, bf16[5,16,128]{2,1,0:T(8,128)(2,1)S(1)}, u32[]{:S(2)}, u32[]{:S(2)}) %collective-permute-start.9) | collective-permute-done | bytes 20512 | tf_op jit(solution)/shard_map/ppermute | solution.py:431
  35.0 0.3 collective-permute-done.10.refs_6_
  35.3 0.0 collective-permute-done.8.refs_4_
  35.3 1.1 %shard_map.63 = (bf16[32,8,16,128]{3,2,1,0:T(8,128)(2,1)S(1)}, f32[256,128]{1,0:T(8,128)S(1)}, bf16[8,16,128]{2,1,0:T(8,128)(2,1)S(1)}, bf16[32,128,128]{2,1,0:T...) custom-call(bf16[32,8,16,128]{3,2,1,0:T(8,128)(2,1)S(1)} %get-tuple-, ...), custom_call_target="tpu_custom_call", output_to_operand_aliasing={{0}: (0, {}), {1}: (1, {}), {2}: (2, {})} | custom-call | tf_op jit(solution)/shard_map/pallas_call | solution.py:18
  36.5 0.1 collective-permute-start.11
  36.5 0.2 collective-permute-start.12
  36.7 4.1 %collective-permute-done.11.refs_1_ = f32[128,128]{1,0:T(8,128)S(1)} collective-permute-done((f32[128,128]{1,0:T(8,128)S(1)}, f32[128,128]{1,0:T(8,128)S(1)}, u32[]{:S(2)}, u32[]{:S(2)}) %collective-permute-start.11) | collective-permute-done | bytes 65568 | tf_op jit(solution)/shard_map/ppermute | solution.py:428
  40.8 0.0 collective-permute-start.13
  40.8 0.0 collective-permute-done.12.refs_2_
  40.8 1.2 %collective-permute-done.13.refs_3_ = f32[128,128]{1,0:T(8,128)S(1)} collective-permute-done((f32[128,128]{1,0:T(8,128)S(1)}, f32[128,128]{1,0:T(8,128)S(1)}, u32[]{:S(2)}, u32[]{:S(2)}) %collective-permute-start.13) | collective-permute-done | bytes 65568 | tf_op jit(solution)/shard_map/ppermute | solution.py:428
  42.0 2.0 %shard_map.64 = (f32[32,128]{1,0:T(8,128)S(1)}, f32[2,16,32]{2,1,0:T(8,128)S(1)}, f32[2,16,32]{2,1,0:T(8,128)S(1)}) custom-call(f32[32,128]{1,0:T(8,128)S(1)} %get-tuple-element.59.om_ref, f32[128,128]{1,0:T(8,128)S(1)} %get-tuple-element.60.refs_0_, f32[128,128]{1,0:T(8,128)S(1)} %collective-permute-done.11.refs_1_, ...), custom_call_target="tpu_custom_call" | custom-call | tf_op jit(solution)/shard_map/pallas_call | solution.py:18
  44.0 0.2 collective-permute-start.14
  44.2 1.3 %shard_map.65 = f32[1024,128]{1,0:T(8,128)} custom-call(bf16[32,128,128]{2,1,0:T(8,128)(2,1)S(1)} %get-tuple-element.58.m_ref, f32[32,128]{1,0:T(8,128)S(1)} %get-tuple-element.61.mix_ref), custom_call_target="tpu_custom_call" | custom-call | tf_op jit(solution)/shard_map/pallas_call | solution.py:18
  45.5 3.3 %collective-permute-done.14 = f32[2,16,32]{2,1,0:T(8,128)S(1)} collective-permute-done((f32[2,16,32]{2,1,0:T(8,128)S(1)}, f32[2,16,32]{2,1,0:T(8,128)S(1)}, u32[]{:S(2)}, u32[]{:S(2)}) %collective-permute-start.14) | collective-permute-done | bytes 4128 | tf_op jit(solution)/shard_map/ppermute | solution.py:428
  48.7 0.6 %add_bitcast_fusion = f32[2,1,32,16]{2,3,1,0:T(8,128)} fusion(f32[2,16,32]{2,1,0:T(8,128)S(1)} %get-tuple-element.62, f32[2,16,32]{2,1,0:T(8,128)S(1)} %collective-permute-done.14), kind=kLoop, calls=%fused_computation | loop fusion | flops 1024 | bytes 12288
Async XLA Ops:
  0.6 1.2 %copy-start = (bf16[16,256,128]{2,1,0:T(8,128)(2,1)S(1)}, bf16[16,256,128]{2,1,0:T(8,128)(2,1)}, u32[]{:S(2)}) copy-start(bf16[16,256,128]{2,1,0:T(8,128)(2,1)} %x_ref.3) | copy-start | bytes 3145732
  1.9 0.7 %copy-start.2 = (bf16[17]{0:T(256)(128)(2,1)S(1)}, bf16[17]{0:T(256)(128)(2,1)}, u32[]{:S(2)}) copy-start(bf16[17]{0:T(256)(128)(2,1)} %param.7) | copy-start | bytes 106
  3.5 15.8 %collective-permute-start.5 = (bf16[34,16,128]{2,1,0:T(8,128)(2,1)S(1)}, bf16[34,16,128]{2,1,0:T(8,128)(2,1)S(1)}, u32[]{:S(2)}, u32[]{:S(2)}) collective-permute-start(bf16[34,16,128]{2,1,0:T(8,128)(2,1)S(1)} %get-tuple-element.45), channel_id=1, source_target_pairs={{0,4},{1,5},{2,6},{3,7},{4,0},{5,1},{6,2},{7,3},{8,12},{9,13},{10,... | collective-permute-start | bytes 417800 | tf_op jit(solution)/shard_map/ppermute | solution.py:431
  6.1 15.5 %collective-permute-start.6 = (bf16[34,16,128]{2,1,0:T(8,128)(2,1)S(1)}, bf16[34,16,128]{2,1,0:T(8,128)(2,1)S(1)}, u32[]{:S(2)}, u32[]{:S(2)}) collective-permute-start(bf16[34,16,128]{2,1,0:T(8,128)(2,1)S(1)} %get-tuple-element.46), channel_id=1, source_target_pairs={{0,5},{1,4},{2,7},{3,6},{4,1},{5,0},{6,3},{7,2},{8,13},{9,12},{10,... | collective-permute-start | bytes 417800 | tf_op jit(solution)/shard_map/ppermute | solution.py:431
  6.1 6.6 %collective-permute-start = (bf16[16,8,256]{2,1,0:T(8,128)(2,1)S(1)}, bf16[16,8,256]{2,1,0:T(8,128)(2,1)S(1)}, u32[]{:S(2)}, u32[]{:S(2)}) collective-permute-start(bf16[16,8,256]{2,1,0:T(8,128)(2,1)S(1)} %get-tuple-element.33), channel_id=1, source_target_pairs={{0,8},{8,0},{16,24},{24,16},{1,9},{9,1},{17,25},{25,17},{2,10},{10... | collective-permute-start | bytes 196616 | tf_op jit(solution)/shard_map/ppermute | solution.py:451
  7.6 7.0 %collective-permute-start.1 = (bf16[16,8,256]{2,1,0:T(8,128)(2,1)S(1)}, bf16[16,8,256]{2,1,0:T(8,128)(2,1)S(1)}, u32[]{:S(2)}, u32[]{:S(2)}) collective-permute-start(bf16[16,8,256]{2,1,0:T(8,128)(2,1)S(1)} %get-tuple-element.34), channel_id=1, source_target_pairs={{8,16},{16,8},{9,17},{17,9},{10,18},{18,10},{11,19},{19,11},{12,20... | collective-permute-start | bytes 196616 | tf_op jit(solution)/shard_map/ppermute | solution.py:453
  10.0 0.7 %copy-start.1 = (bf16[2,1,32,16]{2,3,1,0:T(8,128)(2,1)S(1)}, bf16[2,1,32,16]{2,3,1,0:T(8,128)(2,1)}, u32[]{:S(2)}) copy-start(bf16[2,1,32,16]{2,3,1,0:T(8,128)(2,1)} %param.5) | copy-start | bytes 6148
  10.7 0.7 %copy-start.3 = (bf16[17]{0:T(256)(128)(2,1)S(1)}, bf16[17]{0:T(256)(128)(2,1)}, u32[]{:S(2)}) copy-start(bf16[17]{0:T(256)(128)(2,1)} %param.6) | copy-start | bytes 106
  16.4 5.6 %collective-permute-start.2 = (bf16[35,16,128]{2,1,0:T(8,128)(2,1)S(1)}, bf16[35,16,128]{2,1,0:T(8,128)(2,1)S(1)}, u32[]{:S(2)}, u32[]{:S(2)}) collective-permute-start(bf16[35,16,128]{2,1,0:T(8,128)(2,1)S(1)} %get-tuple-element.42), channel_id=1, source_target_pairs={{0,1},{1,0},{2,3},{3,2},{4,5},{5,4},{6,7},{7,6},{8,9},{9,8},{10,11... | collective-permute-start | bytes 430088 | tf_op jit(solution)/shard_map/ppermute | solution.py:431
  16.4 8.6 %collective-permute-start.3 = (bf16[35,16,128]{2,1,0:T(8,128)(2,1)S(1)}, bf16[35,16,128]{2,1,0:T(8,128)(2,1)S(1)}, u32[]{:S(2)}, u32[]{:S(2)}) collective-permute-start(bf16[35,16,128]{2,1,0:T(8,128)(2,1)S(1)} %get-tuple-element.43), channel_id=1, source_target_pairs={{0,2},{1,3},{2,4},{3,5},{4,6},{5,7},{6,0},{7,1},{8,10},{9,11},{10,... | collective-permute-start | bytes 430088 | tf_op jit(solution)/shard_map/ppermute | solution.py:431
  18.1 9.1 %collective-permute-start.4 = (bf16[35,16,128]{2,1,0:T(8,128)(2,1)S(1)}, bf16[35,16,128]{2,1,0:T(8,128)(2,1)S(1)}, u32[]{:S(2)}, u32[]{:S(2)}) collective-permute-start(bf16[35,16,128]{2,1,0:T(8,128)(2,1)S(1)} %get-tuple-element.44), channel_id=1, source_target_pairs={{0,3},{1,2},{2,5},{3,4},{4,7},{5,6},{6,1},{7,0},{8,11},{9,10},{10,... | collective-permute-start | bytes 430088 | tf_op jit(solution)/shard_map/ppermute | solution.py:431
  19.3 11.3 %collective-permute-start.7 = (bf16[35,16,128]{2,1,0:T(8,128)(2,1)S(1)}, bf16[35,16,128]{2,1,0:T(8,128)(2,1)S(1)}, u32[]{:S(2)}, u32[]{:S(2)}) collective-permute-start(bf16[35,16,128]{2,1,0:T(8,128)(2,1)S(1)} %get-tuple-element.50), channel_id=1, source_target_pairs={{0,6},{1,7},{2,0},{3,1},{4,2},{5,3},{6,4},{7,5},{8,14},{9,15},{10,... | collective-permute-start | bytes 430088 | tf_op jit(solution)/shard_map/ppermute | solution.py:431
  21.7 13.6 %collective-permute-start.8 = (bf16[35,16,128]{2,1,0:T(8,128)(2,1)S(1)}, bf16[35,16,128]{2,1,0:T(8,128)(2,1)S(1)}, u32[]{:S(2)}, u32[]{:S(2)}) collective-permute-start(bf16[35,16,128]{2,1,0:T(8,128)(2,1)S(1)} %get-tuple-element.52), channel_id=1, source_target_pairs={{0,7},{1,6},{2,1},{3,0},{4,3},{5,2},{6,5},{7,4},{8,15},{9,14},{10,... | collective-permute-start | bytes 430088 | tf_op jit(solution)/shard_map/ppermute | solution.py:431
  21.9 13.1 %collective-permute-start.9 = (bf16[5,16,128]{2,1,0:T(8,128)(2,1)S(1)}, bf16[5,16,128]{2,1,0:T(8,128)(2,1)S(1)}, u32[]{:S(2)}, u32[]{:S(2)}) collective-permute-start(bf16[5,16,128]{2,1,0:T(8,128)(2,1)S(1)} %get-tuple-element.54), channel_id=1, source_target_pairs={{0,4},{1,5},{2,6},{3,7},{4,0},{5,1},{6,2},{7,3},{8,12},{9,13},{10,... | collective-permute-start | bytes 61448 | tf_op jit(solution)/shard_map/ppermute | solution.py:431
  25.0 10.3 %collective-permute-start.10 = (bf16[5,16,128]{2,1,0:T(8,128)(2,1)S(1)}, bf16[5,16,128]{2,1,0:T(8,128)(2,1)S(1)}, u32[]{:S(2)}, u32[]{:S(2)}) collective-permute-start(bf16[5,16,128]{2,1,0:T(8,128)(2,1)S(1)} %get-tuple-element.56), channel_id=1, source_target_pairs={{0,5},{1,4},{2,7},{3,6},{4,1},{5,0},{6,3},{7,2},{8,13},{9,12},{10,... | collective-permute-start | bytes 61448 | tf_op jit(solution)/shard_map/ppermute | solution.py:431
  36.5 4.3 %collective-permute-start.11 = (f32[128,128]{1,0:T(8,128)S(1)}, f32[128,128]{1,0:T(8,128)S(1)}, u32[]{:S(2)}, u32[]{:S(2)}) collective-permute-start(f32[128,128]{1,0:T(8,128)S(1)} %get-tuple-element.60.refs_0_), channel_id=1, source_target_pairs={{0,2},{1,3},{2,0},{3,1},{4,6},{5,7},{6,4},{7,5},{8,10},{9,11},{10,... | collective-permute-start | bytes 196616 | tf_op jit(solution)/shard_map/ppermute | solution.py:428
  36.5 4.3 %collective-permute-start.12 = (f32[128,128]{1,0:T(8,128)S(1)}, f32[128,128]{1,0:T(8,128)S(1)}, u32[]{:S(2)}, u32[]{:S(2)}) collective-permute-start(f32[128,128]{1,0:T(8,128)S(1)} %get-tuple-element.60.refs_0_), channel_id=1, source_target_pairs={{0,1},{1,0},{2,3},{3,2},{4,5},{5,4},{6,7},{7,6},{8,9},{9,8},{10,11... | collective-permute-start | bytes 196616 | tf_op jit(solution)/shard_map/ppermute | solution.py:428
  40.8 1.3 %collective-permute-start.13 = (f32[128,128]{1,0:T(8,128)S(1)}, f32[128,128]{1,0:T(8,128)S(1)}, u32[]{:S(2)}, u32[]{:S(2)}) collective-permute-start(f32[128,128]{1,0:T(8,128)S(1)} %collective-permute-done.11.refs_1_), channel_id=1, source_target_pairs={{0,1},{1,0},{2,3},{3,2},{4,5},{5,4},{6,7},{7,6},{8,9},{9,8},{10,11... | collective-permute-start | bytes 196616 | tf_op jit(solution)/shard_map/ppermute | solution.py:428
  44.0 4.7 %collective-permute-start.14 = (f32[2,16,32]{2,1,0:T(8,128)S(1)}, f32[2,16,32]{2,1,0:T(8,128)S(1)}, u32[]{:S(2)}, u32[]{:S(2)}) collective-permute-start(f32[2,16,32]{2,1,0:T(8,128)S(1)} %get-tuple-element.63), channel_id=1, source_target_pairs={{0,4},{1,5},{2,6},{3,7},{4,0},{5,1},{6,2},{7,3},{8,12},{9,13},{10,... | collective-permute-start | bytes 12296 | tf_op jit(solution)/shard_map/ppermute | solution.py:428
